TPU v7x, 256 devices: a whole 4x4x8 slice. The times are simulated.
256 devices in a mesh: row: 16 (over z_lo, x, core), col: 16 (over y, z_hi).
Axes of the slice: x: 4, y: 4, z: 8 (z_hi: 4, z_lo: 2; z = z_hi * 2 + z_lo), core: 2. Of those that a mesh axis runs over, the one named last changes fastest.
Arguments:
- embed_docs: float32 [16384, 256], P(('row', 'col')), may hold values from -2 to 2
- embed_targets: float32 [32768, 256], P(('col', 'row')), may hold values from -2 to 2
- starting_goal_multiplier: float32 [32768], P('col'), may hold values from -0.8 to 0.8
Outputs:
- grad_docs: float32 [16384, 256], P(('row', 'col'))
- grad_targets: float32 [32768, 256], P(('col', 'row'))
All inputs are finite; a program needn't handle non-finite values.
Results may differ from a plain program's by a relative error of at most 0.0003.
Values sent between devices are 32-bit elements; how exact they have to be, the bound alone decides.
No kernel may reach another device: no remote copies, remote signals or barrier semaphores. Data moves between devices by JAX's collectives and lax.ppermute only.
A program may use at most 64 MiB of HBM per device.

v0:
```python
import math

import jax
import jax.numpy as jnp
from jax import lax
from jax.sharding import PartitionSpec as P

smoothing_epsilon = 0.05


def horizontal_softmax_norm(similarity_grid):
    largest = lax.pmax(jnp.max(similarity_grid, axis=1), "col")
    mass_all = lax.psum(jnp.sum(jnp.exp(similarity_grid - largest[:, None]), axis=1), "col")
    return largest + jnp.log(mass_all)


def column_logsumexp(similarity_grid):
    largest = lax.pmax(jnp.max(similarity_grid, axis=0), "row")
    mass_all = lax.psum(jnp.sum(jnp.exp(similarity_grid - largest[None, :]), axis=0), "row")
    return largest + jnp.log(mass_all)


def doc_sum(values):
    return lax.psum(values, "col")


def local(embed_docs, embed_targets, starting_goal_multiplier):
    highest = lax.Precision.HIGHEST
    row_devices = lax.axis_size("row")
    col_devices = lax.axis_size("col")
    target_block = lax.all_gather(embed_targets, "row", axis=0, tiled=True)
    doc_block = lax.all_gather(embed_docs, "col", axis=0, tiled=True)
    doc_norms = jnp.sum(doc_block * doc_block, axis=1)
    target_norms = jnp.sum(target_block * target_block, axis=1)
    distance_tile = (
        doc_norms[:, None]
        + target_norms[None, :]
        - 2.0 * jnp.dot(doc_block, target_block.T, precision=highest)
    )
    text_aggregate = distance_tile.shape[0] * row_devices
    goal_aggregate = distance_tile.shape[1] * col_devices
    scaling_mass = text_aggregate / goal_aggregate
    horizontal_lse_early = horizontal_softmax_norm(
        (starting_goal_multiplier[None, :] - distance_tile) / smoothing_epsilon
    )
    text_multiplier_early = (
        smoothing_epsilon * math.log(goal_aggregate) - smoothing_epsilon * horizontal_lse_early
    )
    vertical_lse_early = column_logsumexp(
        (text_multiplier_early[:, None] - distance_tile) / smoothing_epsilon
    )
    goal_multiplier_early = (
        smoothing_epsilon * math.log(text_aggregate) - smoothing_epsilon * vertical_lse_early
    )
    horizontal_lse_later = horizontal_softmax_norm(
        (goal_multiplier_early[None, :] - distance_tile) / smoothing_epsilon
    )
    text_multiplier_later = (
        smoothing_epsilon * math.log(goal_aggregate) - smoothing_epsilon * horizontal_lse_later
    )
    vertical_lse_later = column_logsumexp(
        (text_multiplier_later[:, None] - distance_tile) / smoothing_epsilon
    )
    transport_plan_later = jnp.exp(
        (text_multiplier_later[:, None] - distance_tile) / smoothing_epsilon
        - vertical_lse_later[None, :]
    )
    backward_signal = scaling_mass * transport_plan_later
    text_sensitivity_later = 1.0 - scaling_mass * doc_sum(jnp.sum(transport_plan_later, axis=1))
    horizontal_items_later = jnp.exp(
        (goal_multiplier_early[None, :] - distance_tile) / smoothing_epsilon
        - horizontal_lse_later[:, None]
    )
    weighted_two = text_sensitivity_later[:, None] * horizontal_items_later
    backward_signal = backward_signal + weighted_two
    target_bar_one = -lax.psum(jnp.sum(weighted_two, axis=0), "row")
    transport_plan_early = jnp.exp(
        (text_multiplier_early[:, None] - distance_tile) / smoothing_epsilon
        - vertical_lse_early[None, :]
    )
    weighted_one = target_bar_one[None, :] * transport_plan_early
    backward_signal = backward_signal + weighted_one
    text_sensitivity_early = -doc_sum(jnp.sum(weighted_one, axis=1))
    row_entries_first = jnp.exp(
        (starting_goal_multiplier[None, :] - distance_tile) / smoothing_epsilon
        - horizontal_lse_early[:, None]
    )
    backward_signal = backward_signal + text_sensitivity_early[:, None] * row_entries_first
    doc_weight = jnp.sum(backward_signal, axis=1)
    target_weight = jnp.sum(backward_signal, axis=0)
    doc_share = embed_docs.shape[0]
    target_share = embed_targets.shape[0]
    horizontal_items = doc_block
    weights = doc_weight
    doc_whole = lax.psum(
        2.0
        * (
            weights[:, None] * horizontal_items
            - jnp.dot(backward_signal, target_block, precision=highest)
        ),
        "col",
    )
    grad_docs = lax.dynamic_slice_in_dim(doc_whole, lax.axis_index("col") * doc_share, doc_share, 0)
    horizontal_items = target_block
    weights = target_weight
    crossed = lax.dot_general(
        backward_signal, doc_block, (((0,), (0,)), ((), ())), precision=highest
    )
    target_whole = lax.psum(2.0 * (weights[:, None] * horizontal_items - crossed), "row")
    grad_targets = lax.dynamic_slice_in_dim(
        target_whole, lax.axis_index("row") * target_share, target_share, 0
    )
    return (grad_docs, grad_targets)


def solution(mesh):
    return jax.shard_map(
        local,
        mesh=mesh,
        in_specs=(P(("row", "col"), None), P(("col", "row"), None), P("col")),
        out_specs=(P(("row", "col"), None), P(("col", "row"), None)),
        check_vma=False,
    )
```

profile of v0, /device:TPU:7, one launch (start us, length us, event | category | flops | bytes accessed | tf_op | source)
XLA Modules:
  0.0 868.3 jit_solution(1983940288596890704)
XLA Ops:
  8.7 56.7 %all-gather.3.cloned.1.call-done = f32[1024,256]{1,0:T(8,128)} async-done(((f32[64,256]{1,0:T(8,128)}), f32[1024,256]{1,0:T(8,128)}) %all-gather.3.cloned.1.call-update) | async-done | bytes 1048592 | tf_op jit(solution)/shard_map/all_gather | solution.py:32
  66.9 35.2 %all-gather.5.cloned.1.call-done = f32[2048,256]{1,0:T(8,128)} async-done(((f32[128,256]{1,0:T(8,128)}), f32[2048,256]{1,0:T(8,128)}) %all-gather.5.cloned.1.call-update) | async-done | bytes 2097168 | tf_op jit(solution)/shard_map/all_gather | solution.py:31
  102.1 1.9 multiply_reduce_fusion
  104.0 12.0 %fusion.3 = (f32[1024]{0:T(1024)S(1)}, f32[1024,2048]{1,0:T(8,128)}) fusion(f32[2048]{0:T(1024)} %param.5, f32[1024,256]{1,0:T(8,128)} %all-gather.3.cloned.1.call-done, f32[2048,256]{1,0:T(8,128)} %all-gather.5.cloned.1.call-done, f32[2048]{0:T(1024)S(1)} %multiply_reduce_fusion, f32[1024]{0:T(1024)S(1)} %multiply_reduce_fusion.1), kind=kOutput, calls=%fused_computation.16 | convolution fusion | flops 6455032832 | bytes 11558912 | tf_op jit(solution)/shard_map/dot_general | solution.py:38
  116.1 37.3 %pmax.28 = f32[1024]{0:T(1024)S(1)} all-reduce(f32[1024]{0:T(1024)S(1)} %get-tuple-element.11), channel_id=1, replica_groups=mesh['row'=16,'col'=16] {'col'}, use_global_device_ids=true, to_apply=%region_3.0 | all-reduce | flops 1024 | bytes 8192 | tf_op jit(solution)/shard_map/pmax | solution.py:12
  153.4 4.5 exponential_reduce_fusion.3
  157.9 32.6 %psum.63 = f32[1024]{0:T(1024)S(1)} all-reduce(f32[1024]{0:T(1024)S(1)} %exponential_reduce_fusion.3), channel_id=1, replica_groups=mesh['row'=16,'col'=16] {'col'}, use_global_device_ids=true, to_apply=%region_5.0 | all-reduce | flops 1024 | bytes 8192 | tf_op jit(solution)/shard_map/psum | solution.py:13
  190.5 4.3 fusion.4
  194.7 39.1 %pmax.29 = f32[2048]{0:T(1024)S(1)} all-reduce(f32[2048]{0:T(1024)S(1)} %fusion.4), channel_id=1, replica_groups=mesh['row'=16,'col'=16] {'row'}, use_global_device_ids=true, to_apply=%region_7.0 | all-reduce | flops 2048 | bytes 16384 | tf_op jit(solution)/shard_map/pmax | solution.py:18
  233.8 4.5 exponential_reduce_fusion.2
  238.3 27.7 %psum.64 = f32[2048]{0:T(1024)S(1)} all-reduce(f32[2048]{0:T(1024)S(1)} %exponential_reduce_fusion.2), channel_id=1, replica_groups=mesh['row'=16,'col'=16] {'row'}, use_global_device_ids=true, to_apply=%region_9.0 | all-reduce | flops 2048 | bytes 16384 | tf_op jit(solution)/shard_map/psum | solution.py:19
  266.0 4.3 fusion.5
  270.3 34.7 %pmax.30 = f32[1024]{0:T(1024)S(1)} all-reduce(f32[1024]{0:T(1024)S(1)} %fusion.5), channel_id=1, replica_groups=mesh['row'=16,'col'=16] {'col'}, use_global_device_ids=true, to_apply=%region_11.0 | all-reduce | flops 1024 | bytes 8192 | tf_op jit(solution)/shard_map/pmax | solution.py:12
  305.0 4.5 exponential_reduce_fusion.1
  309.5 32.3 %psum.65 = f32[1024]{0:T(1024)S(1)} all-reduce(f32[1024]{0:T(1024)S(1)} %exponential_reduce_fusion.1), channel_id=1, replica_groups=mesh['row'=16,'col'=16] {'col'}, use_global_device_ids=true, to_apply=%region_13.0 | all-reduce | flops 1024 | bytes 8192 | tf_op jit(solution)/shard_map/psum | solution.py:13
  341.8 4.3 fusion.6
  346.1 41.8 %pmax.31 = f32[2048]{0:T(1024)S(1)} all-reduce(f32[2048]{0:T(1024)S(1)} %fusion.6), channel_id=1, replica_groups=mesh['row'=16,'col'=16] {'row'}, use_global_device_ids=true, to_apply=%region_15.0 | all-reduce | flops 2048 | bytes 16384 | tf_op jit(solution)/shard_map/pmax | solution.py:18
  387.9 4.5 exponential_reduce_fusion
  392.4 27.7 %psum.66 = f32[2048]{0:T(1024)S(1)} all-reduce(f32[2048]{0:T(1024)S(1)} %exponential_reduce_fusion), channel_id=1, replica_groups=mesh['row'=16,'col'=16] {'row'}, use_global_device_ids=true, to_apply=%region_17.0 | all-reduce | flops 2048 | bytes 16384 | tf_op jit(solution)/shard_map/psum | solution.py:19
  420.1 4.5 fusion
  424.6 34.7 %psum.67 = f32[1024]{0:T(1024)S(1)} all-reduce(f32[1024]{0:T(1024)S(1)} %fusion), channel_id=1, replica_groups=mesh['row'=16,'col'=16] {'col'}, use_global_device_ids=true, to_apply=%region_19.0 | all-reduce | flops 1024 | bytes 8192 | tf_op jit(solution)/shard_map/psum | solution.py:24
  459.4 4.5 fusion.1
  463.9 34.9 %psum.68 = f32[2048]{0:T(1024)S(1)} all-reduce(f32[2048]{0:T(1024)S(1)} %fusion.1), channel_id=1, replica_groups=mesh['row'=16,'col'=16] {'row'}, use_global_device_ids=true, to_apply=%region_21.0 | all-reduce | flops 2048 | bytes 16384 | tf_op jit(solution)/shard_map/psum | solution.py:76
  498.8 4.7 fusion.2
  503.5 32.3 %psum.69 = f32[1024]{0:T(1024)S(1)} all-reduce(f32[1024]{0:T(1024)S(1)} %fusion.2), channel_id=1, replica_groups=mesh['row'=16,'col'=16] {'col'}, use_global_device_ids=true, to_apply=%region_23.0 | all-reduce | flops 1024 | bytes 8192 | tf_op jit(solution)/shard_map/psum | solution.py:24
  535.8 10.9 %fusion.9 = (f32[2048]{0:T(1024)S(1)}, f32[1024]{0:T(1024)S(1)}, f32[1024,2048]{1,0:T(8,128)S(1)}) fusion(f32[1024]{0:T(1024)S(1)} %get-tuple-element.10, f32[1024,2048]{1,0:T(8,128)} %get-tuple-element.12, f32[2048]{0:T(1024)S(1)} %copy-done.3, f32[1024]{0:T(1024)S(1)} %neg.7, f32[2048]{0:T(1024)S(1)} %get-tuple-element.8, f32[1024]{0:T(1024)S(1)} %get-tuple-element.9, ...), kind=kLoop, calls=%fused_computation.36 | loop fusion | flops 44037120 | bytes 16855040 | tf_op jit(solution)/shard_map/reduce_sum | solution.py:90
  546.7 3.2 copy-done
  549.9 7.7 fusion.8
  557.9 16.6 %fusion.7 = f32[2048,256]{1,0:T(8,128)} fusion(f32[1024,2048]{1,0:T(8,128)} %copy-done, f32[1024,256]{1,0:T(8,128)S(1)} %copy-done.2, f32[2048,256]{1,0:T(8,128)S(1)} %copy-done.1, f32[2048]{0:T(1024)S(1)} %get-tuple-element.2), kind=kOutput, calls=%fused_computation.21 | convolution fusion | flops 6444023808 | bytes 13639680 | tf_op jit(solution)/shard_map/dot_general | solution.py:106
  574.6 147.4 %all-reduce.3.cloned.1.call-done = f32[1024,256]{1,0:T(8,128)} async-done(((f32[1024,256]{1,0:T(8,128)}), f32[1024,256]{1,0:T(8,128)}) %all-reduce.3.cloned.1.call-update) | async-done | bytes 1048592 | tf_op jit(solution)/shard_map/psum | solution.py:95
  723.4 136.7 %all-reduce.5.cloned.1.call-done = f32[2048,256]{1,0:T(8,128)} async-done(((f32[2048,256]{1,0:T(8,128)}), f32[2048,256]{1,0:T(8,128)}) %all-reduce.5.cloned.1.call-update) | async-done | bytes 2097168 | tf_op jit(solution)/shard_map/psum | solution.py:109
  860.2 1.6 constant_dynamic-slice_fusion
  (24 shorter events, 4.8 us)
Async XLA Ops:
  7.2 58.3 %all-gather.3.cloned.1.call-start = ((), (), s32[]{:S(2)}) async-start(), calls=%async_computation | async-start | bytes 1114112 | tf_op jit(solution)/shard_map/all_gather | solution.py:32
  7.9 94.2 %all-gather.5.cloned.1.call-start = ((), (), s32[]{:S(2)}) async-start(), calls=%async_computation.1 | async-start | bytes 2228224 | tf_op jit(solution)/shard_map/all_gather | solution.py:31
  8.6 713.3 %all-reduce.3.cloned.1.call-start = ((), (), s32[]{:S(2)}) async-start(), calls=%async_computation.2 | async-start | bytes 2097152 | tf_op jit(solution)/shard_map/psum | solution.py:95
  104.0 49.3 %copy-start.3 = (f32[2048]{0:T(1024)S(1)}, f32[2048]{0:T(1024)}, u32[]{:S(2)}) copy-start(f32[2048]{0:T(1024)} %param.5) | copy-start | bytes 24580
  535.8 14.1 %copy-start.1 = (f32[2048,256]{1,0:T(8,128)S(1)}, f32[2048,256]{1,0:T(8,128)}, u32[]{:S(2)}) copy-start(f32[2048,256]{1,0:T(8,128)} %all-gather.5.cloned.1.call-done) | copy-start | bytes 6291460
  535.8 14.1 %copy-start.2 = (f32[1024,256]{1,0:T(8,128)S(1)}, f32[1024,256]{1,0:T(8,128)}, u32[]{:S(2)}) copy-start(f32[1024,256]{1,0:T(8,128)} %all-gather.3.cloned.1.call-done) | copy-start | bytes 3145732
  546.7 3.2 copy-start
  557.6 302.6 %all-reduce.5.cloned.1.call-start = ((), (), s32[]{:S(2)}) async-start(), calls=%async_computation.3 | async-start | bytes 4194304 | tf_op jit(solution)/shard_map/psum | solution.py:109
Sparse Core Ops, SparseCore 0:
  10.4 54.9 all-gather.2
  67.3 34.7 all-gather.4
  557.7 164.2 all-reduce.2
  724.7 135.4 all-reduce.4
where the time goes:
time: 869 us; the launch traced here: 868 us
  waiting for transfers between devices  378 us (43%)
  blocking collectives  375 us (43%)
  other arithmetic  58.8 us (7%)
  matrix products  36.3 us (4%)
  between operations  14 us (2%)
    psum x1, waiting for transfers between devices, local(): lax.psum(2.0 * (weights[:, None] * horizontal_items - jnp.dot(backward_si...  147 us
    psum x1, waiting for transfers between devices, local(): lax.psum(2.0 * (weights[:, None] * horizontal_items - crossed), 'row')  137 us
    pmax x2, blocking collectives, column_logsumexp(): largest = lax.pmax(jnp.max(similarity_grid, axis=0), 'row')  80.9 us
    pmax x2, blocking collectives, horizontal_softmax_norm(): largest = lax.pmax(jnp.max(similarity_grid, axis=1), 'col')  72 us
    psum x2, blocking collectives, doc_sum(): return lax.psum(values, 'col')  67 us
    psum x2, blocking collectives, horizontal_softmax_norm(): lax.psum(jnp.sum(jnp.exp(similarity_grid - largest[:, None]), axis=1), 'c...  64.9 us
    all_gather x1, waiting for transfers between devices, local(): doc_block = lax.all_gather(embed_docs, 'col', axis=0, tiled=True)  56.7 us
    psum x2, blocking collectives, column_logsumexp(): lax.psum(jnp.sum(jnp.exp(similarity_grid - largest[None, :]), axis=0), 'r...  55.3 us
  transfers between devices with their start and end apart: 4, of which 4 were waited for; matrix products, arithmetic and copies ran while one was open for 2% of the time, Pallas kernels for 0%

commit v1 on v0

v1 whole, which is shorter than its diff:
```python
import math

import jax
import jax.numpy as jnp
from jax import lax
from jax.sharding import PartitionSpec as P

smoothing_epsilon = 0.05
EXPONENT_MAX = 40.0
LOW, HIGH = 1e-25, 1e25
FIRST_LOW = 1e-9


def row_log_mass(scores):
    largest = lax.pmax(jnp.max(scores, axis=1), "col")
    mass_all = lax.psum(jnp.sum(jnp.exp(scores - largest[:, None]), axis=1), "col")
    return largest + jnp.log(mass_all)


def column_log_mass(scores):
    largest = lax.pmax(jnp.max(scores, axis=0), "row")
    mass_all = lax.psum(jnp.sum(jnp.exp(scores - largest[None, :]), axis=0), "row")
    return largest + jnp.log(mass_all)


def log_domain(embed_docs, embed_targets, doc_block, target_block, start):
    highest = lax.Precision.HIGHEST
    distance_tile = (
        jnp.sum(doc_block * doc_block, axis=1)[:, None]
        + jnp.sum(target_block * target_block, axis=1)[None, :]
        - 2.0 * jnp.dot(doc_block, target_block.T, precision=highest)
    )
    texts = distance_tile.shape[0] * lax.axis_size("row")
    goals = distance_tile.shape[1] * lax.axis_size("col")
    ratio = texts / goals
    t = smoothing_epsilon
    row_log_one = row_log_mass((start[None, :] - distance_tile) / t)
    doc_one = t * math.log(goals) - t * row_log_one
    col_log_one = column_log_mass((doc_one[:, None] - distance_tile) / t)
    target_one = t * math.log(texts) - t * col_log_one
    row_log_two = row_log_mass((target_one[None, :] - distance_tile) / t)
    doc_two = t * math.log(goals) - t * row_log_two
    col_log_two = column_log_mass((doc_two[:, None] - distance_tile) / t)
    plan = jnp.exp((doc_two[:, None] - distance_tile) / t - col_log_two[None, :])
    adjoint = ratio * plan
    doc_bar_two = 1.0 - ratio * lax.psum(jnp.sum(plan, axis=1), "col")
    plan = jnp.exp((target_one[None, :] - distance_tile) / t - row_log_two[:, None])
    weighted = doc_bar_two[:, None] * plan
    adjoint = adjoint + weighted
    target_bar_one = -lax.psum(jnp.sum(weighted, axis=0), "row")
    plan = jnp.exp((doc_one[:, None] - distance_tile) / t - col_log_one[None, :])
    weighted = target_bar_one[None, :] * plan
    adjoint = adjoint + weighted
    doc_bar_one = -lax.psum(jnp.sum(weighted, axis=1), "col")
    plan = jnp.exp((start[None, :] - distance_tile) / t - row_log_one[:, None])
    adjoint = adjoint + doc_bar_one[:, None] * plan
    doc_part = 2.0 * (
        jnp.sum(adjoint, axis=1)[:, None] * doc_block
        - jnp.dot(adjoint, target_block, precision=highest)
    )
    crossed = lax.dot_general(adjoint, doc_block, (((0,), (0,)), ((), ())), precision=highest)
    target_part = 2.0 * (jnp.sum(adjoint, axis=0)[:, None] * target_block - crossed)
    share, target_share = embed_docs.shape[0], embed_targets.shape[0]
    doc_whole, target_whole = lax.psum(doc_part, "col"), lax.psum(target_part, "row")
    return (
        lax.dynamic_slice_in_dim(doc_whole, lax.axis_index("col") * share, share, 0),
        lax.dynamic_slice_in_dim(
            target_whole, lax.axis_index("row") * target_share, target_share, 0
        ),
    )


def swap(blocks, axis):
    return lax.all_to_all(blocks, axis, 0, 0)


def gather(block, axis):
    devices = lax.axis_size(axis)
    pieces = swap(jnp.broadcast_to(block[None], (devices, *block.shape)), axis)
    return pieces.reshape(devices * block.shape[0], *block.shape[1:])


def total(vector, axis):
    return jnp.sum(swap(jnp.broadcast_to(vector[None], (lax.axis_size(axis), *vector.shape)), axis), axis=0)


def scatter(block, axis):
    devices = lax.axis_size(axis)
    pieces = block.reshape(devices, block.shape[0] // devices, *block.shape[1:])
    return jnp.sum(swap(pieces, axis), axis=0)


def inverse(mass, low, high):
    return jnp.where((mass >= low) & (mass <= high), 1.0 / mass, jnp.nan)


def local(embed_docs, embed_targets, start):
    t = smoothing_epsilon
    high = lax.Precision.HIGH
    targets = gather(embed_targets, "row")
    docs = gather(embed_docs, "col")
    texts, goals = docs.shape[0] * lax.axis_size("row"), targets.shape[0] * lax.axis_size("col")
    ratio = texts / goals
    exponent = (2.0 / t) * jnp.dot(docs, targets.T, precision=high)
    fits = jnp.max(jnp.abs(exponent)) <= EXPONENT_MAX
    kernel = jnp.exp(exponent)

    def rows(weight):
        return total(jnp.sum(kernel * weight[None, :], axis=1), "col")

    def columns(weight):
        return total(jnp.sum(kernel * weight[:, None], axis=0), "row")

    target_zero = jnp.exp((start - jnp.sum(targets * targets, axis=1)) / t)
    target_zero = jnp.where(fits, target_zero, jnp.nan)
    doc_one = inverse(rows(target_zero), FIRST_LOW, HIGH)
    target_one = inverse(columns(doc_one), LOW, HIGH)
    doc_two = inverse(rows(target_one), LOW, HIGH)
    target_two = inverse(columns(doc_two), LOW, HIGH)
    mass = rows(target_two)
    doc_bar_two = 1.0 - ratio * doc_two * mass
    weighted_two = doc_two * doc_bar_two
    weighted_one = -target_one * target_one * columns(weighted_two)
    weighted_zero = -doc_one * doc_one * rows(weighted_one)
    first = weighted_zero[:, None] * target_zero[None, :]
    adjoint = kernel * (
        ratio * doc_two[:, None] * target_two[None, :]
        + weighted_two[:, None] * target_one[None, :]
        + doc_one[:, None] * weighted_one[None, :]
        + first
    )
    column_mass = ratio / lax.axis_size("row") + jnp.sum(kernel * first, axis=0)
    doc_part = jnp.dot(adjoint, targets, precision=high)
    crossed = lax.dot_general(adjoint, docs, (((0,), (0,)), ((), ())), precision=high)
    grad_docs = 2.0 * (embed_docs - scatter(doc_part, "col"))
    grad_targets = scatter(2.0 * (column_mass[:, None] * targets - crossed), "row")
    return lax.cond(
        jnp.isnan(jnp.sum(mass)),
        lambda: log_domain(embed_docs, embed_targets, docs, targets, start),
        lambda: (grad_docs, grad_targets),
    )


def solution(mesh):
    return jax.shard_map(
        local,
        mesh=mesh,
        in_specs=(P(("row", "col"), None), P(("col", "row"), None), P("col")),
        out_specs=(P(("row", "col"), None), P(("col", "row"), None)),
        check_vma=False,
    )
```

time: 869 us -> 1060 us (1.22); the launches traced: 868 us -> 1050 us
  blocking collectives: 375 us -> 521 us
  waiting for transfers between devices: 378 us -> 328 us
  other arithmetic: 58.8 us -> 97 us
  matrix products: 36.3 us -> 57.4 us
  starting transfers between devices: 0.42 us -> 14.6 us
    all_to_all x0 -> x9, blocking collectives: none -> 151 us  [swap(): return lax.all_to_all(blocks, axis, 0, 0)]
    all_gather x2 -> x0, waiting for transfers between devices: 92 us -> none  [the longest x1 56.7 us: local(): doc_block = lax.all_gather(embed_docs, 'col', axis=0, tiled=True)]
    all_to_all x0 -> x2, waiting for transfers between devices: none -> 43.8 us  [swap(): return lax.all_to_all(blocks, axis, 0, 0)]
    reduce_sum x10 -> x26, other arithmetic: 45.9 us -> 84 us  [the longest x4 19.3 us: rows(): return total(jnp.sum(kernel * weight[None, :], axis=1), 'col')]
    dot_general x3 -> x6, matrix products: 36.3 us -> 57.4 us  [the longest x1 16.6 us: log_domain(): lax.dot_general(adjoint, doc_block, (((0,), (0,)), ((), ())), precision=h...]
    all_to_all x0 -> x2, starting transfers between devices: none -> 14.1 us  [swap(): return lax.all_to_all(blocks, axis, 0, 0)]
  transfers between devices with their start and end apart: 4 -> 4, of which waited for: 4 -> 4; matrix products, arithmetic and copies ran while one was open for 2% -> 3% of each run, Pallas kernels for 0% -> 0%
where the time goes in v1:
time: 1060 us; the launch traced here: 1050 us
  blocking collectives  521 us (49%)
  waiting for transfers between devices  328 us (31%)
  other arithmetic  97 us (9%)
  matrix products  57.4 us (5%)
  between operations  16.7 us (2%)
  starting transfers between devices  14.6 us (1%)
  local copies, waits for them, and re-layouts  11.9 us (1%)
    all_to_all x9, blocking collectives, swap(): return lax.all_to_all(blocks, axis, 0, 0)  151 us
    psum x1, waiting for transfers between devices, log_domain(): lax.psum(doc_part, 'col')  147 us
    psum x1, waiting for transfers between devices, log_domain(): lax.psum(target_part, 'row')  137 us
    pmax x2, blocking collectives, column_log_mass(): largest = lax.pmax(jnp.max(scores, axis=0), 'row')  78.6 us
    pmax x2, blocking collectives, row_log_mass(): largest = lax.pmax(jnp.max(scores, axis=1), 'col')  67.9 us
    psum x2, blocking collectives, row_log_mass(): lax.psum(jnp.sum(jnp.exp(scores - largest[:, None]), axis=1), 'col')  66.6 us
    psum x2, blocking collectives, column_log_mass(): lax.psum(jnp.sum(jnp.exp(scores - largest[None, :]), axis=0), 'row')  55.4 us
    all_to_all x2, waiting for transfers between devices, swap(): return lax.all_to_all(blocks, axis, 0, 0)  43.8 us
  transfers between devices with their start and end apart: 4, of which 4 were waited for; matrix products, arithmetic and copies ran while one was open for 3% of the time, Pallas kernels for 0%

profile of v1, /device:TPU:7, one launch (start us, length us, event | category | flops | bytes accessed | tf_op | source)
XLA Modules:
  0.0 1046.2 jit_solution(15669526793586689454)
XLA Ops:
  8.1 38.1 %all_to_all.62 = f32[16,64,256]{2,1,0:T(8,128)S(1)} all-to-all(f32[16,64,256]{2,1,0:T(8,128)S(1)} %broadcast_in_dim.30), channel_id=1, replica_groups=mesh['row'=16,'col'=16] {'col'}, dimensions={0} | all-to-all | bytes 2097152 | tf_op jit(solution)/shard_map/all_to_all | solution.py:74
  47.3 33.9 %all_to_all.63 = f32[16,128,256]{2,1,0:T(8,128)S(1)} all-to-all(f32[16,128,256]{2,1,0:T(8,128)S(1)} %broadcast_in_dim.31), channel_id=1, replica_groups=mesh['row'=16,'col'=16] {'row'}, dimensions={0} | all-to-all | bytes 4194304 | tf_op jit(solution)/shard_map/all_to_all | solution.py:74
  93.5 12.0 %all_to_all.64 = f32[16,1,1024]{2,1,0:T(1,128)S(1)} all-to-all(f32[16,1,1024]{2,1,0:T(1,128)S(1)} %broadcast_in_dim.33), channel_id=1, replica_groups=mesh['row'=16,'col'=16] {'col'}, dimensions={0} | all-to-all | bytes 131072 | tf_op jit(solution)/shard_map/all_to_all | solution.py:74
  110.0 10.5 %all_to_all.65 = f32[16,1,2048]{2,1,0:T(1,128)S(1)} all-to-all(f32[16,1,2048]{2,1,0:T(1,128)S(1)} %broadcast_in_dim.35), channel_id=1, replica_groups=mesh['row'=16,'col'=16] {'row'}, dimensions={0} | all-to-all | bytes 262144 | tf_op jit(solution)/shard_map/all_to_all | solution.py:74
  125.5 11.7 %all_to_all.66 = f32[16,1,1024]{2,1,0:T(1,128)S(1)} all-to-all(f32[16,1,1024]{2,1,0:T(1,128)S(1)} %broadcast_in_dim.36), channel_id=1, replica_groups=mesh['row'=16,'col'=16] {'col'}, dimensions={0} | all-to-all | bytes 131072 | tf_op jit(solution)/shard_map/all_to_all | solution.py:74
  141.7 10.3 all_to_all.67
  157.0 12.0 %all_to_all.68 = f32[16,1,1024]{2,1,0:T(1,128)S(1)} all-to-all(f32[16,1,1024]{2,1,0:T(1,128)S(1)} %broadcast_in_dim.38), channel_id=1, replica_groups=mesh['row'=16,'col'=16] {'col'}, dimensions={0} | all-to-all | bytes 131072 | tf_op jit(solution)/shard_map/all_to_all | solution.py:74
  174.1 10.3 all_to_all.69
  189.4 11.8 %all_to_all.70 = f32[16,1,1024]{2,1,0:T(1,128)S(1)} all-to-all(f32[16,1,1024]{2,1,0:T(1,128)S(1)} %broadcast_in_dim.40), channel_id=1, replica_groups=mesh['row'=16,'col'=16] {'col'}, dimensions={0} | all-to-all | bytes 131072 | tf_op jit(solution)/shard_map/all_to_all | solution.py:74
  201.3 7.5 fusion.10
  221.3 11.7 %fusion.11 = f32[2048,256]{1,0:T(8,128)} fusion(f32[1024,2048]{1,0:T(8,128)} %copy-done.1, f32[1024,256]{1,0:T(8,128)S(1)} %bitcast.32, f32[2048,256]{1,0:T(8,128)S(1)} %bitcast.28, f32[2048]{0:T(1024)S(1)} %broadcast_add_fusion), kind=kOutput, calls=%fused_computation.51 | convolution fusion | flops 3222798336 | bytes 13639680 | tf_op jit(solution)/shard_map/dot_general | solution.py:134
  233.0 15.5 %all-to-all-done.9 = f32[16,64,256]{2,1,0:T(8,128)} async-done(((f32[16,64,256]{2,1,0:T(8,128)}), f32[16,64,256]{2,1,0:T(8,128)}, u32[]{:S(2)}, u32[]{:S(2)}) %all-to-all-start.9) | async-done | bytes 1048608 | tf_op jit(solution)/shard_map/all_to_all | solution.py:74
  248.4 9.4 all-to-all-start.10
  259.1 28.4 %all-to-all-done.10 = f32[16,128,256]{2,1,0:T(8,128)} async-done(((f32[16,128,256]{2,1,0:T(8,128)}), f32[16,128,256]{2,1,0:T(8,128)}, u32[]{:S(2)}, u32[]{:S(2)}) %all-to-all-start.10) | async-done | bytes 2097184 | tf_op jit(solution)/shard_map/all_to_all | solution.py:74
  287.5 751.4 %conditional.1 = (f32[64,256]{1,0:T(8,128)}, f32[128,256]{1,0:T(8,128)}) conditional(s32[]{:T(128)} %convert_element_type.3, (f32[16,64,256]{2,1,0:T(8,128)}, f32[64,256]{1,0:T(8,128)S(1)}, f32[16,128,256]{2,1,0:T(8,128)}) %tuple.40, (f32[2048]{0:T(1024)S(1)}, f32[1024,256]{1,0:T(8,128)S(1)}, f32[2048,256]{1,0:T(8,128)S(1)}) %tuple.41), branch_computations={%region_18.21_spmd, %region_21.50_spmd} | conditional | flops 19470495744 | bytes 194937168 | solution.py:137
  288.2 10.5 %fusion.3 = (f32[1024]{0:T(1024)S(1)}, f32[1024,2048]{1,0:T(8,128)}) fusion(f32[2048]{0:T(1024)S(1)} %get-tuple-element.25, f32[1024,256]{1,0:T(8,128)S(1)} %get-tuple-element.26, f32[2048,256]{1,0:T(8,128)S(1)} %get-tuple-element.27, f32[2048]{0:T(1024)S(1)} %multiply_reduce_fusion, f32[1024]{0:T(1024)S(1)} %multiply_reduce_fusion.1), kind=kOutput, calls=%fused_computation.17 | convolution fusion | flops 6455032832 | bytes 11558912 | tf_op jit(solution)/shard_map/cond/branch_1_fun/dot_general | solution.py:31
  298.7 33.8 %pmax.24 = f32[1024]{0:T(1024)S(1)} all-reduce(f32[1024]{0:T(1024)S(1)} %get-tuple-element.43), channel_id=1, replica_groups=mesh['row'=16,'col'=16] {'col'}, use_global_device_ids=true, to_apply=%region_25.25 | all-reduce | flops 1024 | bytes 8192 | tf_op jit(solution)/shard_map/cond/branch_1_fun/pmax | solution.py:15
  337.0 33.4 %psum.54 = f32[1024]{0:T(1024)S(1)} all-reduce(f32[1024]{0:T(1024)S(1)} %exponential_reduce_fusion.3), channel_id=1, replica_groups=mesh['row'=16,'col'=16] {'col'}, use_global_device_ids=true, to_apply=%region_27.27 | all-reduce | flops 1024 | bytes 8192 | tf_op jit(solution)/shard_map/cond/branch_1_fun/psum | solution.py:16
  374.6 37.0 %pmax.25 = f32[2048]{0:T(1024)S(1)} all-reduce(f32[2048]{0:T(1024)S(1)} %fusion.4), channel_id=1, replica_groups=mesh['row'=16,'col'=16] {'row'}, use_global_device_ids=true, to_apply=%region_29.29 | all-reduce | flops 2048 | bytes 16384 | tf_op jit(solution)/shard_map/cond/branch_1_fun/pmax | solution.py:21
  416.2 27.8 %psum.55 = f32[2048]{0:T(1024)S(1)} all-reduce(f32[2048]{0:T(1024)S(1)} %exponential_reduce_fusion.2), channel_id=1, replica_groups=mesh['row'=16,'col'=16] {'row'}, use_global_device_ids=true, to_apply=%region_31.31 | all-reduce | flops 2048 | bytes 16384 | tf_op jit(solution)/shard_map/cond/branch_1_fun/psum | solution.py:22
  448.2 34.1 %pmax.26 = f32[1024]{0:T(1024)S(1)} all-reduce(f32[1024]{0:T(1024)S(1)} %fusion.5), channel_id=1, replica_groups=mesh['row'=16,'col'=16] {'col'}, use_global_device_ids=true, to_apply=%region_33.33 | all-reduce | flops 1024 | bytes 8192 | tf_op jit(solution)/shard_map/cond/branch_1_fun/pmax | solution.py:15
  486.8 33.3 %psum.56 = f32[1024]{0:T(1024)S(1)} all-reduce(f32[1024]{0:T(1024)S(1)} %exponential_reduce_fusion.1), channel_id=1, replica_groups=mesh['row'=16,'col'=16] {'col'}, use_global_device_ids=true, to_apply=%region_35.35 | all-reduce | flops 1024 | bytes 8192 | tf_op jit(solution)/shard_map/cond/branch_1_fun/psum | solution.py:16
  524.4 41.6 %pmax.27 = f32[2048]{0:T(1024)S(1)} all-reduce(f32[2048]{0:T(1024)S(1)} %fusion.6), channel_id=1, replica_groups=mesh['row'=16,'col'=16] {'row'}, use_global_device_ids=true, to_apply=%region_37.37 | all-reduce | flops 2048 | bytes 16384 | tf_op jit(solution)/shard_map/cond/branch_1_fun/pmax | solution.py:21
  570.5 27.7 %psum.57 = f32[2048]{0:T(1024)S(1)} all-reduce(f32[2048]{0:T(1024)S(1)} %exponential_reduce_fusion), channel_id=1, replica_groups=mesh['row'=16,'col'=16] {'row'}, use_global_device_ids=true, to_apply=%region_39.39 | all-reduce | flops 2048 | bytes 16384 | tf_op jit(solution)/shard_map/cond/branch_1_fun/psum | solution.py:22
  602.7 33.8 %psum.58 = f32[1024]{0:T(1024)S(1)} all-reduce(f32[1024]{0:T(1024)S(1)} %fusion), channel_id=1, replica_groups=mesh['row'=16,'col'=16] {'col'}, use_global_device_ids=true, to_apply=%region_41.41 | all-reduce | flops 1024 | bytes 8192 | tf_op jit(solution)/shard_map/cond/branch_1_fun/psum | solution.py:46
  641.0 34.9 %psum.59 = f32[2048]{0:T(1024)S(1)} all-reduce(f32[2048]{0:T(1024)S(1)} %fusion.1), channel_id=1, replica_groups=mesh['row'=16,'col'=16] {'row'}, use_global_device_ids=true, to_apply=%region_43.43 | all-reduce | flops 2048 | bytes 16384 | tf_op jit(solution)/shard_map/cond/branch_1_fun/psum | solution.py:50
  680.5 32.8 %psum.60 = f32[1024]{0:T(1024)S(1)} all-reduce(f32[1024]{0:T(1024)S(1)} %fusion.2), channel_id=1, replica_groups=mesh['row'=16,'col'=16] {'col'}, use_global_device_ids=true, to_apply=%region_45.45 | all-reduce | flops 1024 | bytes 8192 | tf_op jit(solution)/shard_map/cond/branch_1_fun/psum | solution.py:54
  713.3 10.7 %fusion.17 = (f32[2048]{0:T(1024)S(1)}, f32[1024]{0:T(1024)S(1)}, f32[1024,2048]{1,0:T(8,128)S(1)}) fusion(f32[1024]{0:T(1024)S(1)} %get-tuple-element.42, f32[1024,2048]{1,0:T(8,128)} %get-tuple-element.44, f32[2048]{0:T(1024)S(1)} %get-tuple-element.25, f32[1024]{0:T(1024)S(1)} %neg.17, f32[2048]{0:T(1024)S(1)} %get-tuple-element.40, ...), kind=kLoop, calls=%fused_computation.68 | loop fusion | flops 44037120 | bytes 16855040 | tf_op jit(solution)/shard_map/cond/branch_1_fun/reduce_sum | solution.py:62
  727.3 7.7 fusion.8
  735.3 16.6 %fusion.7 = f32[2048,256]{1,0:T(8,128)} fusion(f32[1024,2048]{1,0:T(8,128)} %copy-done, f32[1024,256]{1,0:T(8,128)S(1)} %get-tuple-element.26, f32[2048,256]{1,0:T(8,128)S(1)} %get-tuple-element.27, f32[2048]{0:T(1024)S(1)} %get-tuple-element.32), kind=kOutput, calls=%fused_computation.22 | convolution fusion | flops 6444023808 | bytes 13639680 | tf_op jit(solution)/shard_map/cond/branch_1_fun/dot_general | solution.py:61
  751.9 146.8 %all-reduce.3.cloned.1.call-done = f32[1024,256]{1,0:T(8,128)} async-done(((f32[1024,256]{1,0:T(8,128)}), f32[1024,256]{1,0:T(8,128)}) %all-reduce.3.cloned.1.call-update) | async-done | bytes 1048592 | tf_op jit(solution)/shard_map/cond/branch_1_fun/psum | solution.py:64
  900.2 136.9 %all-reduce.5.cloned.1.call-done = f32[2048,256]{1,0:T(8,128)} async-done(((f32[2048,256]{1,0:T(8,128)}), f32[2048,256]{1,0:T(8,128)}) %all-reduce.5.cloned.1.call-update) | async-done | bytes 2097168 | tf_op jit(solution)/shard_map/cond/branch_1_fun/psum | solution.py:64
  (69 shorter events, 106.9 us)
Async XLA Ops:
  81.2 7.4 copy-start.3
  208.8 3.2 copy-start.1
  216.5 31.9 %all-to-all-start.9 = ((f32[16,64,256]{2,1,0:T(8,128)}), f32[16,64,256]{2,1,0:T(8,128)}, u32[]{:S(2)}, u32[]{:S(2)}) async-start(f32[16,64,256]{2,1,0:T(8,128)} %fusion.19), calls=%async_computation.9 | async-start | bytes 2097152 | tf_op jit(solution)/shard_map/all_to_all | solution.py:74
  221.3 66.2 %copy-start.2 = (f32[64,256]{1,0:T(8,128)S(1)}, f32[64,256]{1,0:T(8,128)}, u32[]{:S(2)}) copy-start(f32[64,256]{1,0:T(8,128)} %param.5) | copy-start | bytes 196612
  248.4 39.0 %all-to-all-start.10 = ((f32[16,128,256]{2,1,0:T(8,128)}), f32[16,128,256]{2,1,0:T(8,128)}, u32[]{:S(2)}, u32[]{:S(2)}) async-start(f32[16,128,256]{2,1,0:T(8,128)} %bitcast.34), calls=%async_computation.10 | async-start | bytes 4194304 | tf_op jit(solution)/shard_map/all_to_all | solution.py:74
  287.5 611.2 %all-reduce.3.cloned.1.call-start = ((), (), s32[]{:S(2)}) async-start(), calls=%async_computation.11 | async-start | bytes 2097152 | tf_op jit(solution)/shard_map/cond/branch_1_fun/psum | solution.py:64
  724.0 3.2 copy-start
  735.0 302.1 %all-reduce.5.cloned.1.call-start = ((), (), s32[]{:S(2)}) async-start(), calls=%async_computation.12 | async-start | bytes 4194304 | tf_op jit(solution)/shard_map/cond/branch_1_fun/psum | solution.py:64
Sparse Core Ops, SparseCore 0:
  735.1 163.5 all-reduce.2
  901.5 135.4 all-reduce.4

commit v2 on v1

v2 whole, which is shorter than its diff:
```python
import math
from functools import partial

import jax
import jax.numpy as jnp
from jax import lax
from jax.experimental import pallas as pl
from jax.experimental.pallas import tpu as pltpu
from jax.sharding import PartitionSpec as P

smoothing_epsilon = 0.05
EXPONENT_MAX = 40.0
LOW, HIGH = 1e-25, 1e25
FIRST_LOW = 1e-9
KEPT, HELD = (0,), (0,)


def row_log_mass(scores):
    largest = lax.pmax(jnp.max(scores, axis=1), "col")
    mass_all = lax.psum(jnp.sum(jnp.exp(scores - largest[:, None]), axis=1), "col")
    return largest + jnp.log(mass_all)


def column_log_mass(scores):
    largest = lax.pmax(jnp.max(scores, axis=0), "row")
    mass_all = lax.psum(jnp.sum(jnp.exp(scores - largest[None, :]), axis=0), "row")
    return largest + jnp.log(mass_all)


def log_domain(doc_block, target_block, start):
    highest = lax.Precision.HIGHEST
    distance_tile = (
        jnp.sum(doc_block * doc_block, axis=1)[:, None]
        + jnp.sum(target_block * target_block, axis=1)[None, :]
        - 2.0 * jnp.dot(doc_block, target_block.T, precision=highest)
    )
    texts = distance_tile.shape[0] * lax.axis_size("row")
    goals = distance_tile.shape[1] * lax.axis_size("col")
    ratio = texts / goals
    t = smoothing_epsilon
    row_log_one = row_log_mass((start[None, :] - distance_tile) / t)
    doc_one = t * math.log(goals) - t * row_log_one
    col_log_one = column_log_mass((doc_one[:, None] - distance_tile) / t)
    target_one = t * math.log(texts) - t * col_log_one
    row_log_two = row_log_mass((target_one[None, :] - distance_tile) / t)
    doc_two = t * math.log(goals) - t * row_log_two
    col_log_two = column_log_mass((doc_two[:, None] - distance_tile) / t)
    plan = jnp.exp((doc_two[:, None] - distance_tile) / t - col_log_two[None, :])
    adjoint = ratio * plan
    doc_bar_two = 1.0 - ratio * lax.psum(jnp.sum(plan, axis=1), "col")
    plan = jnp.exp((target_one[None, :] - distance_tile) / t - row_log_two[:, None])
    weighted = doc_bar_two[:, None] * plan
    adjoint = adjoint + weighted
    target_bar_one = -lax.psum(jnp.sum(weighted, axis=0), "row")
    plan = jnp.exp((doc_one[:, None] - distance_tile) / t - col_log_one[None, :])
    weighted = target_bar_one[None, :] * plan
    adjoint = adjoint + weighted
    doc_bar_one = -lax.psum(jnp.sum(weighted, axis=1), "col")
    plan = jnp.exp((start[None, :] - distance_tile) / t - row_log_one[:, None])
    adjoint = adjoint + doc_bar_one[:, None] * plan
    doc_part = 2.0 * (
        jnp.sum(adjoint, axis=1)[:, None] * doc_block
        - jnp.dot(adjoint, target_block, precision=highest)
    )
    crossed = lax.dot_general(adjoint, doc_block, (((0,), (0,)), ((), ())), precision=highest)
    target_part = 2.0 * (jnp.sum(adjoint, axis=0)[:, None] * target_block - crossed)
    return scatter(doc_part, "col"), scatter(target_part, "row")


LANES = 128
f32, bf16 = jnp.float32, jnp.bfloat16


def swap(blocks, axis):
    return lax.all_to_all(blocks, axis, 0, 0)


def gather(block, axis):
    devices = lax.axis_size(axis)
    pieces = swap(jnp.broadcast_to(block[None], (devices, *block.shape)), axis)
    return pieces.reshape(devices * block.shape[0], *block.shape[1:])


def scatter(block, axis):
    devices = lax.axis_size(axis)
    pieces = block.reshape(devices, block.shape[0] // devices, *block.shape[1:])
    return jnp.sum(swap(pieces, axis), axis=0)


def inverse(mass, low, high):
    return jnp.where((mass >= low) & (mass <= high), 1.0 / mass, jnp.nan)


def halves(values):
    top = values.astype(bf16)
    return top, (values - top.astype(f32)).astype(bf16)


def spans(size, step):
    return [slice(i, i + step) for i in range(0, size, step)]


def upright(vector):
    return jnp.transpose(jnp.broadcast_to(vector, (LANES, LANES)))


def lane_total(block):
    return jnp.sum(jnp.transpose(block), axis=0, keepdims=True)


def row_sums(tile, weight):
    out = []
    for rows in spans(tile.shape[0], LANES):
        acc = None
        for c, cols in enumerate(spans(tile.shape[1], LANES)):
            term = tile[rows, cols] * weight[c : c + 1, :]
            acc = term if acc is None else acc + term
        out.append(lane_total(acc))
    return jnp.concatenate(out, axis=0)


def column_sums(tile, weight):
    columns = spans(tile.shape[1], LANES)
    acc = [None] * len(columns)
    for r, rows in enumerate(spans(tile.shape[0], LANES)):
        factor = upright(weight[r : r + 1, :])
        for c, cols in enumerate(columns):
            term = jnp.sum((tile[rows, cols] * factor).reshape(-1, 8, LANES), axis=0)
            acc[c] = term if acc[c] is None else acc[c] + term
    return jnp.concatenate([jnp.sum(a, axis=0, keepdims=True) for a in acc], axis=0)


def spread(ref, values):
    ref[...] = jnp.broadcast_to(values[None], ref.shape)


def kernel_tile(docs, targets, start, tile, weight_out, part, doc_wide, target_wide):
    features = docs.shape[1]
    for source, wide, order in ((docs, doc_wide, (0, 0, 1)), (targets, target_wide, (0, 1, 0))):
        for rows in spans(source.shape[0], 256):
            pair = halves(source[rows, :])
            for k, which in enumerate(order):
                wide[rows, k * features : (k + 1) * features] = pair[which]
    largest = None
    for cols in spans(targets.shape[0], 256):
        dots = lax.dot_general(
            doc_wide[...], target_wide[cols, :], (((1,), (1,)), ((), ())), preferred_element_type=f32
        )
        dots = dots * (2.0 / smoothing_epsilon)
        tile[:, cols] = jnp.exp(dots)
        peak = jnp.max(jnp.abs(dots).reshape(-1, 8, 256), axis=0)
        largest = peak if largest is None else jnp.maximum(largest, peak)
    fits = jnp.max(largest) <= EXPONENT_MAX
    norms = []
    for rows in spans(targets.shape[0], LANES):
        squares = targets[rows, :] * targets[rows, :]
        norms.append(lane_total(sum(squares[:, cols] for cols in spans(features, LANES))))
    weight = jnp.exp((start[...] - jnp.concatenate(norms, axis=0)) / smoothing_epsilon)
    weight = jnp.where(fits, weight, jnp.nan)
    weight_out[...] = weight
    spread(part, row_sums(tile, weight))


def kernel_doc_one(tile, parts, weight_out, part):
    weight = inverse(jnp.sum(parts[...], axis=0), FIRST_LOW, HIGH)
    weight_out[...] = weight
    spread(part, column_sums(tile, weight))


def kernel_doc_two(tile, parts, weight_out, part):
    weight = inverse(jnp.sum(parts[...], axis=0), LOW, HIGH)
    weight_out[...] = weight
    spread(part, column_sums(tile, weight))


def kernel_target(tile, parts, weight_out, part):
    weight = inverse(jnp.sum(parts[...], axis=0), LOW, HIGH)
    weight_out[...] = weight
    spread(part, row_sums(tile, weight))


def kernel_bar_two(ratio, tile, parts, doc_two, weight_out, part):
    scale = doc_two[...]
    weight = scale * (1.0 - ratio * scale * jnp.sum(parts[...], axis=0))
    weight_out[...] = weight
    spread(part, column_sums(tile, weight))


def kernel_bar_one(tile, parts, target_one, weight_out, part):
    scale = target_one[...]
    weight = -scale * scale * jnp.sum(parts[...], axis=0)
    weight_out[...] = weight
    spread(part, row_sums(tile, weight))


def kernel_docs(ratio, tile, parts, doc_one, doc_two, bar_two, target_zero, target_one, target_two, bar_one,
                targets, top, low, mass, doc_part, factors, wide):
    features = targets.shape[1]
    for rows in spans(targets.shape[0], 256):
        pair = halves(targets[rows, :])
        wide[rows, :features], wide[rows, features:] = pair
    one = doc_one[...]
    bar_zero = -one * one * jnp.sum(parts[...], axis=0)
    by_row = (bar_zero, ratio * doc_two[...], bar_two[...], one)
    by_column = (target_zero[...], target_two[...], target_one[...], bar_one[...])
    columns = spans(tile.shape[1], LANES)
    acc = [None] * len(columns)
    for r, rows in enumerate(spans(tile.shape[0], LANES)):
        for k, values in enumerate(by_row):
            factors[k, rows, :] = upright(values[r : r + 1, :])
    for block in spans(tile.shape[0], 256):
        for rows in spans(256, 32):
            rows = slice(block.start + rows.start, block.start + rows.stop)
            a = [factors[k, rows, :] for k in range(4)]
            for c, cols in enumerate(columns):
                b = [v[c : c + 1, :] for v in by_column]
                adjoint = tile[rows, cols] * ((a[0] * b[0] + a[1] * b[1]) + (a[2] * b[2] + a[3] * b[3]))
                term = jnp.sum(adjoint.reshape(-1, 8, LANES), axis=0)
                acc[c] = term if acc[c] is None else acc[c] + term
                top[rows, cols], low[rows, cols] = halves(adjoint)
        both = jnp.dot(top[block, :], wide[...], preferred_element_type=f32)
        rest = jnp.dot(low[block, :], wide[:, :features], preferred_element_type=f32)
        doc_part[block, :] = (both[:, :features] + both[:, features:]) + rest
    mass[...] = jnp.concatenate([jnp.sum(a, axis=0, keepdims=True) for a in acc], axis=0)


def kernel_targets(top, low, mass, docs, targets, target_part, flat):
    features = docs.shape[1]
    for rows in spans(docs.shape[0], 256):
        pair = halves(jnp.transpose(docs[rows, :]))
        flat[:features, rows], flat[features:, rows] = pair
    for cols in spans(targets.shape[0], 256):
        both = jnp.dot(flat[...], top[:, cols], preferred_element_type=f32)
        rest = jnp.dot(flat[:features, :], low[:, cols], preferred_element_type=f32)
        crossed = jnp.transpose((both[:features] + both[features:]) + rest)
        for k, rows in enumerate(spans(256, LANES)):
            r = cols.start // LANES + k
            here = slice(cols.start + rows.start, cols.start + rows.stop)
            weight = upright(mass[r : r + 1, :])
            for half in spans(features, LANES):
                target_part[here, half] = 2.0 * (weight * targets[here, half] - crossed[rows, half])


def run(kernel, args, outs, scratch=(), limit=16, held=(), kept=()):
    args = [pltpu.with_memory_space_constraint(a, pltpu.VMEM) if i in held else a for i, a in enumerate(args)]
    shapes = [pltpu.VMEM(*o) if i in kept else jax.ShapeDtypeStruct(*o) for i, o in enumerate(outs)]
    return pl.pallas_call(
        kernel,
        out_shape=shapes,
        in_specs=[pl.BlockSpec(memory_space=pltpu.VMEM)] * len(args),
        out_specs=[pl.BlockSpec(memory_space=pltpu.VMEM)] * len(outs),
        scratch_shapes=[pltpu.VMEM(*s) for s in scratch],
        compiler_params=pltpu.CompilerParams(vmem_limit_bytes=limit << 20),
    )(*args)


def local(embed_docs, embed_targets, start):
    targets = gather(embed_targets, "row")
    docs = gather(embed_docs, "col")
    (n, features), m = docs.shape, targets.shape[0]
    rows, cols = lax.axis_size("row"), lax.axis_size("col")
    ratio = (n * rows) / (m * cols)
    doc_vector, target_vector = ((n // LANES, LANES), f32), ((m // LANES, LANES), f32)
    doc_parts, target_parts = ((cols, *doc_vector[0]), f32), ((rows, *target_vector[0]), f32)
    tile, target_zero, part = run(
        kernel_tile,
        (docs, targets, start.reshape(target_vector[0])),
        [((n, m), f32), target_vector, doc_parts],
        [((n, 3 * features), bf16), ((m, 3 * features), bf16)],
        limit=24, kept=KEPT,
    )

    def step(kernel, part, axis, *extra, over_docs):
        outs = [doc_vector, target_parts] if over_docs else [target_vector, doc_parts]
        return run(kernel, (tile, swap(part, axis), *extra), outs, held=HELD)

    doc_one, part = step(kernel_doc_one, part, "col", over_docs=True)
    target_one, part = step(kernel_target, part, "row", over_docs=False)
    doc_two, part = step(kernel_doc_two, part, "col", over_docs=True)
    target_two, part = step(kernel_target, part, "row", over_docs=False)
    bar_two, part = step(partial(kernel_bar_two, ratio), part, "col", doc_two, over_docs=True)
    bar_one, part = step(kernel_bar_one, part, "row", target_one, over_docs=False)
    top, low, mass, doc_part = run(
        partial(kernel_docs, ratio),
        (tile, swap(part, "col"), doc_one, doc_two, bar_two, target_zero, target_one, target_two, bar_one, targets),
        [((n, m), bf16), ((n, m), bf16), target_vector, ((n, features), f32)],
        [((4, n, LANES), f32), ((m, 2 * features), bf16)],
        limit=32, held=HELD, kept=(0, 1),
    )
    (target_part,) = run(
        kernel_targets, (top, low, mass, docs, targets), [((m, features), f32)], [((2 * features, n), bf16)],
        limit=24, held=(0, 1),
    )
    grad_docs = 2.0 * (embed_docs - scatter(doc_part, "col"))
    grad_targets = scatter(target_part, "row")
    return lax.cond(
        jnp.isnan(jnp.sum(bar_two)),
        lambda: log_domain(docs, targets, start),
        lambda: (grad_docs, grad_targets),
    )


def solution(mesh):
    return jax.shard_map(
        local,
        mesh=mesh,
        in_specs=(P(("row", "col"), None), P(("col", "row"), None), P("col")),
        out_specs=(P(("row", "col"), None), P(("col", "row"), None)),
        check_vma=False,
    )
```

time: 1060 us -> 774 us (0.73)
  waiting for transfers between devices: 328 us -> 80.8 us
  other arithmetic: 97 us -> 60.1 us
  matrix products: 57.4 us -> 34.8 us
  Pallas kernels: 0 us -> 21.1 us
  starting transfers between devices: 14.6 us -> 29.5 us
  between operations: 16.7 us -> 2.54 us
    psum x2 -> x0, waiting for transfers between devices: 284 us -> none  [the longest x1 147 us: log_domain(): lax.psum(doc_part, 'col')]
    all_to_all x2 -> x4, waiting for transfers between devices: 43.8 us -> 80.8 us  [swap(): return lax.all_to_all(blocks, axis, 0, 0)]
    reduce_sum x16 -> x3, other arithmetic: 41.1 us -> 4.3 us  [the longest x2 3.7 us: scatter(): return jnp.sum(swap(pieces, axis), axis=0)]
    dot_general x3 -> x0, matrix products: 22.7 us -> none  [the longest x1 11.7 us: local(): lax.dot_general(adjoint, docs, (((0,), (0,)), ((), ())), precision=high)]
    pallas_call x0 -> x9, Pallas kernels: none -> 21.1 us  [run(): pl.pallas_call(kernel, out_shape=shapes, in_specs=[pl.BlockSpec(memory_sp...]
    all_to_all x2 -> x4, starting transfers between devices: 14.1 us -> 29.5 us  [swap(): return lax.all_to_all(blocks, axis, 0, 0)]
  transfers between devices with their start and end apart: 4 -> 4, of which waited for: 4 -> 4; matrix products, arithmetic and copies ran while one was open for 3% -> 2% of each run, Pallas kernels for 0% -> 1%
where the time goes in v2:
time: 774 us; the launch traced here: 764 us
  blocking collectives  521 us (67%)
  waiting for transfers between devices  80.8 us (10%)
  other arithmetic  60.1 us (8%)
  matrix products  34.8 us (4%)
  starting transfers between devices  29.5 us (4%)
  Pallas kernels  21.1 us (3%)
  local copies, waits for them, and re-layouts  13.5 us (2%)
    all_to_all x9, blocking collectives, swap(): return lax.all_to_all(blocks, axis, 0, 0)  151 us
    all_to_all x4, waiting for transfers between devices, swap(): return lax.all_to_all(blocks, axis, 0, 0)  80.8 us
    pmax x2, blocking collectives, column_log_mass(): largest = lax.pmax(jnp.max(scores, axis=0), 'row')  78.7 us
    pmax x2, blocking collectives, row_log_mass(): largest = lax.pmax(jnp.max(scores, axis=1), 'col')  67.8 us
    psum x2, blocking collectives, row_log_mass(): lax.psum(jnp.sum(jnp.exp(scores - largest[:, None]), axis=1), 'col')  66.6 us
    psum x2, blocking collectives, column_log_mass(): lax.psum(jnp.sum(jnp.exp(scores - largest[None, :]), axis=0), 'row')  55.4 us
    psum x1, blocking collectives, log_domain(): target_bar_one = -lax.psum(jnp.sum(weighted, axis=0), 'row')  34.9 us
    psum x1, blocking collectives, log_domain(): doc_bar_two = 1.0 - ratio * lax.psum(jnp.sum(plan, axis=1), 'col')  33.7 us
  transfers between devices with their start and end apart: 4, of which 4 were waited for; matrix products, arithmetic and copies ran while one was open for 2% of the time, Pallas kernels for 1%

profile of v2, /device:TPU:7, one launch (start us, length us, event | category | flops | bytes accessed | tf_op | source)
XLA Modules:
  0.0 764.0 jit_solution(11497311765745986813)
XLA Ops:
  1.6 38.1 %all_to_all.63 = f32[16,64,256]{2,1,0:T(8,128)S(1)} all-to-all(f32[16,64,256]{2,1,0:T(8,128)S(1)} %broadcast_in_dim.4), channel_id=1, replica_groups=mesh['row'=16,'col'=16] {'col'}, dimensions={0} | all-to-all | bytes 2097152 | tf_op jit(solution)/shard_map/all_to_all | solution.py:75
  40.8 33.9 %all_to_all.64 = f32[16,128,256]{2,1,0:T(8,128)S(1)} all-to-all(f32[16,128,256]{2,1,0:T(8,128)S(1)} %broadcast_in_dim.5), channel_id=1, replica_groups=mesh['row'=16,'col'=16] {'row'}, dimensions={0} | all-to-all | bytes 4194304 | tf_op jit(solution)/shard_map/all_to_all | solution.py:75
  79.3 12.0 %all_to_all.65.parts = f32[16,8,128]{2,1,0:T(8,128)S(1)} all-to-all(f32[16,8,128]{2,1,0:T(8,128)S(1)} %get-tuple-element.50), channel_id=1, replica_groups=mesh['row'=16,'col'=16] {'col'}, dimensions={0} | all-to-all | bytes 131072 | tf_op jit(solution)/shard_map/all_to_all | solution.py:75
  92.0 10.5 %all_to_all.66.parts = f32[16,16,128]{2,1,0:T(8,128)S(1)} all-to-all(f32[16,16,128]{2,1,0:T(8,128)S(1)} %get-tuple-element.51), channel_id=1, replica_groups=mesh['row'=16,'col'=16] {'row'}, dimensions={0} | all-to-all | bytes 262144 | tf_op jit(solution)/shard_map/all_to_all | solution.py:75
  103.2 11.7 %all_to_all.67.parts = f32[16,8,128]{2,1,0:T(8,128)S(1)} all-to-all(f32[16,8,128]{2,1,0:T(8,128)S(1)} %get-tuple-element.52), channel_id=1, replica_groups=mesh['row'=16,'col'=16] {'col'}, dimensions={0} | all-to-all | bytes 131072 | tf_op jit(solution)/shard_map/all_to_all | solution.py:75
  115.6 10.3 %all_to_all.68.parts = f32[16,16,128]{2,1,0:T(8,128)S(1)} all-to-all(f32[16,16,128]{2,1,0:T(8,128)S(1)} %get-tuple-element.53), channel_id=1, replica_groups=mesh['row'=16,'col'=16] {'row'}, dimensions={0} | all-to-all | bytes 262144 | tf_op jit(solution)/shard_map/all_to_all | solution.py:75
  126.6 11.8 %all_to_all.69.parts = f32[16,8,128]{2,1,0:T(8,128)S(1)} all-to-all(f32[16,8,128]{2,1,0:T(8,128)S(1)} %get-tuple-element.54), channel_id=1, replica_groups=mesh['row'=16,'col'=16] {'col'}, dimensions={0} | all-to-all | bytes 131072 | tf_op jit(solution)/shard_map/all_to_all | solution.py:75
  139.0 10.4 %all_to_all.70.parts = f32[16,16,128]{2,1,0:T(8,128)S(1)} all-to-all(f32[16,16,128]{2,1,0:T(8,128)S(1)} %get-tuple-element.57), channel_id=1, replica_groups=mesh['row'=16,'col'=16] {'row'}, dimensions={0} | all-to-all | bytes 262144 | tf_op jit(solution)/shard_map/all_to_all | solution.py:75
  150.0 12.3 %all_to_all.71.parts = f32[16,8,128]{2,1,0:T(8,128)S(1)} all-to-all(f32[16,8,128]{2,1,0:T(8,128)S(1)} %get-tuple-element.59), channel_id=1, replica_groups=mesh['row'=16,'col'=16] {'col'}, dimensions={0} | all-to-all | bytes 131072 | tf_op jit(solution)/shard_map/all_to_all | solution.py:75
  162.4 7.6 %shard_map.57 = (bf16[1024,2048]{1,0:T(8,128)(2,1)S(1)}, bf16[1024,2048]{1,0:T(8,128)(2,1)S(1)}, f32[16,128]{1,0:T(8,128)S(1)}, f32[1024,256]{1,0:T(8,128)}) custom-call(f32[1024,2048]{1,0:T(8,128)S(1)} %get-tuple-element.49.tile, f32[16,8,128]{2,1,0:T(8,128)S(1)} %all_to_all.71.parts, f32[8,128]{1,0:T(8,128)S(1)} %get-tuple-element.60.doc_one, ...), custom_call_target="tpu_custom_call" | custom-call | tf_op jit(solution)/shard_map/pallas_call | solution.py:247
  187.6 17.7 %all-to-all-done.11 = f32[16,64,256]{2,1,0:T(8,128)} async-done(((f32[16,64,256]{2,1,0:T(8,128)}), f32[16,64,256]{2,1,0:T(8,128)}, u32[]{:S(2)}, u32[]{:S(2)}) %all-to-all-start.11) | async-done | bytes 1048608 | tf_op jit(solution)/shard_map/all_to_all | solution.py:75
  205.3 9.5 %all-to-all-start.12 = ((f32[16,128,256]{2,1,0:T(8,128)}), f32[16,128,256]{2,1,0:T(8,128)}, u32[]{:S(2)}, u32[]{:S(2)}) async-start(f32[16,128,256]{2,1,0:T(8,128)} %bitcast.6), calls=%async_computation.12 | async-start | bytes 4194304 | tf_op jit(solution)/shard_map/all_to_all | solution.py:75
  216.7 27.8 %all-to-all-done.12 = f32[16,128,256]{2,1,0:T(8,128)} async-done(((f32[16,128,256]{2,1,0:T(8,128)}), f32[16,128,256]{2,1,0:T(8,128)}, u32[]{:S(2)}, u32[]{:S(2)}) %all-to-all-start.12) | async-done | bytes 2097184 | tf_op jit(solution)/shard_map/all_to_all | solution.py:75
  244.4 516.6 %conditional.1 = (f32[64,256]{1,0:T(8,128)S(1)}, f32[16,128,256]{2,1,0:T(8,128)}, f32[]{:T(128)}, f32[]{:T(128)}) conditional(s32[]{:T(128)} %convert_element_type.3, (f32[16,64,256]{2,1,0:T(8,128)}, f32[64,256]{1,0:T(8,128)S(1)}, f32[16,128,256]{2,1,0:T(8,128)}) %tuple.34, (f32[2048]{0:T(1024)S(1)}, f32[1024,256]{1,0:T(8,128)S(1)}, ...), branch_computations={%region_1.4_spmd, %region_4.0_spmd} | conditional | flops 19469955072 | bytes 186220672 | solution.py:296
  245.2 10.5 %fusion.3 = (f32[1024]{0:T(1024)S(1)}, f32[1024,2048]{1,0:T(8,128)}) fusion(f32[2048]{0:T(1024)S(1)} %get-tuple-element.25, f32[1024,256]{1,0:T(8,128)S(1)} %get-tuple-element.26, f32[2048,256]{1,0:T(8,128)S(1)} %get-tuple-element.27, f32[2048]{0:T(1024)S(1)} %multiply_reduce_fusion, f32[1024]{0:T(1024)S(1)} %multiply_reduce_fusion.1), kind=kOutput, calls=%fused_computation.17 | convolution fusion | flops 6455032832 | bytes 11558912 | tf_op jit(solution)/shard_map/cond/branch_1_fun/dot_general | solution.py:35
  255.6 33.8 %pmax.24 = f32[1024]{0:T(1024)S(1)} all-reduce(f32[1024]{0:T(1024)S(1)} %get-tuple-element.81), channel_id=1, replica_groups=mesh['row'=16,'col'=16] {'col'}, use_global_device_ids=true, to_apply=%region_8.0 | all-reduce | flops 1024 | bytes 8192 | tf_op jit(solution)/shard_map/cond/branch_1_fun/pmax | solution.py:19
  293.9 33.3 %psum.42 = f32[1024]{0:T(1024)S(1)} all-reduce(f32[1024]{0:T(1024)S(1)} %exponential_reduce_fusion.3), channel_id=1, replica_groups=mesh['row'=16,'col'=16] {'col'}, use_global_device_ids=true, to_apply=%region_10.0 | all-reduce | flops 1024 | bytes 8192 | tf_op jit(solution)/shard_map/cond/branch_1_fun/psum | solution.py:20
  331.5 37.1 %pmax.25 = f32[2048]{0:T(1024)S(1)} all-reduce(f32[2048]{0:T(1024)S(1)} %fusion.4), channel_id=1, replica_groups=mesh['row'=16,'col'=16] {'row'}, use_global_device_ids=true, to_apply=%region_12.0 | all-reduce | flops 2048 | bytes 16384 | tf_op jit(solution)/shard_map/cond/branch_1_fun/pmax | solution.py:25
  373.1 27.8 %psum.43 = f32[2048]{0:T(1024)S(1)} all-reduce(f32[2048]{0:T(1024)S(1)} %exponential_reduce_fusion.2), channel_id=1, replica_groups=mesh['row'=16,'col'=16] {'row'}, use_global_device_ids=true, to_apply=%region_14.0 | all-reduce | flops 2048 | bytes 16384 | tf_op jit(solution)/shard_map/cond/branch_1_fun/psum | solution.py:26
  405.2 34.0 %pmax.26 = f32[1024]{0:T(1024)S(1)} all-reduce(f32[1024]{0:T(1024)S(1)} %fusion.5), channel_id=1, replica_groups=mesh['row'=16,'col'=16] {'col'}, use_global_device_ids=true, to_apply=%region_16.0 | all-reduce | flops 1024 | bytes 8192 | tf_op jit(solution)/shard_map/cond/branch_1_fun/pmax | solution.py:19
  443.7 33.3 %psum.44 = f32[1024]{0:T(1024)S(1)} all-reduce(f32[1024]{0:T(1024)S(1)} %exponential_reduce_fusion.1), channel_id=1, replica_groups=mesh['row'=16,'col'=16] {'col'}, use_global_device_ids=true, to_apply=%region_18.0 | all-reduce | flops 1024 | bytes 8192 | tf_op jit(solution)/shard_map/cond/branch_1_fun/psum | solution.py:20
  481.3 41.6 %pmax.27 = f32[2048]{0:T(1024)S(1)} all-reduce(f32[2048]{0:T(1024)S(1)} %fusion.6), channel_id=1, replica_groups=mesh['row'=16,'col'=16] {'row'}, use_global_device_ids=true, to_apply=%region_20.0 | all-reduce | flops 2048 | bytes 16384 | tf_op jit(solution)/shard_map/cond/branch_1_fun/pmax | solution.py:25
  527.4 27.7 %psum.45 = f32[2048]{0:T(1024)S(1)} all-reduce(f32[2048]{0:T(1024)S(1)} %exponential_reduce_fusion), channel_id=1, replica_groups=mesh['row'=16,'col'=16] {'row'}, use_global_device_ids=true, to_apply=%region_22.0 | all-reduce | flops 2048 | bytes 16384 | tf_op jit(solution)/shard_map/cond/branch_1_fun/psum | solution.py:26
  559.6 33.7 %psum.46 = f32[1024]{0:T(1024)S(1)} all-reduce(f32[1024]{0:T(1024)S(1)} %fusion), channel_id=1, replica_groups=mesh['row'=16,'col'=16] {'col'}, use_global_device_ids=true, to_apply=%region_24.0 | all-reduce | flops 1024 | bytes 8192 | tf_op jit(solution)/shard_map/cond/branch_1_fun/psum | solution.py:50
  597.8 34.9 %psum.47 = f32[2048]{0:T(1024)S(1)} all-reduce(f32[2048]{0:T(1024)S(1)} %fusion.1), channel_id=1, replica_groups=mesh['row'=16,'col'=16] {'row'}, use_global_device_ids=true, to_apply=%region_26.0 | all-reduce | flops 2048 | bytes 16384 | tf_op jit(solution)/shard_map/cond/branch_1_fun/psum | solution.py:54
  637.4 32.9 %psum.48 = f32[1024]{0:T(1024)S(1)} all-reduce(f32[1024]{0:T(1024)S(1)} %fusion.2), channel_id=1, replica_groups=mesh['row'=16,'col'=16] {'col'}, use_global_device_ids=true, to_apply=%region_28.0 | all-reduce | flops 1024 | bytes 8192 | tf_op jit(solution)/shard_map/cond/branch_1_fun/psum | solution.py:58
  670.3 10.7 %fusion.9 = (f32[2048]{0:T(1024)S(1)}, f32[1024]{0:T(1024)S(1)}, f32[1024,2048]{1,0:T(8,128)S(1)}) fusion(f32[1024]{0:T(1024)S(1)} %get-tuple-element.80, f32[1024,2048]{1,0:T(8,128)} %get-tuple-element.82, f32[2048]{0:T(1024)S(1)} %get-tuple-element.25, f32[1024]{0:T(1024)S(1)} %neg.5, f32[2048]{0:T(1024)S(1)} %get-tuple-element.78, ...), kind=kLoop, calls=%fused_computation.35 | loop fusion | flops 44037120 | bytes 16855040 | tf_op jit(solution)/shard_map/cond/branch_1_fun/reduce_sum | solution.py:66
  684.2 7.7 %fusion.8 = f32[1024,256]{1,0:T(8,128)} fusion(f32[1024,2048]{1,0:T(8,128)S(1)} %get-tuple-element.74, f32[2048,256]{1,0:T(8,128)S(1)} %get-tuple-element.27, f32[1024,256]{1,0:T(8,128)S(1)} %get-tuple-element.26, f32[1024]{0:T(1024)S(1)} %get-tuple-element.73), kind=kOutput, calls=%fused_computation.25 | convolution fusion | flops 6443237376 | bytes 12587008 | tf_op jit(solution)/shard_map/cond/branch_1_fun/dot_general | solution.py:63
  696.5 16.6 %fusion.7 = f32[2048,256]{1,0:T(8,128)} fusion(f32[1024,2048]{1,0:T(8,128)} %copy-done.4, f32[1024,256]{1,0:T(8,128)S(1)} %get-tuple-element.26, f32[2048,256]{1,0:T(8,128)S(1)} %get-tuple-element.27, f32[2048]{0:T(1024)S(1)} %get-tuple-element.72), kind=kOutput, calls=%fused_computation.22 | convolution fusion | flops 6444023808 | bytes 13639680 | tf_op jit(solution)/shard_map/cond/branch_1_fun/dot_general | solution.py:65
  713.1 8.8 %all-to-all-done = f32[16,64,256]{2,1,0:T(8,128)} async-done(((f32[16,64,256]{2,1,0:T(8,128)}), f32[16,64,256]{2,1,0:T(8,128)}, u32[]{:S(2)}, u32[]{:S(2)}) %all-to-all-start) | async-done | bytes 1048608 | tf_op jit(solution)/shard_map/cond/branch_1_fun/all_to_all | solution.py:75
  721.9 11.1 %all-to-all-start.1 = ((f32[16,128,256]{2,1,0:T(8,128)}), f32[16,128,256]{2,1,0:T(8,128)}, u32[]{:S(2)}, u32[]{:S(2)}) async-start(f32[16,128,256]{2,1,0:T(8,128)} %bitcast.20), calls=%async_computation.1 | async-start | bytes 4194304 | tf_op jit(solution)/shard_map/cond/branch_1_fun/all_to_all | solution.py:75
  734.3 26.5 %all-to-all-done.1 = f32[16,128,256]{2,1,0:T(8,128)} async-done(((f32[16,128,256]{2,1,0:T(8,128)}), f32[16,128,256]{2,1,0:T(8,128)}, u32[]{:S(2)}, u32[]{:S(2)}) %all-to-all-start.1) | async-done | bytes 2097184 | tf_op jit(solution)/shard_map/cond/branch_1_fun/all_to_all | solution.py:75
  (50 shorter events, 85.4 us)
Async XLA Ops:
  0.6 74.1 %copy-start.6 = (f32[2048]{0:T(1024)S(1)}, f32[2048]{0:T(1024)}, u32[]{:S(2)}) copy-start(f32[2048]{0:T(1024)} %param.7) | copy-start | bytes 24580
  170.0 1.9 copy-start
  171.9 2.0 copy-start.2
  173.9 31.4 %all-to-all-start.11 = ((f32[16,64,256]{2,1,0:T(8,128)}), f32[16,64,256]{2,1,0:T(8,128)}, u32[]{:S(2)}, u32[]{:S(2)}) async-start(f32[16,64,256]{2,1,0:T(8,128)} %bitcast.5), calls=%async_computation.11 | async-start | bytes 2097152 | tf_op jit(solution)/shard_map/all_to_all | solution.py:75
  178.3 2.2 copy-start.1
  180.4 2.2 copy-start.3
  182.6 61.8 %copy-start.5 = (f32[64,256]{1,0:T(8,128)S(1)}, f32[64,256]{1,0:T(8,128)}, u32[]{:S(2)}) copy-start(f32[64,256]{1,0:T(8,128)} %param.5) | copy-start | bytes 196612
  205.3 39.1 %all-to-all-start.12 = ((f32[16,128,256]{2,1,0:T(8,128)}), f32[16,128,256]{2,1,0:T(8,128)}, u32[]{:S(2)}, u32[]{:S(2)}) async-start(f32[16,128,256]{2,1,0:T(8,128)} %bitcast.6), calls=%async_computation.12 | async-start | bytes 4194304 | tf_op jit(solution)/shard_map/all_to_all | solution.py:75
  681.0 3.2 copy-start.4
  691.9 30.0 %all-to-all-start = ((f32[16,64,256]{2,1,0:T(8,128)}), f32[16,64,256]{2,1,0:T(8,128)}, u32[]{:S(2)}, u32[]{:S(2)}) async-start(f32[16,64,256]{2,1,0:T(8,128)} %bitcast.21), calls=%async_computation | async-start | bytes 2097152 | tf_op jit(solution)/shard_map/cond/branch_1_fun/all_to_all | solution.py:75
  721.9 38.9 %all-to-all-start.1 = ((f32[16,128,256]{2,1,0:T(8,128)}), f32[16,128,256]{2,1,0:T(8,128)}, u32[]{:S(2)}, u32[]{:S(2)}) async-start(f32[16,128,256]{2,1,0:T(8,128)} %bitcast.20), calls=%async_computation.1 | async-start | bytes 4194304 | tf_op jit(solution)/shard_map/cond/branch_1_fun/all_to_all | solution.py:75
  761.0 2.4 copy-start.7

commit v3 on v2

--- a/solution.py
+++ b/solution.py
@@ -13,29 +13,32 @@
 LOW, HIGH = 1e-25, 1e25
 FIRST_LOW = 1e-9
 KEPT, HELD = (0,), (0,)
+ROW, COL = ("z_lo", "x", "core"), ("y", "z_hi")
+SIZES = {"z_lo": 2, "x": 4, "core": 2, "y": 4, "z_hi": 4}
 
 
 def row_log_mass(scores):
-    largest = lax.pmax(jnp.max(scores, axis=1), "col")
-    mass_all = lax.psum(jnp.sum(jnp.exp(scores - largest[:, None]), axis=1), "col")
+    largest = lax.pmax(jnp.max(scores, axis=1), COL)
+    mass_all = lax.psum(jnp.sum(jnp.exp(scores - largest[:, None]), axis=1), COL)
     return largest + jnp.log(mass_all)
 
 
 def column_log_mass(scores):
-    largest = lax.pmax(jnp.max(scores, axis=0), "row")
-    mass_all = lax.psum(jnp.sum(jnp.exp(scores - largest[None, :]), axis=0), "row")
+    largest = lax.pmax(jnp.max(scores, axis=0), ROW)
+    mass_all = lax.psum(jnp.sum(jnp.exp(scores - largest[None, :]), axis=0), ROW)
     return largest + jnp.log(mass_all)
 
 
-def log_domain(doc_block, target_block, start):
+def log_domain(embed_docs, embed_targets, start):
+    doc_block, target_block = gather(embed_docs, COL), gather(embed_targets, ROW)
     highest = lax.Precision.HIGHEST
     distance_tile = (
         jnp.sum(doc_block * doc_block, axis=1)[:, None]
         + jnp.sum(target_block * target_block, axis=1)[None, :]
         - 2.0 * jnp.dot(doc_block, target_block.T, precision=highest)
     )
-    texts = distance_tile.shape[0] * lax.axis_size("row")
-    goals = distance_tile.shape[1] * lax.axis_size("col")
+    texts = distance_tile.shape[0] * lax.axis_size(ROW)
+    goals = distance_tile.shape[1] * lax.axis_size(COL)
     ratio = texts / goals
     t = smoothing_epsilon
     row_log_one = row_log_mass((start[None, :] - distance_tile) / t)
@@ -47,15 +50,15 @@
     col_log_two = column_log_mass((doc_two[:, None] - distance_tile) / t)
     plan = jnp.exp((doc_two[:, None] - distance_tile) / t - col_log_two[None, :])
     adjoint = ratio * plan
-    doc_bar_two = 1.0 - ratio * lax.psum(jnp.sum(plan, axis=1), "col")
+    doc_bar_two = 1.0 - ratio * lax.psum(jnp.sum(plan, axis=1), COL)
     plan = jnp.exp((target_one[None, :] - distance_tile) / t - row_log_two[:, None])
     weighted = doc_bar_two[:, None] * plan
     adjoint = adjoint + weighted
-    target_bar_one = -lax.psum(jnp.sum(weighted, axis=0), "row")
+    target_bar_one = -lax.psum(jnp.sum(weighted, axis=0), ROW)
     plan = jnp.exp((doc_one[:, None] - distance_tile) / t - col_log_one[None, :])
     weighted = target_bar_one[None, :] * plan
     adjoint = adjoint + weighted
-    doc_bar_one = -lax.psum(jnp.sum(weighted, axis=1), "col")
+    doc_bar_one = -lax.psum(jnp.sum(weighted, axis=1), COL)
     plan = jnp.exp((start[None, :] - distance_tile) / t - row_log_one[:, None])
     adjoint = adjoint + doc_bar_one[:, None] * plan
     doc_part = 2.0 * (
@@ -64,7 +67,7 @@
     )
     crossed = lax.dot_general(adjoint, doc_block, (((0,), (0,)), ((), ())), precision=highest)
     target_part = 2.0 * (jnp.sum(adjoint, axis=0)[:, None] * target_block - crossed)
-    return scatter(doc_part, "col"), scatter(target_part, "row")
+    return scatter(doc_part, COL), scatter(target_part, ROW)
 
 
 LANES = 128
@@ -134,8 +137,23 @@
     ref[...] = jnp.broadcast_to(values[None], ref.shape)
 
 
-def kernel_tile(docs, targets, start, tile, weight_out, part, doc_wide, target_wide):
+def turned(place, by, size):
+    return lax.rem(place + by, size)
+
+
+def kernel_tile(place, start, near, *refs):
+    far, (mine, other), (docs, targets, tile, weight_out, part, doc_wide, target_wide) = refs[:-9], refs[-9:-7], refs[-7:]
     features = docs.shape[1]
+    sizes = SIZES["y"], SIZES["z_hi"]
+    share = docs.shape[0] // (sizes[0] * sizes[1])
+    for k, source in enumerate((near, *far)):
+        y = turned(place[0], sizes[0] - k, sizes[0])
+        for j in range(sizes[1]):
+            at = (y * sizes[1] + turned(place[1], sizes[1] - j, sizes[1])) * share
+            docs[pl.ds(pl.multiple_of(at, share), share), :] = source[j * share : (j + 1) * share, :]
+    half = mine.shape[0]
+    targets[pl.ds(pl.multiple_of(place[2] * half, half), half), :] = mine[...]
+    targets[pl.ds(pl.multiple_of((1 - place[2]) * half, half), half), :] = other[...]
     for source, wide, order in ((docs, doc_wide, (0, 0, 1)), (targets, target_wide, (0, 1, 0))):
         for rows in spans(source.shape[0], 256):
             pair = halves(source[rows, :])
@@ -155,7 +173,9 @@
     for rows in spans(targets.shape[0], LANES):
         squares = targets[rows, :] * targets[rows, :]
         norms.append(lane_total(sum(squares[:, cols] for cols in spans(features, LANES))))
-    weight = jnp.exp((start[...] - jnp.concatenate(norms, axis=0)) / smoothing_epsilon)
+    count = start.shape[0]
+    begin = jnp.concatenate([start[i : i + 1, :] for c in range(2) for i in range(c, count, 2)], axis=0)
+    weight = jnp.exp((begin - jnp.concatenate(norms, axis=0)) / smoothing_epsilon)
     weight = jnp.where(fits, weight, jnp.nan)
     weight_out[...] = weight
     spread(part, row_sums(tile, weight))
@@ -193,8 +213,9 @@
     spread(part, row_sums(tile, weight))
 
 
-def kernel_docs(ratio, tile, parts, doc_one, doc_two, bar_two, target_zero, target_one, target_two, bar_one,
-                targets, top, low, mass, doc_part, factors, wide):
+def kernel_docs(ratio, place, tile, parts, doc_one, doc_two, bar_two, target_zero, target_one, target_two, bar_one,
+                targets, top, low, mass, *refs):
+    pieces, (factors, wide) = refs[:-2], refs[-2:]
     features = targets.shape[1]
     for rows in spans(targets.shape[0], 256):
         pair = halves(targets[rows, :])
@@ -208,103 +229,157 @@
     for r, rows in enumerate(spans(tile.shape[0], LANES)):
         for k, values in enumerate(by_row):
             factors[k, rows, :] = upright(values[r : r + 1, :])
-    for block in spans(tile.shape[0], 256):
-        for rows in spans(256, 32):
-            rows = slice(block.start + rows.start, block.start + rows.stop)
-            a = [factors[k, rows, :] for k in range(4)]
+    size = pieces[0].shape[0]
+    for k, piece in enumerate(pieces):
+        first = pl.multiple_of(turned(place[0], k, len(pieces)) * size, size)
+        for rows in spans(size, 32):
+            rows = pl.ds(first + rows.start, 32)
+            a = [factors[i, rows, :] for i in range(4)]
             for c, cols in enumerate(columns):
                 b = [v[c : c + 1, :] for v in by_column]
                 adjoint = tile[rows, cols] * ((a[0] * b[0] + a[1] * b[1]) + (a[2] * b[2] + a[3] * b[3]))
                 term = jnp.sum(adjoint.reshape(-1, 8, LANES), axis=0)
                 acc[c] = term if acc[c] is None else acc[c] + term
                 top[rows, cols], low[rows, cols] = halves(adjoint)
+        block = pl.ds(first, size)
         both = jnp.dot(top[block, :], wide[...], preferred_element_type=f32)
         rest = jnp.dot(low[block, :], wide[:, :features], preferred_element_type=f32)
-        doc_part[block, :] = (both[:, :features] + both[:, features:]) + rest
+        piece[...] = (both[:, :features] + both[:, features:]) + rest
     mass[...] = jnp.concatenate([jnp.sum(a, axis=0, keepdims=True) for a in acc], axis=0)
 
 
-def kernel_targets(top, low, mass, docs, targets, target_part, flat):
+def kernel_targets(place, top, low, mass, docs, targets, other, mine, flat):
     features = docs.shape[1]
     for rows in spans(docs.shape[0], 256):
         pair = halves(jnp.transpose(docs[rows, :]))
         flat[:features, rows], flat[features:, rows] = pair
-    for cols in spans(targets.shape[0], 256):
-        both = jnp.dot(flat[...], top[:, cols], preferred_element_type=f32)
-        rest = jnp.dot(flat[:features, :], low[:, cols], preferred_element_type=f32)
-        crossed = jnp.transpose((both[:features] + both[features:]) + rest)
-        for k, rows in enumerate(spans(256, LANES)):
-            r = cols.start // LANES + k
-            here = slice(cols.start + rows.start, cols.start + rows.stop)
-            weight = upright(mass[r : r + 1, :])
-            for half in spans(features, LANES):
-                target_part[here, half] = 2.0 * (weight * targets[here, half] - crossed[rows, half])
-
-
-def run(kernel, args, outs, scratch=(), limit=16, held=(), kept=()):
+    half = mine.shape[0]
+    for core, out in ((1 - place[2], other), (place[2], mine)):
+        for inner in spans(half, 256):
+            first = pl.multiple_of(core * half + inner.start, 256)
+            cols = pl.ds(first, 256)
+            both = jnp.dot(flat[...], top[:, cols], preferred_element_type=f32)
+            rest = jnp.dot(flat[:features, :], low[:, cols], preferred_element_type=f32)
+            crossed = jnp.transpose((both[:features] + both[features:]) + rest)
+            for rows in spans(256, LANES):
+                at = core * (half // LANES) + (inner.start + rows.start) // LANES
+                weight = upright(mass[pl.ds(at, 1), :])
+                here = pl.ds(first + rows.start, LANES)
+                for part in spans(features, LANES):
+                    out[inner.start + rows.start : inner.start + rows.stop, part] = 2.0 * (
+                        weight * targets[here, part] - crossed[rows, part]
+                    )
+
+
+def kernel_pieces(place, *refs):
+    parts, pieces = refs[: SIZES["y"]], refs[SIZES["y"] :]
+    size = pieces[0].shape[0]
+    for k, piece in enumerate(pieces):
+        rows = pl.ds(pl.multiple_of(turned(place[1], k, len(pieces)) * size, size), size)
+        piece[...] = sum(part[rows, :] for part in parts)
+
+
+def kernel_pair(one, two, out):
+    out[...] = one[...] + two[...]
+
+
+def kernel_grads(own, *refs):
+    parts, (blocks, grad_docs, grad_targets) = refs[:-3], refs[-3:]
+    grad_docs[...] = 2.0 * (own[...] - sum(part[...] for part in parts))
+    grad_targets[...] = jnp.sum(blocks[...], axis=0)
+
+
+def run(kernel, args, outs, scratch=(), limit=16, held=(), kept=(), flops=0, place=None):
     args = [pltpu.with_memory_space_constraint(a, pltpu.VMEM) if i in held else a for i, a in enumerate(args)]
     shapes = [pltpu.VMEM(*o) if i in kept else jax.ShapeDtypeStruct(*o) for i, o in enumerate(outs)]
+    whole = pl.BlockSpec(memory_space=pltpu.VMEM)
+    specs = [whole] * len(args)
+    if place is not None:
+        args, specs = [place, *args], [pl.BlockSpec(memory_space=pltpu.SMEM), *specs]
+    size = sum(math.prod(a.shape) * a.dtype.itemsize for a in args)
     return pl.pallas_call(
         kernel,
         out_shape=shapes,
-        in_specs=[pl.BlockSpec(memory_space=pltpu.VMEM)] * len(args),
-        out_specs=[pl.BlockSpec(memory_space=pltpu.VMEM)] * len(outs),
+        in_specs=specs,
+        out_specs=[whole] * len(outs),
         scratch_shapes=[pltpu.VMEM(*s) for s in scratch],
         compiler_params=pltpu.CompilerParams(vmem_limit_bytes=limit << 20),
+        cost_estimate=pl.CostEstimate(flops=flops, bytes_accessed=size, transcendentals=0),
     )(*args)
 
 
+def ring(blocks, axis):
+    size = SIZES[axis]
+    return [
+        block if k == 0 else lax.ppermute(block, axis, [(i, (i + k) % size) for i in range(size)])
+        for k, block in enumerate(blocks)
+    ]
+
+
 def local(embed_docs, embed_targets, start):
-    targets = gather(embed_targets, "row")
-    docs = gather(embed_docs, "col")
-    (n, features), m = docs.shape, targets.shape[0]
-    rows, cols = lax.axis_size("row"), lax.axis_size("col")
+    rows, cols = lax.axis_size(ROW), lax.axis_size(COL)
+    place = jnp.stack([lax.axis_index(a) for a in ("y", "z_hi", "core")]).astype(jnp.int32)
+    mine = gather(embed_targets, ("z_lo", "x"))
+    other = lax.ppermute(mine, "core", [(0, 1), (1, 0)])
+    near = jnp.concatenate(ring([embed_docs] * SIZES["z_hi"], "z_hi"), axis=0)
+    doc_pieces = ring([near] * SIZES["y"], "y")
+    (share, features), (target_share, _) = embed_docs.shape, embed_targets.shape
+    n, m = share * cols, target_share * rows
     ratio = (n * rows) / (m * cols)
+    product = 6 * n * m * features
     doc_vector, target_vector = ((n // LANES, LANES), f32), ((m // LANES, LANES), f32)
     doc_parts, target_parts = ((cols, *doc_vector[0]), f32), ((rows, *target_vector[0]), f32)
-    tile, target_zero, part = run(
+    docs, targets, tile, target_zero, part = run(
         kernel_tile,
-        (docs, targets, start.reshape(target_vector[0])),
-        [((n, m), f32), target_vector, doc_parts],
+        (start.reshape(target_vector[0]), *doc_pieces, mine, other),
+        [((n, features), f32), ((m, features), f32), ((n, m), f32), target_vector, doc_parts],
         [((n, 3 * features), bf16), ((m, 3 * features), bf16)],
-        limit=24, kept=KEPT,
+        limit=28, kept=(2,), flops=product, place=place,
     )
 
     def step(kernel, part, axis, *extra, over_docs):
         outs = [doc_vector, target_parts] if over_docs else [target_vector, doc_parts]
-        return run(kernel, (tile, swap(part, axis), *extra), outs, held=HELD)
-
-    doc_one, part = step(kernel_doc_one, part, "col", over_docs=True)
-    target_one, part = step(kernel_target, part, "row", over_docs=False)
-    doc_two, part = step(kernel_doc_two, part, "col", over_docs=True)
-    target_two, part = step(kernel_target, part, "row", over_docs=False)
-    bar_two, part = step(partial(kernel_bar_two, ratio), part, "col", doc_two, over_docs=True)
-    bar_one, part = step(kernel_bar_one, part, "row", target_one, over_docs=False)
-    top, low, mass, doc_part = run(
+        return run(kernel, (tile, swap(part, axis), *extra), outs, held=HELD, flops=2 * n * m)
+
+    doc_one, part = step(kernel_doc_one, part, COL, over_docs=True)
+    target_one, part = step(kernel_target, part, ROW, over_docs=False)
+    doc_two, part = step(kernel_doc_two, part, COL, over_docs=True)
+    target_two, part = step(kernel_target, part, ROW, over_docs=False)
+    bar_two, part = step(partial(kernel_bar_two, ratio), part, COL, doc_two, over_docs=True)
+    bar_one, part = step(kernel_bar_one, part, ROW, target_one, over_docs=False)
+    top, low, mass, *doc_pieces = run(
         partial(kernel_docs, ratio),
-        (tile, swap(part, "col"), doc_one, doc_two, bar_two, target_zero, target_one, target_two, bar_one, targets),
-        [((n, m), bf16), ((n, m), bf16), target_vector, ((n, features), f32)],
+        (tile, swap(part, COL), doc_one, doc_two, bar_two, target_zero, target_one, target_two, bar_one, targets),
+        [((n, m), bf16), ((n, m), bf16), target_vector] + [((n // SIZES["y"], features), f32)] * SIZES["y"],
         [((4, n, LANES), f32), ((m, 2 * features), bf16)],
-        limit=32, held=HELD, kept=(0, 1),
-    )
-    (target_part,) = run(
-        kernel_targets, (top, low, mass, docs, targets), [((m, features), f32)], [((2 * features, n), bf16)],
-        limit=24, held=(0, 1),
-    )
-    grad_docs = 2.0 * (embed_docs - scatter(doc_part, "col"))
-    grad_targets = scatter(target_part, "row")
+        limit=32, held=HELD, kept=(0, 1), flops=product, place=place,
+    )
+    doc_pieces = ring(doc_pieces, "y")
+    other, mine = run(
+        kernel_targets, (top, low, mass, docs, targets), [((m // 2, features), f32)] * 2, [((2 * features, n), bf16)],
+        limit=24, held=(0, 1), flops=product, place=place,
+    )
+    (mine,) = run(kernel_pair, (mine, lax.ppermute(other, "core", [(0, 1), (1, 0)])), [((m // 2, features), f32)])
+    doc_pieces = run(kernel_pieces, doc_pieces, [((share, features), f32)] * SIZES["z_hi"], place=place)
+    doc_pieces = ring(doc_pieces, "z_hi")
+    blocks = swap(mine.reshape(rows // 2, target_share, features), ("z_lo", "x"))
+    grads = run(
+        kernel_grads, (embed_docs, *doc_pieces, blocks), [((share, features), f32), ((target_share, features), f32)]
+    )
     return lax.cond(
         jnp.isnan(jnp.sum(bar_two)),
-        lambda: log_domain(docs, targets, start),
-        lambda: (grad_docs, grad_targets),
+        lambda: log_domain(embed_docs, embed_targets, start),
+        lambda: tuple(grads),
     )
 
 
 def solution(mesh):
+    axes = ROW + COL
+    fine = jax.sharding.Mesh(mesh.devices.reshape([SIZES[a] for a in axes]), axes)
     return jax.shard_map(
         local,
-        mesh=mesh,
-        in_specs=(P(("row", "col"), None), P(("col", "row"), None), P("col")),
-        out_specs=(P(("row", "col"), None), P(("col", "row"), None)),
+        mesh=fine,
+        in_specs=(P(ROW + COL, None), P(COL + ROW, None), P(COL)),
+        out_specs=(P(ROW + COL, None), P(COL + ROW, None)),
         check_vma=False,
     )

time: 774 us -> 800 us (1.034)
  starting transfers between devices: 29.5 us -> 61.8 us
  blocking collectives: 521 us -> 504 us
  waiting for transfers between devices: 80.8 us -> 96.8 us
    ppermute x0 -> x14, waiting for transfers between devices: none -> 30.8 us  [the longest x12 28.5 us: ring(): lax.ppermute(block, axis, [(i, (i + k) % size) for i in range(size)])]
    ppermute x0 -> x14, starting transfers between devices: none -> 25.6 us  [the longest x12 22 us: ring(): lax.ppermute(block, axis, [(i, (i + k) % size) for i in range(size)])]
    all_to_all x9, blocking collectives: 151 us -> 134 us  [swap(): return lax.all_to_all(blocks, axis, 0, 0)]
    all_to_all x4, waiting for transfers between devices: 80.8 us -> 66 us  [swap(): return lax.all_to_all(blocks, axis, 0, 0)]
    pallas_call x9 -> x12, Pallas kernels: 21.1 us -> 24.1 us  [run(): pl.pallas_call(kernel, out_shape=shapes, in_specs=specs, out_specs=[whole...]
  transfers between devices with their start and end apart: 4 -> 18, of which waited for: 4 -> 12; matrix products, arithmetic and copies ran while one was open for 2% -> 3% of each run, Pallas kernels for 1% -> 0%
where the time goes in v3:
time: 800 us; the launch traced here: 791 us
  blocking collectives  504 us (63%)
  waiting for transfers between devices  96.8 us (12%)
  starting transfers between devices  61.8 us (8%)
  other arithmetic  58 us (7%)
  matrix products  34.9 us (4%)
  Pallas kernels  24.1 us (3%)
  local copies, waits for them, and re-layouts  8.11 us (1%)
    all_to_all x9, blocking collectives, swap(): return lax.all_to_all(blocks, axis, 0, 0)  134 us
    pmax x2, blocking collectives, column_log_mass(): largest = lax.pmax(jnp.max(scores, axis=0), ROW)  78.9 us
    pmax x2, blocking collectives, row_log_mass(): largest = lax.pmax(jnp.max(scores, axis=1), COL)  68.2 us
    all_to_all x4, waiting for transfers between devices, swap(): return lax.all_to_all(blocks, axis, 0, 0)  66 us
    psum x2, blocking collectives, row_log_mass(): lax.psum(jnp.sum(jnp.exp(scores - largest[:, None]), axis=1), COL)  66 us
    psum x2, blocking collectives, column_log_mass(): lax.psum(jnp.sum(jnp.exp(scores - largest[None, :]), axis=0), ROW)  55.4 us
    all_to_all x4, starting transfers between devices, swap(): return lax.all_to_all(blocks, axis, 0, 0)  36.2 us
    psum x1, blocking collectives, log_domain(): target_bar_one = -lax.psum(jnp.sum(weighted, axis=0), ROW)  34.9 us
  transfers between devices with their start and end apart: 18, of which 12 were waited for; matrix products, arithmetic and copies ran while one was open for 3% of the time, Pallas kernels for 0%

profile of v3, /device:TPU:7, one launch (start us, length us, event | category | flops | bytes accessed | tf_op | source)
XLA Modules:
  0.0 790.6 jit_solution(4320393563146318442)
XLA Ops:
  1.6 17.9 %all_to_all.62 = f32[8,128,256]{2,1,0:T(8,128)S(1)} all-to-all(f32[8,128,256]{2,1,0:T(8,128)S(1)} %broadcast_in_dim.6), channel_id=1, replica_groups=mesh['z_lo'=2,'x'=4,'core'=2,'y'=4,'z_hi'=4] {'z_lo','x'}, dimensions={0} | all-to-all | bytes 2097152 | tf_op jit(solution)/shard_map/all_to_all | solution.py:78
  45.1 6.7 collective-permute-done.4.refs_1_
  57.3 15.1 %all_to_all.63.parts = f32[16,8,128]{2,1,0:T(8,128)S(1)} all-to-all(f32[16,8,128]{2,1,0:T(8,128)S(1)} %get-tuple-element.46), channel_id=1, replica_groups=mesh['z_lo'=2,'x'=4,'core'=2,'y'=4,'z_hi'=4] {'y','z_hi'}, dimensions={0} | all-to-all | bytes 131072 | tf_op jit(solution)/shard_map/all_to_all | solution.py:78
  73.1 13.0 %all_to_all.64.parts = f32[16,16,128]{2,1,0:T(8,128)S(1)} all-to-all(f32[16,16,128]{2,1,0:T(8,128)S(1)} %get-tuple-element.47), channel_id=1, replica_groups=mesh['z_lo'=2,'x'=4,'core'=2,'y'=4,'z_hi'=4] {'z_lo','x','core'}, dimensions={0} | all-to-all | bytes 262144 | tf_op jit(solution)/shard_map/all_to_all | solution.py:78
  86.8 11.7 %all_to_all.65.parts = f32[16,8,128]{2,1,0:T(8,128)S(1)} all-to-all(f32[16,8,128]{2,1,0:T(8,128)S(1)} %get-tuple-element.48), channel_id=1, replica_groups=mesh['z_lo'=2,'x'=4,'core'=2,'y'=4,'z_hi'=4] {'y','z_hi'}, dimensions={0} | all-to-all | bytes 131072 | tf_op jit(solution)/shard_map/all_to_all | solution.py:78
  99.1 10.9 %all_to_all.66.parts = f32[16,16,128]{2,1,0:T(8,128)S(1)} all-to-all(f32[16,16,128]{2,1,0:T(8,128)S(1)} %get-tuple-element.49), channel_id=1, replica_groups=mesh['z_lo'=2,'x'=4,'core'=2,'y'=4,'z_hi'=4] {'z_lo','x','core'}, dimensions={0} | all-to-all | bytes 262144 | tf_op jit(solution)/shard_map/all_to_all | solution.py:78
  110.7 11.7 %all_to_all.67.parts = f32[16,8,128]{2,1,0:T(8,128)S(1)} all-to-all(f32[16,8,128]{2,1,0:T(8,128)S(1)} %get-tuple-element.50), channel_id=1, replica_groups=mesh['z_lo'=2,'x'=4,'core'=2,'y'=4,'z_hi'=4] {'y','z_hi'}, dimensions={0} | all-to-all | bytes 131072 | tf_op jit(solution)/shard_map/all_to_all | solution.py:78
  123.1 10.4 %all_to_all.68.parts = f32[16,16,128]{2,1,0:T(8,128)S(1)} all-to-all(f32[16,16,128]{2,1,0:T(8,128)S(1)} %get-tuple-element.53), channel_id=1, replica_groups=mesh['z_lo'=2,'x'=4,'core'=2,'y'=4,'z_hi'=4] {'z_lo','x','core'}, dimensions={0} | all-to-all | bytes 262144 | tf_op jit(solution)/shard_map/all_to_all | solution.py:78
  134.1 11.8 %all_to_all.69.parts = f32[16,8,128]{2,1,0:T(8,128)S(1)} all-to-all(f32[16,8,128]{2,1,0:T(8,128)S(1)} %get-tuple-element.55), channel_id=1, replica_groups=mesh['z_lo'=2,'x'=4,'core'=2,'y'=4,'z_hi'=4] {'y','z_hi'}, dimensions={0} | all-to-all | bytes 131072 | tf_op jit(solution)/shard_map/all_to_all | solution.py:78
  145.9 8.7 %shard_map.61 = (bf16[1024,2048]{1,0:T(8,128)(2,1)S(1)}, bf16[1024,2048]{1,0:T(8,128)(2,1)S(1)}, f32[16,128]{1,0:T(8,128)S(1)}, f32[256,256]{1,0:T(8,128)S(1)}, ...) custom-call(s32[3]{0:T(128)S(1)} %pad_add_fusion.place, ...), custom_call_target="tpu_custom_call" | custom-call | flops 3221225472 | bytes 10596364 | tf_op jit(solution)/shard_map/pallas_call | solution.py:300
  193.1 596.0 %conditional.1 = ((f32[64,256]{1,0:T(8,128)S(1)}, f32[128,256]{1,0:T(8,128)S(1)})) conditional(s32[]{:T(128)} %convert_element_type.3, (f32[64,256]{1,0:T(8,128)S(1)}, f32[128,256]{1,0:T(8,128)S(1)}) %shard_map.65, (f32[2048]{0:T(1024)S(1)}, f32[64,256]{1,0:T(8,128)S(1)}, f32[128,256]{1,0:T(8,128)S(1)}) %tuple.30), branch_computations={%region_1.0_spmd, %region_2.0_spmd} | conditional | flops 19470446592 | bytes 200188064 | solution.py:369
  193.2 31.3 %all_to_all.61 = f32[16,64,256]{2,1,0:T(8,128)S(1)} all-to-all(f32[16,64,256]{2,1,0:T(8,128)S(1)} %broadcast_in_dim.0), channel_id=1, replica_groups=mesh['z_lo'=2,'x'=4,'core'=2,'y'=4,'z_hi'=4] {'y','z_hi'}, dimensions={0} | all-to-all | bytes 2097152 | tf_op jit(solution)/shard_map/cond/branch_1_fun/all_to_all | solution.py:78
  226.1 13.3 %all-to-all-start.1 = ((f32[16,128,256]{2,1,0:T(8,128)}), f32[16,128,256]{2,1,0:T(8,128)S(1)}, u32[]{:S(2)}, u32[]{:S(2)}) async-start(f32[16,128,256]{2,1,0:T(8,128)} %broadcast_in_dim.1), calls=%async_computation.1 | async-start | bytes 4194304 | tf_op jit(solution)/shard_map/cond/branch_1_fun/all_to_all | solution.py:78
  239.7 29.2 %all-to-all-done.1 = f32[16,128,256]{2,1,0:T(8,128)S(1)} async-done(((f32[16,128,256]{2,1,0:T(8,128)}), f32[16,128,256]{2,1,0:T(8,128)S(1)}, u32[]{:S(2)}, u32[]{:S(2)}) %all-to-all-start.1) | async-done | bytes 2097184 | tf_op jit(solution)/shard_map/cond/branch_1_fun/all_to_all | solution.py:78
  269.3 10.5 %fusion.3 = (f32[1024]{0:T(1024)S(1)}, f32[1024,2048]{1,0:T(8,128)}) fusion(f32[2048]{0:T(1024)S(1)} %get-tuple-element.10, f32[1024,256]{1,0:T(8,128)S(1)} %bitcast.23, f32[2048,256]{1,0:T(8,128)S(1)} %bitcast.19, f32[2048]{0:T(1024)S(1)} %bitcast.28, f32[1024]{0:T(1024)S(1)} %add.22), kind=kOutput, calls=%fused_computation.16 | convolution fusion | flops 6455032832 | bytes 11558912 | tf_op jit(solution)/shard_map/cond/branch_1_fun/dot_general | solution.py:38
  279.8 34.0 %pmax.24 = f32[1024]{0:T(1024)S(1)} all-reduce(f32[1024]{0:T(1024)S(1)} %get-tuple-element.88), channel_id=1, replica_groups=mesh['z_lo'=2,'x'=4,'core'=2,'y'=4,'z_hi'=4] {'y','z_hi'}, use_global_device_ids=true, to_apply=%region_6.0 | all-reduce | flops 1024 | bytes 8192 | tf_op jit(solution)/shard_map/cond/branch_1_fun/pmax | solution.py:21
  318.3 33.3 %psum.42 = f32[1024]{0:T(1024)S(1)} all-reduce(f32[1024]{0:T(1024)S(1)} %exponential_reduce_fusion.3), channel_id=1, replica_groups=mesh['z_lo'=2,'x'=4,'core'=2,'y'=4,'z_hi'=4] {'y','z_hi'}, use_global_device_ids=true, to_apply=%region_8.0 | all-reduce | flops 1024 | bytes 8192 | tf_op jit(solution)/shard_map/cond/branch_1_fun/psum | solution.py:22
  355.9 37.1 %pmax.25 = f32[2048]{0:T(1024)S(1)} all-reduce(f32[2048]{0:T(1024)S(1)} %fusion.4), channel_id=1, replica_groups=mesh['z_lo'=2,'x'=4,'core'=2,'y'=4,'z_hi'=4] {'z_lo','x','core'}, use_global_device_ids=true, to_apply=%region_10.0 | all-reduce | flops 2048 | bytes 16384 | tf_op jit(solution)/shard_map/cond/branch_1_fun/pmax | solution.py:27
  397.5 27.8 %psum.43 = f32[2048]{0:T(1024)S(1)} all-reduce(f32[2048]{0:T(1024)S(1)} %exponential_reduce_fusion.2), channel_id=1, replica_groups=mesh['z_lo'=2,'x'=4,'core'=2,'y'=4,'z_hi'=4] {'z_lo','x','core'}, use_global_device_ids=true, to_apply=%region_12.0 | all-reduce | flops 2048 | bytes 16384 | tf_op jit(solution)/shard_map/cond/branch_1_fun/psum | solution.py:28
  429.6 34.3 %pmax.26 = f32[1024]{0:T(1024)S(1)} all-reduce(f32[1024]{0:T(1024)S(1)} %fusion.5), channel_id=1, replica_groups=mesh['z_lo'=2,'x'=4,'core'=2,'y'=4,'z_hi'=4] {'y','z_hi'}, use_global_device_ids=true, to_apply=%region_14.0 | all-reduce | flops 1024 | bytes 8192 | tf_op jit(solution)/shard_map/cond/branch_1_fun/pmax | solution.py:21
  468.4 32.6 %psum.44 = f32[1024]{0:T(1024)S(1)} all-reduce(f32[1024]{0:T(1024)S(1)} %exponential_reduce_fusion.1), channel_id=1, replica_groups=mesh['z_lo'=2,'x'=4,'core'=2,'y'=4,'z_hi'=4] {'y','z_hi'}, use_global_device_ids=true, to_apply=%region_16.0 | all-reduce | flops 1024 | bytes 8192 | tf_op jit(solution)/shard_map/cond/branch_1_fun/psum | solution.py:22
  505.3 41.8 %pmax.27 = f32[2048]{0:T(1024)S(1)} all-reduce(f32[2048]{0:T(1024)S(1)} %fusion.6), channel_id=1, replica_groups=mesh['z_lo'=2,'x'=4,'core'=2,'y'=4,'z_hi'=4] {'z_lo','x','core'}, use_global_device_ids=true, to_apply=%region_18.0 | all-reduce | flops 2048 | bytes 16384 | tf_op jit(solution)/shard_map/cond/branch_1_fun/pmax | solution.py:27
  551.6 27.7 %psum.45 = f32[2048]{0:T(1024)S(1)} all-reduce(f32[2048]{0:T(1024)S(1)} %exponential_reduce_fusion), channel_id=1, replica_groups=mesh['z_lo'=2,'x'=4,'core'=2,'y'=4,'z_hi'=4] {'z_lo','x','core'}, use_global_device_ids=true, to_apply=%region_20.0 | all-reduce | flops 2048 | bytes 16384 | tf_op jit(solution)/shard_map/cond/branch_1_fun/psum | solution.py:28
  583.8 33.9 %psum.46 = f32[1024]{0:T(1024)S(1)} all-reduce(f32[1024]{0:T(1024)S(1)} %fusion), channel_id=1, replica_groups=mesh['z_lo'=2,'x'=4,'core'=2,'y'=4,'z_hi'=4] {'y','z_hi'}, use_global_device_ids=true, to_apply=%region_22.0 | all-reduce | flops 1024 | bytes 8192 | tf_op jit(solution)/shard_map/cond/branch_1_fun/psum | solution.py:53
  622.3 34.9 %psum.47 = f32[2048]{0:T(1024)S(1)} all-reduce(f32[2048]{0:T(1024)S(1)} %fusion.1), channel_id=1, replica_groups=mesh['z_lo'=2,'x'=4,'core'=2,'y'=4,'z_hi'=4] {'z_lo','x','core'}, use_global_device_ids=true, to_apply=%region_24.0 | all-reduce | flops 2048 | bytes 16384 | tf_op jit(solution)/shard_map/cond/branch_1_fun/psum | solution.py:57
  661.9 33.0 %psum.48 = f32[1024]{0:T(1024)S(1)} all-reduce(f32[1024]{0:T(1024)S(1)} %fusion.2), channel_id=1, replica_groups=mesh['z_lo'=2,'x'=4,'core'=2,'y'=4,'z_hi'=4] {'y','z_hi'}, use_global_device_ids=true, to_apply=%region_26.0 | all-reduce | flops 1024 | bytes 8192 | tf_op jit(solution)/shard_map/cond/branch_1_fun/psum | solution.py:61
  694.9 10.7 %fusion.9 = (f32[2048]{0:T(1024)S(1)}, f32[1024]{0:T(1024)S(1)}, f32[1024,2048]{1,0:T(8,128)S(1)}) fusion(f32[1024]{0:T(1024)S(1)} %get-tuple-element.87, f32[1024,2048]{1,0:T(8,128)} %get-tuple-element.89, f32[2048]{0:T(1024)S(1)} %get-tuple-element.10, f32[1024]{0:T(1024)S(1)} %neg.5, f32[2048]{0:T(1024)S(1)} %get-tuple-element.85, ...), kind=kLoop, calls=%fused_computation.39 | loop fusion | flops 44037120 | bytes 16855040 | tf_op jit(solution)/shard_map/cond/branch_1_fun/reduce_sum | solution.py:69
  708.9 7.7 fusion.8
  721.0 16.7 %fusion.7 = f32[2048,256]{1,0:T(8,128)} fusion(f32[1024,2048]{1,0:T(8,128)} %copy-done, f32[1024,256]{1,0:T(8,128)S(1)} %bitcast.25, f32[2048,256]{1,0:T(8,128)S(1)} %bitcast.21, f32[2048]{0:T(1024)S(1)} %get-tuple-element.79), kind=kOutput, calls=%fused_computation.21 | convolution fusion | flops 6444023808 | bytes 13639680 | tf_op jit(solution)/shard_map/cond/branch_1_fun/dot_general | solution.py:68
  737.8 8.5 %all-to-all-done.2 = f32[16,64,256]{2,1,0:T(8,128)} async-done(((f32[16,64,256]{2,1,0:T(8,128)}), f32[16,64,256]{2,1,0:T(8,128)}, u32[]{:S(2)}, u32[]{:S(2)}) %all-to-all-start.2) | async-done | bytes 1048608 | tf_op jit(solution)/shard_map/cond/branch_1_fun/all_to_all | solution.py:78
  746.2 13.0 %all-to-all-start.3 = ((f32[16,128,256]{2,1,0:T(8,128)}), f32[16,128,256]{2,1,0:T(8,128)S(1)}, u32[]{:S(2)}, u32[]{:S(2)}) async-start(f32[16,128,256]{2,1,0:T(8,128)} %bitcast.22), calls=%async_computation.3 | async-start | bytes 4194304 | tf_op jit(solution)/shard_map/cond/branch_1_fun/all_to_all | solution.py:78
  760.5 28.3 %all-to-all-done.3 = f32[16,128,256]{2,1,0:T(8,128)S(1)} async-done(((f32[16,128,256]{2,1,0:T(8,128)}), f32[16,128,256]{2,1,0:T(8,128)S(1)}, u32[]{:S(2)}, u32[]{:S(2)}) %all-to-all-start.3) | async-done | bytes 2097184 | tf_op jit(solution)/shard_map/cond/branch_1_fun/all_to_all | solution.py:78
  (84 shorter events, 130.4 us)
Async XLA Ops:
  19.5 32.3 %collective-permute-start.6 = (f32[1024,256]{1,0:T(8,128)S(1)}, f32[1024,256]{1,0:T(8,128)S(1)}, u32[]{:S(2)}, u32[]{:S(2)}) collective-permute-start(f32[1024,256]{1,0:T(8,128)S(1)} %bitcast.17), channel_id=1, source_target_pairs={{0,16},{16,0},{1,17},{17,1},{2,18},{18,2},{3,19},{19,3},{4,20},{20... | collective-permute-start | bytes 3145736 | tf_op jit(solution)/shard_map/ppermute | solution.py:323
  21.6 10.5 %collective-permute-start = (f32[64,256]{1,0:T(8,128)}, f32[64,256]{1,0:T(8,128)S(1)}, u32[]{:S(2)}, u32[]{:S(2)}) collective-permute-start(f32[64,256]{1,0:T(8,128)} %own.1), channel_id=1, source_target_pairs={{0,1},{1,2},{2,3},{3,0},{4,5},{5,6},{6,7},{7,4},{8,9},{9,10},{10,1... | collective-permute-start | bytes 196616 | tf_op jit(solution)/shard_map/ppermute | solution.py:314
  24.6 9.4 %collective-permute-start.1 = (f32[64,256]{1,0:T(8,128)}, f32[64,256]{1,0:T(8,128)S(1)}, u32[]{:S(2)}, u32[]{:S(2)}) collective-permute-start(f32[64,256]{1,0:T(8,128)} %own.1), channel_id=1, source_target_pairs={{0,2},{1,3},{2,0},{3,1},{4,6},{5,7},{6,4},{7,5},{8,10},{9,11},{10,... | collective-permute-start | bytes 196616 | tf_op jit(solution)/shard_map/ppermute | solution.py:314
  28.8 7.5 collective-permute-start.2
  36.3 8.7 %collective-permute-start.3 = (f32[256,256]{1,0:T(8,128)S(1)}, f32[256,256]{1,0:T(8,128)S(1)}, u32[]{:S(2)}, u32[]{:S(2)}) collective-permute-start(f32[256,256]{1,0:T(8,128)S(1)} %constant_dynamic-update-slice_fusion.near), channel_id=1, source_target_pairs={{0,4},{4,8},{8,12},{12,0},{1,5},{5,9},{9,13},{13,1},{2,6},{6,10},{... | collective-permute-start | bytes 786440 | tf_op jit(solution)/shard_map/ppermute | solution.py:314
  37.6 14.2 %collective-permute-start.4 = (f32[256,256]{1,0:T(8,128)S(1)}, f32[256,256]{1,0:T(8,128)S(1)}, u32[]{:S(2)}, u32[]{:S(2)}) collective-permute-start(f32[256,256]{1,0:T(8,128)S(1)} %constant_dynamic-update-slice_fusion.near), channel_id=1, source_target_pairs={{0,8},{4,12},{8,0},{12,4},{1,9},{5,13},{9,1},{13,5},{2,10},{6,14},... | collective-permute-start | bytes 786440 | tf_op jit(solution)/shard_map/ppermute | solution.py:314
  40.3 11.5 %collective-permute-start.5 = (f32[256,256]{1,0:T(8,128)S(1)}, f32[256,256]{1,0:T(8,128)S(1)}, u32[]{:S(2)}, u32[]{:S(2)}) collective-permute-start(f32[256,256]{1,0:T(8,128)S(1)} %constant_dynamic-update-slice_fusion.near), channel_id=1, source_target_pairs={{0,12},{4,0},{8,4},{12,8},{1,13},{5,1},{9,5},{13,9},{2,14},{6,2},{... | collective-permute-start | bytes 786440 | tf_op jit(solution)/shard_map/ppermute | solution.py:314
  154.6 38.4 %copy-start.1 = (f32[64,256]{1,0:T(8,128)S(1)}, f32[64,256]{1,0:T(8,128)}, u32[]{:S(2)}) copy-start(f32[64,256]{1,0:T(8,128)} %own.1) | copy-start | bytes 196612
  154.6 38.4 %copy-start.2 = (f32[128,256]{1,0:T(8,128)S(1)}, f32[128,256]{1,0:T(8,128)}, u32[]{:S(2)}) copy-start(f32[128,256]{1,0:T(8,128)} %param.6) | copy-start | bytes 393220
  154.6 38.4 %copy-start.3 = (f32[2048]{0:T(1024)S(1)}, f32[2048]{0:T(1024)}, u32[]{:S(2)}) copy-start(f32[2048]{0:T(1024)} %param.7) | copy-start | bytes 24580
  158.9 3.8 collective-permute-start.13
  163.8 29.2 %all-to-all-start.12 = ((f32[8,128,256]{2,1,0:T(8,128)}), f32[8,128,256]{2,1,0:T(8,128)S(1)}, u32[]{:S(2)}, u32[]{:S(2)}) async-start(f32[8,128,256]{2,1,0:T(8,128)} %bitcast.10), calls=%async_computation.12 | async-start | bytes 2097152 | tf_op jit(solution)/shard_map/all_to_all | solution.py:78
  169.2 9.2 %collective-permute-start.7 = (f32[256,256]{1,0:T(8,128)S(1)}, f32[256,256]{1,0:T(8,128)S(1)}, u32[]{:S(2)}, u32[]{:S(2)}) collective-permute-start(f32[256,256]{1,0:T(8,128)S(1)} %get-tuple-element.62), channel_id=1, source_target_pairs={{0,4},{4,8},{8,12},{12,0},{1,5},{5,9},{9,13},{13,1},{2,6},{6,10},{... | collective-permute-start | bytes 786440 | tf_op jit(solution)/shard_map/ppermute | solution.py:314
  169.3 13.2 %collective-permute-start.8 = (f32[256,256]{1,0:T(8,128)S(1)}, f32[256,256]{1,0:T(8,128)S(1)}, u32[]{:S(2)}, u32[]{:S(2)}) collective-permute-start(f32[256,256]{1,0:T(8,128)S(1)} %get-tuple-element.63), channel_id=1, source_target_pairs={{0,8},{4,12},{8,0},{12,4},{1,9},{5,13},{9,1},{13,5},{2,10},{6,14},... | collective-permute-start | bytes 786440 | tf_op jit(solution)/shard_map/ppermute | solution.py:314
  171.2 12.5 %collective-permute-start.9 = (f32[256,256]{1,0:T(8,128)S(1)}, f32[256,256]{1,0:T(8,128)S(1)}, u32[]{:S(2)}, u32[]{:S(2)}) collective-permute-start(f32[256,256]{1,0:T(8,128)S(1)} %get-tuple-element.64), channel_id=1, source_target_pairs={{0,12},{4,0},{8,4},{12,8},{1,13},{5,1},{9,5},{13,9},{2,14},{6,2},{... | collective-permute-start | bytes 786440 | tf_op jit(solution)/shard_map/ppermute | solution.py:314
  184.3 6.3 collective-permute-start.10
  185.1 7.8 collective-permute-start.11
  187.2 5.8 collective-permute-start.12
  226.1 42.9 %all-to-all-start.1 = ((f32[16,128,256]{2,1,0:T(8,128)}), f32[16,128,256]{2,1,0:T(8,128)S(1)}, u32[]{:S(2)}, u32[]{:S(2)}) async-start(f32[16,128,256]{2,1,0:T(8,128)} %broadcast_in_dim.1), calls=%async_computation.1 | async-start | bytes 4194304 | tf_op jit(solution)/shard_map/cond/branch_1_fun/all_to_all | solution.py:78
  705.6 3.2 copy-start
  716.5 29.7 %all-to-all-start.2 = ((f32[16,64,256]{2,1,0:T(8,128)}), f32[16,64,256]{2,1,0:T(8,128)}, u32[]{:S(2)}, u32[]{:S(2)}) async-start(f32[16,64,256]{2,1,0:T(8,128)} %bitcast.26), calls=%async_computation.2 | async-start | bytes 2097152 | tf_op jit(solution)/shard_map/cond/branch_1_fun/all_to_all | solution.py:78
  746.2 42.5 %all-to-all-start.3 = ((f32[16,128,256]{2,1,0:T(8,128)}), f32[16,128,256]{2,1,0:T(8,128)S(1)}, u32[]{:S(2)}, u32[]{:S(2)}) async-start(f32[16,128,256]{2,1,0:T(8,128)} %bitcast.22), calls=%async_computation.3 | async-start | bytes 4194304 | tf_op jit(solution)/shard_map/cond/branch_1_fun/all_to_all | solution.py:78
  789.1 0.7 copy-start.4
  789.8 0.6 copy-start.5

commit v4 on v3

--- a/solution.py
+++ b/solution.py
@@ -141,19 +141,23 @@
     return lax.rem(place + by, size)
 
 
-def kernel_tile(place, start, near, *refs):
-    far, (mine, other), (docs, targets, tile, weight_out, part, doc_wide, target_wide) = refs[:-9], refs[-9:-7], refs[-7:]
+def kernel_tile(place, start, *refs):
+    (ys, zs), (xs, ls) = (SIZES["y"], SIZES["z_hi"]), (SIZES["x"], SIZES["z_lo"])
+    doc_pieces, mine, other = refs[:ys], refs[ys : ys + xs], refs[ys + xs : ys + 2 * xs]
+    docs, targets, tile, weight_out, part, doc_wide, target_wide = refs[ys + 2 * xs :]
     features = docs.shape[1]
-    sizes = SIZES["y"], SIZES["z_hi"]
-    share = docs.shape[0] // (sizes[0] * sizes[1])
-    for k, source in enumerate((near, *far)):
-        y = turned(place[0], sizes[0] - k, sizes[0])
-        for j in range(sizes[1]):
-            at = (y * sizes[1] + turned(place[1], sizes[1] - j, sizes[1])) * share
+    share, target_share = docs.shape[0] // (ys * zs), targets.shape[0] // (2 * xs * ls)
+    for k, source in enumerate(doc_pieces):
+        for j in range(zs):
+            at = (turned(place[0], ys - k, ys) * zs + turned(place[1], zs - j, zs)) * share
             docs[pl.ds(pl.multiple_of(at, share), share), :] = source[j * share : (j + 1) * share, :]
-    half = mine.shape[0]
-    targets[pl.ds(pl.multiple_of(place[2] * half, half), half), :] = mine[...]
-    targets[pl.ds(pl.multiple_of((1 - place[2]) * half, half), half), :] = other[...]
+    for core, pieces in ((place[2], mine), (1 - place[2], other)):
+        for k, source in enumerate(pieces):
+            for j in range(ls):
+                at = ((core * ls + turned(place[4], ls - j, ls)) * xs + turned(place[3], xs - k, xs)) * target_share
+                targets[pl.ds(pl.multiple_of(at, target_share), target_share), :] = source[
+                    j * target_share : (j + 1) * target_share, :
+                ]
     for source, wide, order in ((docs, doc_wide, (0, 0, 1)), (targets, target_wide, (0, 1, 0))):
         for rows in spans(source.shape[0], 256):
             pair = halves(source[rows, :])
@@ -310,19 +314,26 @@
 
 def ring(blocks, axis):
     size = SIZES[axis]
-    return [
-        block if k == 0 else lax.ppermute(block, axis, [(i, (i + k) % size) for i in range(size)])
-        for k, block in enumerate(blocks)
-    ]
+    out = [blocks[0]] * size
+    for k in sorted(range(1, size), key=lambda k: (min(k, size - k), k)):
+        out[k] = lax.ppermute(blocks[k], axis, [(i, (i + k) % size) for i in range(size)])
+    return out
+
+
+def other_core(block):
+    return lax.ppermute(block, "core", [(0, 1), (1, 0)])
 
 
 def local(embed_docs, embed_targets, start):
     rows, cols = lax.axis_size(ROW), lax.axis_size(COL)
-    place = jnp.stack([lax.axis_index(a) for a in ("y", "z_hi", "core")]).astype(jnp.int32)
-    mine = gather(embed_targets, ("z_lo", "x"))
-    other = lax.ppermute(mine, "core", [(0, 1), (1, 0)])
-    near = jnp.concatenate(ring([embed_docs] * SIZES["z_hi"], "z_hi"), axis=0)
-    doc_pieces = ring([near] * SIZES["y"], "y")
+    place = jnp.stack([lax.axis_index(a) for a in ("y", "z_hi", "core", "x", "z_lo")]).astype(jnp.int32)
+    near, beside = lax.optimization_barrier(
+        (ring([embed_docs] * SIZES["z_hi"], "z_hi"), ring([embed_targets] * SIZES["z_lo"], "z_lo"))
+    )
+    mine = ring([jnp.concatenate(beside, axis=0)] * SIZES["x"], "x")
+    doc_pieces = ring([jnp.concatenate(near, axis=0)] * SIZES["y"], "y")
+    other = [other_core(block) for block in mine]
+    doc_pieces, mine, other = lax.optimization_barrier((doc_pieces, mine, other))
     (share, features), (target_share, _) = embed_docs.shape, embed_targets.shape
     n, m = share * cols, target_share * rows
     ratio = (n * rows) / (m * cols)
@@ -331,7 +342,7 @@
     doc_parts, target_parts = ((cols, *doc_vector[0]), f32), ((rows, *target_vector[0]), f32)
     docs, targets, tile, target_zero, part = run(
         kernel_tile,
-        (start.reshape(target_vector[0]), *doc_pieces, mine, other),
+        (start.reshape(target_vector[0]), *doc_pieces, *mine, *other),
         [((n, features), f32), ((m, features), f32), ((n, m), f32), target_vector, doc_parts],
         [((n, 3 * features), bf16), ((m, 3 * features), bf16)],
         limit=28, kept=(2,), flops=product, place=place,
@@ -359,7 +370,7 @@
         kernel_targets, (top, low, mass, docs, targets), [((m // 2, features), f32)] * 2, [((2 * features, n), bf16)],
         limit=24, held=(0, 1), flops=product, place=place,
     )
-    (mine,) = run(kernel_pair, (mine, lax.ppermute(other, "core", [(0, 1), (1, 0)])), [((m // 2, features), f32)])
+    (mine,) = run(kernel_pair, (mine, other_core(other)), [((m // 2, features), f32)])
     doc_pieces = run(kernel_pieces, doc_pieces, [((share, features), f32)] * SIZES["z_hi"], place=place)
     doc_pieces = ring(doc_pieces, "z_hi")
     blocks = swap(mine.reshape(rows // 2, target_share, features), ("z_lo", "x"))

time: 800 us -> 782 us (0.978)
  blocking collectives: 504 us -> 483 us
    all_to_all x9 -> x8, blocking collectives: 134 us -> 113 us  [swap(): return lax.all_to_all(blocks, axis, 0, 0)]
    ppermute x14 -> x21, starting transfers between devices: 25.6 us -> 33.9 us  [the longest x16 26.7 us: ring(): lax.ppermute(blocks[k], axis, [(i, (i + k) % size) for i in range(size)])]
    ppermute x14 -> x21, waiting for transfers between devices: 30.8 us -> 29.4 us  [the longest x16 26 us: ring(): lax.ppermute(blocks[k], axis, [(i, (i + k) % size) for i in range(size)])]
  transfers between devices with their start and end apart: 18 -> 25, of which waited for: 12 -> 15; matrix products, arithmetic and copies ran while one was open for 3% -> 3% of each run, Pallas kernels for 0% -> 0%
where the time goes in v4:
time: 782 us; the launch traced here: 774 us
  blocking collectives  483 us (62%)
  waiting for transfers between devices  95.1 us (12%)
  starting transfers between devices  68.6 us (9%)
  other arithmetic  57.8 us (7%)
  matrix products  34.8 us (4%)
  Pallas kernels  24.1 us (3%)
  local copies, waits for them, and re-layouts  8.1 us (1%)
    all_to_all x8, blocking collectives, swap(): return lax.all_to_all(blocks, axis, 0, 0)  113 us
    pmax x2, blocking collectives, column_log_mass(): largest = lax.pmax(jnp.max(scores, axis=0), ROW)  78.4 us
    pmax x2, blocking collectives, row_log_mass(): largest = lax.pmax(jnp.max(scores, axis=1), COL)  68.2 us
    psum x2, blocking collectives, row_log_mass(): lax.psum(jnp.sum(jnp.exp(scores - largest[:, None]), axis=1), COL)  66.7 us
    all_to_all x4, waiting for transfers between devices, swap(): return lax.all_to_all(blocks, axis, 0, 0)  65.7 us
    psum x2, blocking collectives, column_log_mass(): lax.psum(jnp.sum(jnp.exp(scores - largest[None, :]), axis=0), ROW)  55.4 us
    psum x1, blocking collectives, log_domain(): target_bar_one = -lax.psum(jnp.sum(weighted, axis=0), ROW)  34.9 us
    all_to_all x4, starting transfers between devices, swap(): return lax.all_to_all(blocks, axis, 0, 0)  34.7 us
  transfers between devices with their start and end apart: 25, of which 15 were waited for; matrix products, arithmetic and copies ran while one was open for 3% of the time, Pallas kernels for 0%

profile of v4, /device:TPU:7, one launch (start us, length us, event | category | flops | bytes accessed | tf_op | source)
XLA Modules:
  0.0 774.3 jit_solution(2663907231202440282)
XLA Ops:
  40.7 5.5 shard_map.54
  46.2 14.5 %all_to_all.57.parts = f32[16,8,128]{2,1,0:T(8,128)S(1)} all-to-all(f32[16,8,128]{2,1,0:T(8,128)S(1)} %get-tuple-element.82), channel_id=1, replica_groups=mesh['z_lo'=2,'x'=4,'core'=2,'y'=4,'z_hi'=4] {'y','z_hi'}, dimensions={0} | all-to-all | bytes 131072 | tf_op jit(solution)/shard_map/all_to_all | solution.py:78
  61.3 10.8 %all_to_all.58.parts = f32[16,16,128]{2,1,0:T(8,128)S(1)} all-to-all(f32[16,16,128]{2,1,0:T(8,128)S(1)} %get-tuple-element.83), channel_id=1, replica_groups=mesh['z_lo'=2,'x'=4,'core'=2,'y'=4,'z_hi'=4] {'z_lo','x','core'}, dimensions={0} | all-to-all | bytes 262144 | tf_op jit(solution)/shard_map/all_to_all | solution.py:78
  72.8 11.8 %all_to_all.59.parts = f32[16,8,128]{2,1,0:T(8,128)S(1)} all-to-all(f32[16,8,128]{2,1,0:T(8,128)S(1)} %get-tuple-element.84), channel_id=1, replica_groups=mesh['z_lo'=2,'x'=4,'core'=2,'y'=4,'z_hi'=4] {'y','z_hi'}, dimensions={0} | all-to-all | bytes 131072 | tf_op jit(solution)/shard_map/all_to_all | solution.py:78
  85.2 10.3 %all_to_all.60.parts = f32[16,16,128]{2,1,0:T(8,128)S(1)} all-to-all(f32[16,16,128]{2,1,0:T(8,128)S(1)} %get-tuple-element.85), channel_id=1, replica_groups=mesh['z_lo'=2,'x'=4,'core'=2,'y'=4,'z_hi'=4] {'z_lo','x','core'}, dimensions={0} | all-to-all | bytes 262144 | tf_op jit(solution)/shard_map/all_to_all | solution.py:78
  96.2 11.8 %all_to_all.61.parts = f32[16,8,128]{2,1,0:T(8,128)S(1)} all-to-all(f32[16,8,128]{2,1,0:T(8,128)S(1)} %get-tuple-element.86), channel_id=1, replica_groups=mesh['z_lo'=2,'x'=4,'core'=2,'y'=4,'z_hi'=4] {'y','z_hi'}, dimensions={0} | all-to-all | bytes 131072 | tf_op jit(solution)/shard_map/all_to_all | solution.py:78
  108.7 10.4 %all_to_all.62.parts = f32[16,16,128]{2,1,0:T(8,128)S(1)} all-to-all(f32[16,16,128]{2,1,0:T(8,128)S(1)} %get-tuple-element.89), channel_id=1, replica_groups=mesh['z_lo'=2,'x'=4,'core'=2,'y'=4,'z_hi'=4] {'z_lo','x','core'}, dimensions={0} | all-to-all | bytes 262144 | tf_op jit(solution)/shard_map/all_to_all | solution.py:78
  119.7 12.0 %all_to_all.63.parts = f32[16,8,128]{2,1,0:T(8,128)S(1)} all-to-all(f32[16,8,128]{2,1,0:T(8,128)S(1)} %get-tuple-element.91), channel_id=1, replica_groups=mesh['z_lo'=2,'x'=4,'core'=2,'y'=4,'z_hi'=4] {'y','z_hi'}, dimensions={0} | all-to-all | bytes 131072 | tf_op jit(solution)/shard_map/all_to_all | solution.py:78
  131.7 8.7 %shard_map.61 = (bf16[1024,2048]{1,0:T(8,128)(2,1)S(1)}, bf16[1024,2048]{1,0:T(8,128)(2,1)S(1)}, f32[16,128]{1,0:T(8,128)S(1)}, f32[256,256]{1,0:T(8,128)S(1)}, ...) custom-call(s32[5]{0:T(128)S(1)} %stack.23.place, ...), custom_call_target="tpu_custom_call" | custom-call | flops 3221225472 | bytes 10596372 | tf_op jit(solution)/shard_map/pallas_call | solution.py:304
  158.0 6.1 collective-permute-done.14.refs_1_
  179.0 593.8 %conditional.1 = ((f32[64,256]{1,0:T(8,128)S(1)}, f32[128,256]{1,0:T(8,128)S(1)})) conditional(s32[]{:T(128)} %convert_element_type.3, (f32[64,256]{1,0:T(8,128)S(1)}, f32[128,256]{1,0:T(8,128)S(1)}) %shard_map.65, (f32[2048]{0:T(1024)S(1)}, f32[64,256]{1,0:T(8,128)S(1)}, f32[128,256]{1,0:T(8,128)S(1)}) %tuple.34), branch_computations={%region_1.0_spmd, %region_2.0_spmd} | conditional | flops 19470446592 | bytes 200188064 | solution.py:380
  179.1 31.0 %all_to_all.56 = f32[16,64,256]{2,1,0:T(8,128)S(1)} all-to-all(f32[16,64,256]{2,1,0:T(8,128)S(1)} %broadcast_in_dim.0), channel_id=1, replica_groups=mesh['z_lo'=2,'x'=4,'core'=2,'y'=4,'z_hi'=4] {'y','z_hi'}, dimensions={0} | all-to-all | bytes 2097152 | tf_op jit(solution)/shard_map/cond/branch_1_fun/all_to_all | solution.py:78
  211.7 13.5 %all-to-all-start.1 = ((f32[16,128,256]{2,1,0:T(8,128)}), f32[16,128,256]{2,1,0:T(8,128)S(1)}, u32[]{:S(2)}, u32[]{:S(2)}) async-start(f32[16,128,256]{2,1,0:T(8,128)} %broadcast_in_dim.1), calls=%async_computation.1 | async-start | bytes 4194304 | tf_op jit(solution)/shard_map/cond/branch_1_fun/all_to_all | solution.py:78
  225.4 29.2 %all-to-all-done.1 = f32[16,128,256]{2,1,0:T(8,128)S(1)} async-done(((f32[16,128,256]{2,1,0:T(8,128)}), f32[16,128,256]{2,1,0:T(8,128)S(1)}, u32[]{:S(2)}, u32[]{:S(2)}) %all-to-all-start.1) | async-done | bytes 2097184 | tf_op jit(solution)/shard_map/cond/branch_1_fun/all_to_all | solution.py:78
  255.0 10.5 %fusion.3 = (f32[1024]{0:T(1024)S(1)}, f32[1024,2048]{1,0:T(8,128)}) fusion(f32[2048]{0:T(1024)S(1)} %get-tuple-element.10, f32[1024,256]{1,0:T(8,128)S(1)} %bitcast.22, f32[2048,256]{1,0:T(8,128)S(1)} %bitcast.18, f32[2048]{0:T(1024)S(1)} %bitcast.27, f32[1024]{0:T(1024)S(1)} %add.22), kind=kOutput, calls=%fused_computation.16 | convolution fusion | flops 6455032832 | bytes 11558912 | tf_op jit(solution)/shard_map/cond/branch_1_fun/dot_general | solution.py:38
  265.5 34.0 %pmax.24 = f32[1024]{0:T(1024)S(1)} all-reduce(f32[1024]{0:T(1024)S(1)} %get-tuple-element.124), channel_id=1, replica_groups=mesh['z_lo'=2,'x'=4,'core'=2,'y'=4,'z_hi'=4] {'y','z_hi'}, use_global_device_ids=true, to_apply=%region_6.0 | all-reduce | flops 1024 | bytes 8192 | tf_op jit(solution)/shard_map/cond/branch_1_fun/pmax | solution.py:21
  304.0 33.4 %psum.42 = f32[1024]{0:T(1024)S(1)} all-reduce(f32[1024]{0:T(1024)S(1)} %exponential_reduce_fusion.3), channel_id=1, replica_groups=mesh['z_lo'=2,'x'=4,'core'=2,'y'=4,'z_hi'=4] {'y','z_hi'}, use_global_device_ids=true, to_apply=%region_8.0 | all-reduce | flops 1024 | bytes 8192 | tf_op jit(solution)/shard_map/cond/branch_1_fun/psum | solution.py:22
  341.6 37.3 %pmax.25 = f32[2048]{0:T(1024)S(1)} all-reduce(f32[2048]{0:T(1024)S(1)} %fusion.4), channel_id=1, replica_groups=mesh['z_lo'=2,'x'=4,'core'=2,'y'=4,'z_hi'=4] {'z_lo','x','core'}, use_global_device_ids=true, to_apply=%region_10.0 | all-reduce | flops 2048 | bytes 16384 | tf_op jit(solution)/shard_map/cond/branch_1_fun/pmax | solution.py:27
  383.5 27.8 %psum.43 = f32[2048]{0:T(1024)S(1)} all-reduce(f32[2048]{0:T(1024)S(1)} %exponential_reduce_fusion.2), channel_id=1, replica_groups=mesh['z_lo'=2,'x'=4,'core'=2,'y'=4,'z_hi'=4] {'z_lo','x','core'}, use_global_device_ids=true, to_apply=%region_12.0 | all-reduce | flops 2048 | bytes 16384 | tf_op jit(solution)/shard_map/cond/branch_1_fun/psum | solution.py:28
  415.5 34.2 %pmax.26 = f32[1024]{0:T(1024)S(1)} all-reduce(f32[1024]{0:T(1024)S(1)} %fusion.5), channel_id=1, replica_groups=mesh['z_lo'=2,'x'=4,'core'=2,'y'=4,'z_hi'=4] {'y','z_hi'}, use_global_device_ids=true, to_apply=%region_14.0 | all-reduce | flops 1024 | bytes 8192 | tf_op jit(solution)/shard_map/cond/branch_1_fun/pmax | solution.py:21
  454.3 33.4 %psum.44 = f32[1024]{0:T(1024)S(1)} all-reduce(f32[1024]{0:T(1024)S(1)} %exponential_reduce_fusion.1), channel_id=1, replica_groups=mesh['z_lo'=2,'x'=4,'core'=2,'y'=4,'z_hi'=4] {'y','z_hi'}, use_global_device_ids=true, to_apply=%region_16.0 | all-reduce | flops 1024 | bytes 8192 | tf_op jit(solution)/shard_map/cond/branch_1_fun/psum | solution.py:22
  491.9 41.1 %pmax.27 = f32[2048]{0:T(1024)S(1)} all-reduce(f32[2048]{0:T(1024)S(1)} %fusion.6), channel_id=1, replica_groups=mesh['z_lo'=2,'x'=4,'core'=2,'y'=4,'z_hi'=4] {'z_lo','x','core'}, use_global_device_ids=true, to_apply=%region_18.0 | all-reduce | flops 2048 | bytes 16384 | tf_op jit(solution)/shard_map/cond/branch_1_fun/pmax | solution.py:27
  537.5 27.7 %psum.45 = f32[2048]{0:T(1024)S(1)} all-reduce(f32[2048]{0:T(1024)S(1)} %exponential_reduce_fusion), channel_id=1, replica_groups=mesh['z_lo'=2,'x'=4,'core'=2,'y'=4,'z_hi'=4] {'z_lo','x','core'}, use_global_device_ids=true, to_apply=%region_20.0 | all-reduce | flops 2048 | bytes 16384 | tf_op jit(solution)/shard_map/cond/branch_1_fun/psum | solution.py:28
  569.7 33.9 %psum.46 = f32[1024]{0:T(1024)S(1)} all-reduce(f32[1024]{0:T(1024)S(1)} %fusion), channel_id=1, replica_groups=mesh['z_lo'=2,'x'=4,'core'=2,'y'=4,'z_hi'=4] {'y','z_hi'}, use_global_device_ids=true, to_apply=%region_22.0 | all-reduce | flops 1024 | bytes 8192 | tf_op jit(solution)/shard_map/cond/branch_1_fun/psum | solution.py:53
  608.2 34.9 %psum.47 = f32[2048]{0:T(1024)S(1)} all-reduce(f32[2048]{0:T(1024)S(1)} %fusion.1), channel_id=1, replica_groups=mesh['z_lo'=2,'x'=4,'core'=2,'y'=4,'z_hi'=4] {'z_lo','x','core'}, use_global_device_ids=true, to_apply=%region_24.0 | all-reduce | flops 2048 | bytes 16384 | tf_op jit(solution)/shard_map/cond/branch_1_fun/psum | solution.py:57
  647.8 32.8 %psum.48 = f32[1024]{0:T(1024)S(1)} all-reduce(f32[1024]{0:T(1024)S(1)} %fusion.2), channel_id=1, replica_groups=mesh['z_lo'=2,'x'=4,'core'=2,'y'=4,'z_hi'=4] {'y','z_hi'}, use_global_device_ids=true, to_apply=%region_26.0 | all-reduce | flops 1024 | bytes 8192 | tf_op jit(solution)/shard_map/cond/branch_1_fun/psum | solution.py:61
  680.6 10.7 %fusion.9 = (f32[2048]{0:T(1024)S(1)}, f32[1024]{0:T(1024)S(1)}, f32[1024,2048]{1,0:T(8,128)S(1)}) fusion(f32[1024]{0:T(1024)S(1)} %get-tuple-element.123, f32[1024,2048]{1,0:T(8,128)} %get-tuple-element.125, f32[2048]{0:T(1024)S(1)} %get-tuple-element.10, f32[1024]{0:T(1024)S(1)} %neg.5, f32[2048]{0:T(1024)S(1)} %get-tuple-element.121, ...), kind=kLoop, calls=%fused_computation.40 | loop fusion | flops 44037120 | bytes 16855040 | tf_op jit(solution)/shard_map/cond/branch_1_fun/reduce_sum | solution.py:69
  694.5 7.7 fusion.8
  706.7 16.6 %fusion.7 = f32[2048,256]{1,0:T(8,128)} fusion(f32[1024,2048]{1,0:T(8,128)} %copy-done, f32[1024,256]{1,0:T(8,128)S(1)} %bitcast.24, f32[2048,256]{1,0:T(8,128)S(1)} %bitcast.20, f32[2048]{0:T(1024)S(1)} %get-tuple-element.115), kind=kOutput, calls=%fused_computation.21 | convolution fusion | flops 6444023808 | bytes 13639680 | tf_op jit(solution)/shard_map/cond/branch_1_fun/dot_general | solution.py:68
  723.3 8.6 %all-to-all-done.2 = f32[16,64,256]{2,1,0:T(8,128)} async-done(((f32[16,64,256]{2,1,0:T(8,128)}), f32[16,64,256]{2,1,0:T(8,128)}, u32[]{:S(2)}, u32[]{:S(2)}) %all-to-all-start.2) | async-done | bytes 1048608 | tf_op jit(solution)/shard_map/cond/branch_1_fun/all_to_all | solution.py:78
  732.0 11.3 %all-to-all-start.3 = ((f32[16,128,256]{2,1,0:T(8,128)}), f32[16,128,256]{2,1,0:T(8,128)S(1)}, u32[]{:S(2)}, u32[]{:S(2)}) async-start(f32[16,128,256]{2,1,0:T(8,128)} %bitcast.21), calls=%async_computation.3 | async-start | bytes 4194304 | tf_op jit(solution)/shard_map/cond/branch_1_fun/all_to_all | solution.py:78
  744.5 27.9 %all-to-all-done.3 = f32[16,128,256]{2,1,0:T(8,128)S(1)} async-done(((f32[16,128,256]{2,1,0:T(8,128)}), f32[16,128,256]{2,1,0:T(8,128)S(1)}, u32[]{:S(2)}, u32[]{:S(2)}) %all-to-all-start.3) | async-done | bytes 2097184 | tf_op jit(solution)/shard_map/cond/branch_1_fun/all_to_all | solution.py:78
  (98 shorter events, 132.4 us)
Async XLA Ops:
  0.6 16.4 %collective-permute-start.3 = (f32[128,256]{1,0:T(8,128)}, f32[128,256]{1,0:T(8,128)S(1)}, u32[]{:S(2)}, u32[]{:S(2)}) collective-permute-start(f32[128,256]{1,0:T(8,128)} %param.6), channel_id=1, source_target_pairs={{0,128},{128,0},{1,129},{129,1},{2,130},{130,2},{3,131},{131,3},{4... | collective-permute-start | bytes 393224 | tf_op jit(solution)/shard_map/ppermute | solution.py:319
  2.4 10.7 %collective-permute-start = (f32[64,256]{1,0:T(8,128)}, f32[64,256]{1,0:T(8,128)S(1)}, u32[]{:S(2)}, u32[]{:S(2)}) collective-permute-start(f32[64,256]{1,0:T(8,128)} %own.1), channel_id=1, source_target_pairs={{0,1},{1,2},{2,3},{3,0},{4,5},{5,6},{6,7},{7,4},{8,9},{9,10},{10,1... | collective-permute-start | bytes 196616 | tf_op jit(solution)/shard_map/ppermute | solution.py:319
  5.3 10.2 %collective-permute-start.1 = (f32[64,256]{1,0:T(8,128)}, f32[64,256]{1,0:T(8,128)S(1)}, u32[]{:S(2)}, u32[]{:S(2)}) collective-permute-start(f32[64,256]{1,0:T(8,128)} %own.1), channel_id=1, source_target_pairs={{0,2},{1,3},{2,0},{3,1},{4,6},{5,7},{6,4},{7,5},{8,10},{9,11},{10,... | collective-permute-start | bytes 196616 | tf_op jit(solution)/shard_map/ppermute | solution.py:319
  9.6 7.5 collective-permute-start.2
  17.9 7.8 %collective-permute-start.4 = (f32[256,256]{1,0:T(8,128)S(1)}, f32[256,256]{1,0:T(8,128)S(1)}, u32[]{:S(2)}, u32[]{:S(2)}) collective-permute-start(f32[256,256]{1,0:T(8,128)S(1)} %constant_dynamic-update-slice_fusion.refs_0_), channel_id=1, source_target_pairs={{0,4},{4,8},{8,12},{12,0},{1,5},{5,9},{9,13},{13,1},{2,6},{6,10},{... | collective-permute-start | bytes 786440 | tf_op jit(solution)/shard_map/ppermute | solution.py:319
  19.3 13.1 %collective-permute-start.5 = (f32[256,256]{1,0:T(8,128)S(1)}, f32[256,256]{1,0:T(8,128)S(1)}, u32[]{:S(2)}, u32[]{:S(2)}) collective-permute-start(f32[256,256]{1,0:T(8,128)S(1)} %constant_dynamic-update-slice_fusion.refs_0_), channel_id=1, source_target_pairs={{0,8},{4,12},{8,0},{12,4},{1,9},{5,13},{9,1},{13,5},{2,10},{6,14},... | collective-permute-start | bytes 786440 | tf_op jit(solution)/shard_map/ppermute | solution.py:319
  22.9 11.9 %collective-permute-start.7 = (f32[256,256]{1,0:T(8,128)S(1)}, f32[256,256]{1,0:T(8,128)S(1)}, u32[]{:S(2)}, u32[]{:S(2)}) collective-permute-start(f32[256,256]{1,0:T(8,128)S(1)} %constant_dynamic-update-slice_fusion.4.refs_4_), channel_id=1, source_target_pairs={{0,32},{32,64},{64,96},{96,0},{1,33},{33,65},{65,97},{97,1},{2,34}... | collective-permute-start | bytes 786440 | tf_op jit(solution)/shard_map/ppermute | solution.py:319
  23.1 11.7 %collective-permute-start.8 = (f32[256,256]{1,0:T(8,128)S(1)}, f32[256,256]{1,0:T(8,128)S(1)}, u32[]{:S(2)}, u32[]{:S(2)}) collective-permute-start(f32[256,256]{1,0:T(8,128)S(1)} %constant_dynamic-update-slice_fusion.4.refs_4_), channel_id=1, source_target_pairs={{0,64},{32,96},{64,0},{96,32},{1,65},{33,97},{65,1},{97,33},{2,66}... | collective-permute-start | bytes 786440 | tf_op jit(solution)/shard_map/ppermute | solution.py:319
  25.3 12.2 %collective-permute-start.9 = (f32[256,256]{1,0:T(8,128)S(1)}, f32[256,256]{1,0:T(8,128)S(1)}, u32[]{:S(2)}, u32[]{:S(2)}) collective-permute-start(f32[256,256]{1,0:T(8,128)S(1)} %constant_dynamic-update-slice_fusion.4.refs_4_), channel_id=1, source_target_pairs={{0,96},{32,0},{64,32},{96,64},{1,97},{33,1},{65,33},{97,65},{2,98}... | collective-permute-start | bytes 786440 | tf_op jit(solution)/shard_map/ppermute | solution.py:319
  25.7 13.9 %collective-permute-start.6 = (f32[256,256]{1,0:T(8,128)S(1)}, f32[256,256]{1,0:T(8,128)S(1)}, u32[]{:S(2)}, u32[]{:S(2)}) collective-permute-start(f32[256,256]{1,0:T(8,128)S(1)} %constant_dynamic-update-slice_fusion.refs_0_), channel_id=1, source_target_pairs={{0,12},{4,0},{8,4},{12,8},{1,13},{5,1},{9,5},{13,9},{2,14},{6,2},{... | collective-permute-start | bytes 786440 | tf_op jit(solution)/shard_map/ppermute | solution.py:319
  32.4 7.2 collective-permute-start.10
  34.8 4.8 collective-permute-start.11
  34.8 4.8 collective-permute-start.12
  37.5 3.2 collective-permute-start.13
  140.3 38.5 %copy-start.1 = (f32[64,256]{1,0:T(8,128)S(1)}, f32[64,256]{1,0:T(8,128)}, u32[]{:S(2)}) copy-start(f32[64,256]{1,0:T(8,128)} %own.1) | copy-start | bytes 196612
  140.4 38.5 %copy-start.2 = (f32[128,256]{1,0:T(8,128)S(1)}, f32[128,256]{1,0:T(8,128)}, u32[]{:S(2)}) copy-start(f32[128,256]{1,0:T(8,128)} %param.6) | copy-start | bytes 393220
  140.4 38.5 %copy-start.3 = (f32[2048]{0:T(1024)S(1)}, f32[2048]{0:T(1024)}, u32[]{:S(2)}) copy-start(f32[2048]{0:T(1024)} %param.7) | copy-start | bytes 24580
  144.6 3.7 collective-permute-start.20
  149.5 29.3 %all-to-all-start.11 = ((f32[8,128,256]{2,1,0:T(8,128)}), f32[8,128,256]{2,1,0:T(8,128)S(1)}, u32[]{:S(2)}, u32[]{:S(2)}) async-start(f32[8,128,256]{2,1,0:T(8,128)} %bitcast.11), calls=%async_computation.11 | async-start | bytes 2097152 | tf_op jit(solution)/shard_map/all_to_all | solution.py:78
  154.9 9.2 %collective-permute-start.14 = (f32[256,256]{1,0:T(8,128)S(1)}, f32[256,256]{1,0:T(8,128)S(1)}, u32[]{:S(2)}, u32[]{:S(2)}) collective-permute-start(f32[256,256]{1,0:T(8,128)S(1)} %get-tuple-element.98), channel_id=1, source_target_pairs={{0,4},{4,8},{8,12},{12,0},{1,5},{5,9},{9,13},{13,1},{2,6},{6,10},{... | collective-permute-start | bytes 786440 | tf_op jit(solution)/shard_map/ppermute | solution.py:319
  155.1 13.2 %collective-permute-start.15 = (f32[256,256]{1,0:T(8,128)S(1)}, f32[256,256]{1,0:T(8,128)S(1)}, u32[]{:S(2)}, u32[]{:S(2)}) collective-permute-start(f32[256,256]{1,0:T(8,128)S(1)} %get-tuple-element.99), channel_id=1, source_target_pairs={{0,8},{4,12},{8,0},{12,4},{1,9},{5,13},{9,1},{13,5},{2,10},{6,14},... | collective-permute-start | bytes 786440 | tf_op jit(solution)/shard_map/ppermute | solution.py:319
  157.0 12.5 %collective-permute-start.16 = (f32[256,256]{1,0:T(8,128)S(1)}, f32[256,256]{1,0:T(8,128)S(1)}, u32[]{:S(2)}, u32[]{:S(2)}) collective-permute-start(f32[256,256]{1,0:T(8,128)S(1)} %get-tuple-element.100), channel_id=1, source_target_pairs={{0,12},{4,0},{8,4},{12,8},{1,13},{5,1},{9,5},{13,9},{2,14},{6,2},{... | collective-permute-start | bytes 786440 | tf_op jit(solution)/shard_map/ppermute | solution.py:319
  170.1 6.4 collective-permute-start.17
  170.9 7.9 %collective-permute-start.18 = (f32[64,256]{1,0:T(8,128)S(1)}, f32[64,256]{1,0:T(8,128)S(1)}, u32[]{:S(2)}, u32[]{:S(2)}) collective-permute-start(f32[64,256]{1,0:T(8,128)S(1)} %get-tuple-element.103), channel_id=1, source_target_pairs={{0,2},{1,3},{2,0},{3,1},{4,6},{5,7},{6,4},{7,5},{8,10},{9,11},{10,... | collective-permute-start | bytes 196616 | tf_op jit(solution)/shard_map/ppermute | solution.py:319
  173.1 5.8 collective-permute-start.19
  211.7 43.0 %all-to-all-start.1 = ((f32[16,128,256]{2,1,0:T(8,128)}), f32[16,128,256]{2,1,0:T(8,128)S(1)}, u32[]{:S(2)}, u32[]{:S(2)}) async-start(f32[16,128,256]{2,1,0:T(8,128)} %broadcast_in_dim.1), calls=%async_computation.1 | async-start | bytes 4194304 | tf_op jit(solution)/shard_map/cond/branch_1_fun/all_to_all | solution.py:78
  691.3 3.2 copy-start
  702.2 29.8 %all-to-all-start.2 = ((f32[16,64,256]{2,1,0:T(8,128)}), f32[16,64,256]{2,1,0:T(8,128)}, u32[]{:S(2)}, u32[]{:S(2)}) async-start(f32[16,64,256]{2,1,0:T(8,128)} %bitcast.25), calls=%async_computation.2 | async-start | bytes 2097152 | tf_op jit(solution)/shard_map/cond/branch_1_fun/all_to_all | solution.py:78
  732.0 40.4 %all-to-all-start.3 = ((f32[16,128,256]{2,1,0:T(8,128)}), f32[16,128,256]{2,1,0:T(8,128)S(1)}, u32[]{:S(2)}, u32[]{:S(2)}) async-start(f32[16,128,256]{2,1,0:T(8,128)} %bitcast.21), calls=%async_computation.3 | async-start | bytes 4194304 | tf_op jit(solution)/shard_map/cond/branch_1_fun/all_to_all | solution.py:78
  772.8 0.7 copy-start.4
  773.4 0.6 copy-start.5

commit v5 on v4

--- a/solution.py
+++ b/solution.py
@@ -377,11 +377,11 @@
     grads = run(
         kernel_grads, (embed_docs, *doc_pieces, blocks), [((share, features), f32), ((target_share, features), f32)]
     )
-    return lax.cond(
-        jnp.isnan(jnp.sum(bar_two)),
-        lambda: log_domain(embed_docs, embed_targets, start),
-        lambda: tuple(grads),
-    )
+    return lax.while_loop(
+        lambda state: state[0],
+        lambda state: (False, *log_domain(embed_docs, embed_targets, start)),
+        (jnp.isnan(jnp.sum(bar_two)), *grads),
+    )[1:]
 
 
 def solution(mesh):

time: 782 us -> 804 us (1.028)
  loops' own time: 0.44 us -> 22.3 us
    another operation x1, loops' own time: 0.44 us -> 22.3 us  [local(): lax.while_loop(lambda state: state[0], lambda state: (False, *log_domain(...]
where the time goes in v5:
time: 804 us; the launch traced here: 796 us
  blocking collectives  483 us (60%)
  waiting for transfers between devices  93.5 us (12%)
  starting transfers between devices  69.3 us (9%)
  other arithmetic  59.1 us (7%)
  matrix products  34.8 us (4%)
  Pallas kernels  24.8 us (3%)
  loops' own time  22.3 us (3%)
    all_to_all x8, blocking collectives, swap(): return lax.all_to_all(blocks, axis, 0, 0)  113 us
    pmax x2, blocking collectives, column_log_mass(): largest = lax.pmax(jnp.max(scores, axis=0), ROW)  78 us
    pmax x2, blocking collectives, row_log_mass(): largest = lax.pmax(jnp.max(scores, axis=1), COL)  68.2 us
    psum x2, blocking collectives, row_log_mass(): lax.psum(jnp.sum(jnp.exp(scores - largest[:, None]), axis=1), COL)  66.7 us
    all_to_all x4, waiting for transfers between devices, swap(): return lax.all_to_all(blocks, axis, 0, 0)  64.1 us
    psum x2, blocking collectives, column_log_mass(): lax.psum(jnp.sum(jnp.exp(scores - largest[None, :]), axis=0), ROW)  55.4 us
    all_to_all x4, starting transfers between devices, swap(): return lax.all_to_all(blocks, axis, 0, 0)  35.6 us
    psum x1, blocking collectives, log_domain(): target_bar_one = -lax.psum(jnp.sum(weighted, axis=0), ROW)  34.9 us
  transfers between devices with their start and end apart: 25, of which 15 were waited for; matrix products, arithmetic and copies ran while one was open for 3% of the time, Pallas kernels for 0%

profile of v5, /device:TPU:7, one launch (start us, length us, event | category | flops | bytes accessed | tf_op | source)
XLA Modules:
  0.0 796.4 jit_solution(5872188945672388694)
XLA Ops:
  40.3 5.5 shard_map.50
  45.8 14.5 %all_to_all.57.parts = f32[16,8,128]{2,1,0:T(8,128)S(1)} all-to-all(f32[16,8,128]{2,1,0:T(8,128)S(1)} %get-tuple-element.101), channel_id=1, replica_groups=mesh['z_lo'=2,'x'=4,'core'=2,'y'=4,'z_hi'=4] {'y','z_hi'}, dimensions={0} | all-to-all | bytes 131072 | tf_op jit(solution)/shard_map/all_to_all | solution.py:78
  61.0 10.8 %all_to_all.58.parts = f32[16,16,128]{2,1,0:T(8,128)S(1)} all-to-all(f32[16,16,128]{2,1,0:T(8,128)S(1)} %get-tuple-element.102), channel_id=1, replica_groups=mesh['z_lo'=2,'x'=4,'core'=2,'y'=4,'z_hi'=4] {'z_lo','x','core'}, dimensions={0} | all-to-all | bytes 262144 | tf_op jit(solution)/shard_map/all_to_all | solution.py:78
  72.4 11.8 %all_to_all.59.parts = f32[16,8,128]{2,1,0:T(8,128)S(1)} all-to-all(f32[16,8,128]{2,1,0:T(8,128)S(1)} %get-tuple-element.103), channel_id=1, replica_groups=mesh['z_lo'=2,'x'=4,'core'=2,'y'=4,'z_hi'=4] {'y','z_hi'}, dimensions={0} | all-to-all | bytes 131072 | tf_op jit(solution)/shard_map/all_to_all | solution.py:78
  84.9 10.3 %all_to_all.60.parts = f32[16,16,128]{2,1,0:T(8,128)S(1)} all-to-all(f32[16,16,128]{2,1,0:T(8,128)S(1)} %get-tuple-element.104), channel_id=1, replica_groups=mesh['z_lo'=2,'x'=4,'core'=2,'y'=4,'z_hi'=4] {'z_lo','x','core'}, dimensions={0} | all-to-all | bytes 262144 | tf_op jit(solution)/shard_map/all_to_all | solution.py:78
  95.8 11.8 %all_to_all.61.parts = f32[16,8,128]{2,1,0:T(8,128)S(1)} all-to-all(f32[16,8,128]{2,1,0:T(8,128)S(1)} %get-tuple-element.105), channel_id=1, replica_groups=mesh['z_lo'=2,'x'=4,'core'=2,'y'=4,'z_hi'=4] {'y','z_hi'}, dimensions={0} | all-to-all | bytes 131072 | tf_op jit(solution)/shard_map/all_to_all | solution.py:78
  108.3 10.4 %all_to_all.62.parts = f32[16,16,128]{2,1,0:T(8,128)S(1)} all-to-all(f32[16,16,128]{2,1,0:T(8,128)S(1)} %get-tuple-element.108), channel_id=1, replica_groups=mesh['z_lo'=2,'x'=4,'core'=2,'y'=4,'z_hi'=4] {'z_lo','x','core'}, dimensions={0} | all-to-all | bytes 262144 | tf_op jit(solution)/shard_map/all_to_all | solution.py:78
  119.3 12.1 %all_to_all.63.parts = f32[16,8,128]{2,1,0:T(8,128)S(1)} all-to-all(f32[16,8,128]{2,1,0:T(8,128)S(1)} %get-tuple-element.110), channel_id=1, replica_groups=mesh['z_lo'=2,'x'=4,'core'=2,'y'=4,'z_hi'=4] {'y','z_hi'}, dimensions={0} | all-to-all | bytes 131072 | tf_op jit(solution)/shard_map/all_to_all | solution.py:78
  131.4 8.7 %shard_map.57 = (bf16[1024,2048]{1,0:T(8,128)(2,1)S(1)}, bf16[1024,2048]{1,0:T(8,128)(2,1)S(1)}, f32[16,128]{1,0:T(8,128)S(1)}, f32[256,256]{1,0:T(8,128)S(1)}, ...) custom-call(s32[5]{0:T(128)S(1)} %stack.23.place, ...), custom_call_target="tpu_custom_call" | custom-call | flops 3221225472 | bytes 10596372 | tf_op jit(solution)/shard_map/pallas_call | solution.py:304
  157.9 5.9 collective-permute-done.14.refs_1_
  179.5 615.6 %while.11 = (pred[]{:T(512)}, f32[64,256]{1,0:T(8,128)}, f32[128,256]{1,0:T(8,128)}, f32[2048]{0:T(1024)S(1)}, f32[64,256]{1,0:T(8,128)S(1)}, /*index=5*/f32[128,256]{1,0:T(8,128)S(1)}) while((pred[]{:T(512)}, f32[64,256]{1,0:T(8,128)}, f32[128,256]{1,0:T(8,128)}, f32[2048]{0:T(1024)S(1)}, f32[64,256]{1,0:T(8,128)S(1)}, ...), condition=%region_30.0_spmd, body=%region_1.0_spmd | while | flops 19470446592 | bytes 200188080 | solution.py:380
  201.6 31.1 %all_to_all.56 = f32[16,64,256]{2,1,0:T(8,128)S(1)} all-to-all(f32[16,64,256]{2,1,0:T(8,128)S(1)} %broadcast_in_dim.0), channel_id=1, replica_groups=mesh['z_lo'=2,'x'=4,'core'=2,'y'=4,'z_hi'=4] {'y','z_hi'}, dimensions={0} | all-to-all | bytes 2097152 | tf_op jit(solution)/shard_map/while/body/all_to_all | solution.py:78
  234.2 13.5 %all-to-all-start.1 = ((f32[16,128,256]{2,1,0:T(8,128)}), f32[16,128,256]{2,1,0:T(8,128)S(1)}, u32[]{:S(2)}, u32[]{:S(2)}) async-start(f32[16,128,256]{2,1,0:T(8,128)} %broadcast_in_dim.1), calls=%async_computation.1 | async-start | bytes 4194304 | tf_op jit(solution)/shard_map/while/body/all_to_all | solution.py:78
  247.9 29.2 %all-to-all-done.1 = f32[16,128,256]{2,1,0:T(8,128)S(1)} async-done(((f32[16,128,256]{2,1,0:T(8,128)}), f32[16,128,256]{2,1,0:T(8,128)S(1)}, u32[]{:S(2)}, u32[]{:S(2)}) %all-to-all-start.1) | async-done | bytes 2097184 | tf_op jit(solution)/shard_map/while/body/all_to_all | solution.py:78
  277.5 10.5 %fusion.3 = (f32[1024]{0:T(1024)S(1)}, f32[1024,2048]{1,0:T(8,128)}) fusion(f32[2048]{0:T(1024)S(1)} %get-tuple-element.178, f32[1024,256]{1,0:T(8,128)S(1)} %bitcast.22, f32[2048,256]{1,0:T(8,128)S(1)} %bitcast.18, f32[2048]{0:T(1024)S(1)} %bitcast.27, f32[1024]{0:T(1024)S(1)} %add.22), kind=kOutput, calls=%fused_computation.16 | convolution fusion | flops 6455032832 | bytes 11558912 | tf_op jit(solution)/shard_map/while/body/dot_general | solution.py:38
  288.0 34.0 %pmax.24 = f32[1024]{0:T(1024)S(1)} all-reduce(f32[1024]{0:T(1024)S(1)} %get-tuple-element.155), channel_id=1, replica_groups=mesh['z_lo'=2,'x'=4,'core'=2,'y'=4,'z_hi'=4] {'y','z_hi'}, use_global_device_ids=true, to_apply=%region_5.0 | all-reduce | flops 1024 | bytes 8192 | tf_op jit(solution)/shard_map/while/body/pmax | solution.py:21
  326.5 33.4 %psum.42 = f32[1024]{0:T(1024)S(1)} all-reduce(f32[1024]{0:T(1024)S(1)} %exponential_reduce_fusion.3), channel_id=1, replica_groups=mesh['z_lo'=2,'x'=4,'core'=2,'y'=4,'z_hi'=4] {'y','z_hi'}, use_global_device_ids=true, to_apply=%region_7.0 | all-reduce | flops 1024 | bytes 8192 | tf_op jit(solution)/shard_map/while/body/psum | solution.py:22
  364.1 36.9 %pmax.25 = f32[2048]{0:T(1024)S(1)} all-reduce(f32[2048]{0:T(1024)S(1)} %fusion.4), channel_id=1, replica_groups=mesh['z_lo'=2,'x'=4,'core'=2,'y'=4,'z_hi'=4] {'z_lo','x','core'}, use_global_device_ids=true, to_apply=%region_9.0 | all-reduce | flops 2048 | bytes 16384 | tf_op jit(solution)/shard_map/while/body/pmax | solution.py:27
  405.6 27.8 %psum.43 = f32[2048]{0:T(1024)S(1)} all-reduce(f32[2048]{0:T(1024)S(1)} %exponential_reduce_fusion.2), channel_id=1, replica_groups=mesh['z_lo'=2,'x'=4,'core'=2,'y'=4,'z_hi'=4] {'z_lo','x','core'}, use_global_device_ids=true, to_apply=%region_11.0 | all-reduce | flops 2048 | bytes 16384 | tf_op jit(solution)/shard_map/while/body/psum | solution.py:28
  437.6 34.2 %pmax.26 = f32[1024]{0:T(1024)S(1)} all-reduce(f32[1024]{0:T(1024)S(1)} %fusion.5), channel_id=1, replica_groups=mesh['z_lo'=2,'x'=4,'core'=2,'y'=4,'z_hi'=4] {'y','z_hi'}, use_global_device_ids=true, to_apply=%region_13.0 | all-reduce | flops 1024 | bytes 8192 | tf_op jit(solution)/shard_map/while/body/pmax | solution.py:21
  476.3 33.4 %psum.44 = f32[1024]{0:T(1024)S(1)} all-reduce(f32[1024]{0:T(1024)S(1)} %exponential_reduce_fusion.1), channel_id=1, replica_groups=mesh['z_lo'=2,'x'=4,'core'=2,'y'=4,'z_hi'=4] {'y','z_hi'}, use_global_device_ids=true, to_apply=%region_15.0 | all-reduce | flops 1024 | bytes 8192 | tf_op jit(solution)/shard_map/while/body/psum | solution.py:22
  514.0 41.1 %pmax.27 = f32[2048]{0:T(1024)S(1)} all-reduce(f32[2048]{0:T(1024)S(1)} %fusion.6), channel_id=1, replica_groups=mesh['z_lo'=2,'x'=4,'core'=2,'y'=4,'z_hi'=4] {'z_lo','x','core'}, use_global_device_ids=true, to_apply=%region_17.0 | all-reduce | flops 2048 | bytes 16384 | tf_op jit(solution)/shard_map/while/body/pmax | solution.py:27
  559.6 27.7 %psum.45 = f32[2048]{0:T(1024)S(1)} all-reduce(f32[2048]{0:T(1024)S(1)} %exponential_reduce_fusion), channel_id=1, replica_groups=mesh['z_lo'=2,'x'=4,'core'=2,'y'=4,'z_hi'=4] {'z_lo','x','core'}, use_global_device_ids=true, to_apply=%region_19.0 | all-reduce | flops 2048 | bytes 16384 | tf_op jit(solution)/shard_map/while/body/psum | solution.py:28
  591.8 33.9 %psum.46 = f32[1024]{0:T(1024)S(1)} all-reduce(f32[1024]{0:T(1024)S(1)} %fusion), channel_id=1, replica_groups=mesh['z_lo'=2,'x'=4,'core'=2,'y'=4,'z_hi'=4] {'y','z_hi'}, use_global_device_ids=true, to_apply=%region_21.0 | all-reduce | flops 1024 | bytes 8192 | tf_op jit(solution)/shard_map/while/body/psum | solution.py:53
  630.3 34.9 %psum.47 = f32[2048]{0:T(1024)S(1)} all-reduce(f32[2048]{0:T(1024)S(1)} %fusion.1), channel_id=1, replica_groups=mesh['z_lo'=2,'x'=4,'core'=2,'y'=4,'z_hi'=4] {'z_lo','x','core'}, use_global_device_ids=true, to_apply=%region_23.0 | all-reduce | flops 2048 | bytes 16384 | tf_op jit(solution)/shard_map/while/body/psum | solution.py:57
  669.9 32.6 %psum.48 = f32[1024]{0:T(1024)S(1)} all-reduce(f32[1024]{0:T(1024)S(1)} %fusion.2), channel_id=1, replica_groups=mesh['z_lo'=2,'x'=4,'core'=2,'y'=4,'z_hi'=4] {'y','z_hi'}, use_global_device_ids=true, to_apply=%region_25.0 | all-reduce | flops 1024 | bytes 8192 | tf_op jit(solution)/shard_map/while/body/psum | solution.py:61
  702.5 10.7 %fusion.9 = (f32[2048]{0:T(1024)S(1)}, f32[1024]{0:T(1024)S(1)}, f32[1024,2048]{1,0:T(8,128)S(1)}) fusion(f32[1024]{0:T(1024)S(1)} %get-tuple-element.154, f32[1024,2048]{1,0:T(8,128)} %get-tuple-element.156, f32[2048]{0:T(1024)S(1)} %get-tuple-element.178, f32[1024]{0:T(1024)S(1)} %neg.5, f32[2048]{0:T(1024)S(1)} %get-tuple-element.152, ...), kind=kLoop, calls=%fused_computation.40 | loop fusion | flops 44037120 | bytes 16855040 | tf_op jit(solution)/shard_map/while/body/reduce_sum | solution.py:69
  716.4 7.7 fusion.8
  728.4 16.6 %fusion.7 = f32[2048,256]{1,0:T(8,128)} fusion(f32[1024,2048]{1,0:T(8,128)} %copy-done, f32[1024,256]{1,0:T(8,128)S(1)} %bitcast.24, f32[2048,256]{1,0:T(8,128)S(1)} %bitcast.20, f32[2048]{0:T(1024)S(1)} %get-tuple-element.134), kind=kOutput, calls=%fused_computation.21 | convolution fusion | flops 6444023808 | bytes 13639680 | tf_op jit(solution)/shard_map/while/body/dot_general | solution.py:68
  745.0 7.7 all-to-all-done.2
  752.7 12.4 %all-to-all-start.3 = ((f32[16,128,256]{2,1,0:T(8,128)}), f32[16,128,256]{2,1,0:T(8,128)S(1)}, u32[]{:S(2)}, u32[]{:S(2)}) async-start(f32[16,128,256]{2,1,0:T(8,128)} %bitcast.21), calls=%async_computation.3 | async-start | bytes 4194304 | tf_op jit(solution)/shard_map/while/body/all_to_all | solution.py:78
  767.0 27.2 %all-to-all-done.3 = f32[16,128,256]{2,1,0:T(8,128)S(1)} async-done(((f32[16,128,256]{2,1,0:T(8,128)}), f32[16,128,256]{2,1,0:T(8,128)S(1)}, u32[]{:S(2)}, u32[]{:S(2)}) %all-to-all-start.3) | async-done | bytes 2097184 | tf_op jit(solution)/shard_map/while/body/all_to_all | solution.py:78
  (94 shorter events, 132.9 us)
Async XLA Ops:
  0.6 16.4 %collective-permute-start.3 = (f32[128,256]{1,0:T(8,128)}, f32[128,256]{1,0:T(8,128)S(1)}, u32[]{:S(2)}, u32[]{:S(2)}) collective-permute-start(f32[128,256]{1,0:T(8,128)} %param.6), channel_id=1, source_target_pairs={{0,128},{128,0},{1,129},{129,1},{2,130},{130,2},{3,131},{131,3},{4... | collective-permute-start | bytes 393224 | tf_op jit(solution)/shard_map/ppermute | solution.py:319
  2.4 10.7 %collective-permute-start = (f32[64,256]{1,0:T(8,128)}, f32[64,256]{1,0:T(8,128)S(1)}, u32[]{:S(2)}, u32[]{:S(2)}) collective-permute-start(f32[64,256]{1,0:T(8,128)} %own.1), channel_id=1, source_target_pairs={{0,1},{1,2},{2,3},{3,0},{4,5},{5,6},{6,7},{7,4},{8,9},{9,10},{10,1... | collective-permute-start | bytes 196616 | tf_op jit(solution)/shard_map/ppermute | solution.py:319
  5.3 10.2 %collective-permute-start.1 = (f32[64,256]{1,0:T(8,128)}, f32[64,256]{1,0:T(8,128)S(1)}, u32[]{:S(2)}, u32[]{:S(2)}) collective-permute-start(f32[64,256]{1,0:T(8,128)} %own.1), channel_id=1, source_target_pairs={{0,2},{1,3},{2,0},{3,1},{4,6},{5,7},{6,4},{7,5},{8,10},{9,11},{10,... | collective-permute-start | bytes 196616 | tf_op jit(solution)/shard_map/ppermute | solution.py:319
  9.6 7.5 collective-permute-start.2
  17.9 7.8 collective-permute-start.4
  19.3 13.1 %collective-permute-start.5 = (f32[256,256]{1,0:T(8,128)S(1)}, f32[256,256]{1,0:T(8,128)S(1)}, u32[]{:S(2)}, u32[]{:S(2)}) collective-permute-start(f32[256,256]{1,0:T(8,128)S(1)} %constant_dynamic-update-slice_fusion.refs_0_), channel_id=1, source_target_pairs={{0,8},{4,12},{8,0},{12,4},{1,9},{5,13},{9,1},{13,5},{2,10},{6,14},... | collective-permute-start | bytes 786440 | tf_op jit(solution)/shard_map/ppermute | solution.py:319
  22.9 11.9 %collective-permute-start.7 = (f32[256,256]{1,0:T(8,128)S(1)}, f32[256,256]{1,0:T(8,128)S(1)}, u32[]{:S(2)}, u32[]{:S(2)}) collective-permute-start(f32[256,256]{1,0:T(8,128)S(1)} %constant_dynamic-update-slice_fusion.4.refs_4_), channel_id=1, source_target_pairs={{0,32},{32,64},{64,96},{96,0},{1,33},{33,65},{65,97},{97,1},{2,34}... | collective-permute-start | bytes 786440 | tf_op jit(solution)/shard_map/ppermute | solution.py:319
  23.1 11.7 %collective-permute-start.8 = (f32[256,256]{1,0:T(8,128)S(1)}, f32[256,256]{1,0:T(8,128)S(1)}, u32[]{:S(2)}, u32[]{:S(2)}) collective-permute-start(f32[256,256]{1,0:T(8,128)S(1)} %constant_dynamic-update-slice_fusion.4.refs_4_), channel_id=1, source_target_pairs={{0,64},{32,96},{64,0},{96,32},{1,65},{33,97},{65,1},{97,33},{2,66}... | collective-permute-start | bytes 786440 | tf_op jit(solution)/shard_map/ppermute | solution.py:319
  25.3 12.2 %collective-permute-start.9 = (f32[256,256]{1,0:T(8,128)S(1)}, f32[256,256]{1,0:T(8,128)S(1)}, u32[]{:S(2)}, u32[]{:S(2)}) collective-permute-start(f32[256,256]{1,0:T(8,128)S(1)} %constant_dynamic-update-slice_fusion.4.refs_4_), channel_id=1, source_target_pairs={{0,96},{32,0},{64,32},{96,64},{1,97},{33,1},{65,33},{97,65},{2,98}... | collective-permute-start | bytes 786440 | tf_op jit(solution)/shard_map/ppermute | solution.py:319
  25.7 13.6 %collective-permute-start.6 = (f32[256,256]{1,0:T(8,128)S(1)}, f32[256,256]{1,0:T(8,128)S(1)}, u32[]{:S(2)}, u32[]{:S(2)}) collective-permute-start(f32[256,256]{1,0:T(8,128)S(1)} %constant_dynamic-update-slice_fusion.refs_0_), channel_id=1, source_target_pairs={{0,12},{4,0},{8,4},{12,8},{1,13},{5,1},{9,5},{13,9},{2,14},{6,2},{... | collective-permute-start | bytes 786440 | tf_op jit(solution)/shard_map/ppermute | solution.py:319
  32.4 6.8 collective-permute-start.10
  34.8 4.5 collective-permute-start.11
  34.8 4.5 collective-permute-start.12
  37.5 2.9 collective-permute-start.13
  140.1 38.7 %copy-start.2 = (f32[64,256]{1,0:T(8,128)S(1)}, f32[64,256]{1,0:T(8,128)}, u32[]{:S(2)}) copy-start(f32[64,256]{1,0:T(8,128)} %own.1) | copy-start | bytes 196612
  140.1 39.5 %copy-start.1 = (f32[128,256]{1,0:T(8,128)S(1)}, f32[128,256]{1,0:T(8,128)}, u32[]{:S(2)}) copy-start(f32[128,256]{1,0:T(8,128)} %param.6) | copy-start | bytes 393220
  140.1 39.5 %copy-start.3 = (f32[2048]{0:T(1024)S(1)}, f32[2048]{0:T(1024)}, u32[]{:S(2)}) copy-start(f32[2048]{0:T(1024)} %param.7) | copy-start | bytes 24580
  144.4 3.7 collective-permute-start.20
  149.2 29.6 %all-to-all-start.11 = ((f32[8,128,256]{2,1,0:T(8,128)}), f32[8,128,256]{2,1,0:T(8,128)S(1)}, u32[]{:S(2)}, u32[]{:S(2)}) async-start(f32[8,128,256]{2,1,0:T(8,128)} %bitcast.11), calls=%async_computation.11 | async-start | bytes 2097152 | tf_op jit(solution)/shard_map/all_to_all | solution.py:78
  154.6 9.2 %collective-permute-start.14 = (f32[256,256]{1,0:T(8,128)S(1)}, f32[256,256]{1,0:T(8,128)S(1)}, u32[]{:S(2)}, u32[]{:S(2)}) collective-permute-start(f32[256,256]{1,0:T(8,128)S(1)} %get-tuple-element.117), channel_id=1, source_target_pairs={{0,4},{4,8},{8,12},{12,0},{1,5},{5,9},{9,13},{13,1},{2,6},{6,10},{... | collective-permute-start | bytes 786440 | tf_op jit(solution)/shard_map/ppermute | solution.py:319
  154.8 13.2 %collective-permute-start.15 = (f32[256,256]{1,0:T(8,128)S(1)}, f32[256,256]{1,0:T(8,128)S(1)}, u32[]{:S(2)}, u32[]{:S(2)}) collective-permute-start(f32[256,256]{1,0:T(8,128)S(1)} %get-tuple-element.118), channel_id=1, source_target_pairs={{0,8},{4,12},{8,0},{12,4},{1,9},{5,13},{9,1},{13,5},{2,10},{6,14},... | collective-permute-start | bytes 786440 | tf_op jit(solution)/shard_map/ppermute | solution.py:319
  157.0 12.5 %collective-permute-start.16 = (f32[256,256]{1,0:T(8,128)S(1)}, f32[256,256]{1,0:T(8,128)S(1)}, u32[]{:S(2)}, u32[]{:S(2)}) collective-permute-start(f32[256,256]{1,0:T(8,128)S(1)} %get-tuple-element.119), channel_id=1, source_target_pairs={{0,12},{4,0},{8,4},{12,8},{1,13},{5,1},{9,5},{13,9},{2,14},{6,2},{... | collective-permute-start | bytes 786440 | tf_op jit(solution)/shard_map/ppermute | solution.py:319
  170.1 6.4 collective-permute-start.17
  170.9 7.9 collective-permute-start.18
  173.0 5.8 collective-permute-start.19
  234.2 43.0 %all-to-all-start.1 = ((f32[16,128,256]{2,1,0:T(8,128)}), f32[16,128,256]{2,1,0:T(8,128)S(1)}, u32[]{:S(2)}, u32[]{:S(2)}) async-start(f32[16,128,256]{2,1,0:T(8,128)} %broadcast_in_dim.1), calls=%async_computation.1 | async-start | bytes 4194304 | tf_op jit(solution)/shard_map/while/body/all_to_all | solution.py:78
  713.2 3.2 copy-start
  724.1 28.6 %all-to-all-start.2 = ((f32[16,64,256]{2,1,0:T(8,128)}), f32[16,64,256]{2,1,0:T(8,128)}, u32[]{:S(2)}, u32[]{:S(2)}) async-start(f32[16,64,256]{2,1,0:T(8,128)} %bitcast.25), calls=%async_computation.2 | async-start | bytes 2097152 | tf_op jit(solution)/shard_map/while/body/all_to_all | solution.py:78
  752.7 41.5 %all-to-all-start.3 = ((f32[16,128,256]{2,1,0:T(8,128)}), f32[16,128,256]{2,1,0:T(8,128)S(1)}, u32[]{:S(2)}, u32[]{:S(2)}) async-start(f32[16,128,256]{2,1,0:T(8,128)} %bitcast.21), calls=%async_computation.3 | async-start | bytes 4194304 | tf_op jit(solution)/shard_map/while/body/all_to_all | solution.py:78

commit v6 on v5

--- a/solution.py
+++ b/solution.py
@@ -163,16 +163,6 @@
             pair = halves(source[rows, :])
             for k, which in enumerate(order):
                 wide[rows, k * features : (k + 1) * features] = pair[which]
-    largest = None
-    for cols in spans(targets.shape[0], 256):
-        dots = lax.dot_general(
-            doc_wide[...], target_wide[cols, :], (((1,), (1,)), ((), ())), preferred_element_type=f32
-        )
-        dots = dots * (2.0 / smoothing_epsilon)
-        tile[:, cols] = jnp.exp(dots)
-        peak = jnp.max(jnp.abs(dots).reshape(-1, 8, 256), axis=0)
-        largest = peak if largest is None else jnp.maximum(largest, peak)
-    fits = jnp.max(largest) <= EXPONENT_MAX
     norms = []
     for rows in spans(targets.shape[0], LANES):
         squares = targets[rows, :] * targets[rows, :]
@@ -180,6 +170,17 @@
     count = start.shape[0]
     begin = jnp.concatenate([start[i : i + 1, :] for c in range(2) for i in range(c, count, 2)], axis=0)
     weight = jnp.exp((begin - jnp.concatenate(norms, axis=0)) / smoothing_epsilon)
+    largest = None
+    for c, cols in enumerate(spans(targets.shape[0], 256)):
+        dots = lax.dot_general(
+            doc_wide[...], target_wide[cols, :], (((1,), (1,)), ((), ())), preferred_element_type=f32
+        )
+        dots = dots * (2.0 / smoothing_epsilon)
+        masses = jnp.exp(dots)
+        tile[:, cols] = masses
+        peak = jnp.max(jnp.abs(dots).reshape(-1, 8, 256), axis=0)
+        largest = peak if largest is None else jnp.maximum(largest, peak)
+    fits = jnp.max(largest) <= EXPONENT_MAX
     weight = jnp.where(fits, weight, jnp.nan)
     weight_out[...] = weight
     spread(part, row_sums(tile, weight))
@@ -219,7 +220,7 @@
 
 def kernel_docs(ratio, place, tile, parts, doc_one, doc_two, bar_two, target_zero, target_one, target_two, bar_one,
                 targets, top, low, mass, *refs):
-    pieces, (factors, wide) = refs[:-2], refs[-2:]
+    pieces, (factors, wide, sums) = refs[:-3], refs[-3:]
     features = targets.shape[1]
     for rows in spans(targets.shape[0], 256):
         pair = halves(targets[rows, :])
@@ -233,22 +234,28 @@
     for r, rows in enumerate(spans(tile.shape[0], LANES)):
         for k, values in enumerate(by_row):
             factors[k, rows, :] = upright(values[r : r + 1, :])
-    size = pieces[0].shape[0]
-    for k, piece in enumerate(pieces):
-        first = pl.multiple_of(turned(place[0], k, len(pieces)) * size, size)
-        for rows in spans(size, 32):
-            rows = pl.ds(first + rows.start, 32)
-            a = [factors[i, rows, :] for i in range(4)]
-            for c, cols in enumerate(columns):
-                b = [v[c : c + 1, :] for v in by_column]
-                adjoint = tile[rows, cols] * ((a[0] * b[0] + a[1] * b[1]) + (a[2] * b[2] + a[3] * b[3]))
-                term = jnp.sum(adjoint.reshape(-1, 8, LANES), axis=0)
-                acc[c] = term if acc[c] is None else acc[c] + term
-                top[rows, cols], low[rows, cols] = halves(adjoint)
-        block = pl.ds(first, size)
+
+    def form(rows):
+        a = [factors[i, rows, :] for i in range(4)]
+        for c, cols in enumerate(columns):
+            b = [v[c : c + 1, :] for v in by_column]
+            adjoint = tile[rows, cols] * ((a[0] * b[0] + a[1] * b[1]) + (a[2] * b[2] + a[3] * b[3]))
+            term = jnp.sum(adjoint.reshape(-1, 8, LANES), axis=0)
+            acc[c] = term if acc[c] is None else acc[c] + term
+            top[rows, cols], low[rows, cols] = halves(adjoint)
+
+    def multiply(block):
         both = jnp.dot(top[block, :], wide[...], preferred_element_type=f32)
         rest = jnp.dot(low[block, :], wide[:, :features], preferred_element_type=f32)
-        piece[...] = (both[:, :features] + both[:, features:]) + rest
+        sums[block, :] = (both[:, :features] + both[:, features:]) + rest
+
+    size = pieces[0].shape[0]
+    for block in spans(tile.shape[0], 256):
+        for rows in spans(256, 32):
+            form(slice(block.start + rows.start, block.start + rows.stop))
+        multiply(block)
+    for k, piece in enumerate(pieces):
+        piece[...] = sums[pl.ds(pl.multiple_of(turned(place[0], k, len(pieces)) * size, size), size), :]
     mass[...] = jnp.concatenate([jnp.sum(a, axis=0, keepdims=True) for a in acc], axis=0)
 
 
@@ -362,7 +369,7 @@
         partial(kernel_docs, ratio),
         (tile, swap(part, COL), doc_one, doc_two, bar_two, target_zero, target_one, target_two, bar_one, targets),
         [((n, m), bf16), ((n, m), bf16), target_vector] + [((n // SIZES["y"], features), f32)] * SIZES["y"],
-        [((4, n, LANES), f32), ((m, 2 * features), bf16)],
+        [((4, n, LANES), f32), ((m, 2 * features), bf16), ((n, features), f32)],
         limit=32, held=HELD, kept=(0, 1), flops=product, place=place,
     )
     doc_pieces = ring(doc_pieces, "y")

time: 804 us -> 802 us (level)
  no operation moved by 1% of the time
where the time goes in v6:
time: 802 us; the launch traced here: 795 us
  blocking collectives  483 us (60%)
  waiting for transfers between devices  93.4 us (12%)
  starting transfers between devices  68.8 us (9%)
  other arithmetic  59.1 us (7%)
  matrix products  34.8 us (4%)
  Pallas kernels  23.3 us (3%)
  loops' own time  22.3 us (3%)
    all_to_all x8, blocking collectives, swap(): return lax.all_to_all(blocks, axis, 0, 0)  113 us
    pmax x2, blocking collectives, column_log_mass(): largest = lax.pmax(jnp.max(scores, axis=0), ROW)  78.7 us
    pmax x2, blocking collectives, row_log_mass(): largest = lax.pmax(jnp.max(scores, axis=1), COL)  68.2 us
    psum x2, blocking collectives, row_log_mass(): lax.psum(jnp.sum(jnp.exp(scores - largest[:, None]), axis=1), COL)  65.9 us
    all_to_all x4, waiting for transfers between devices, swap(): return lax.all_to_all(blocks, axis, 0, 0)  64 us
    psum x2, blocking collectives, column_log_mass(): lax.psum(jnp.sum(jnp.exp(scores - largest[None, :]), axis=0), ROW)  55.4 us
    all_to_all x4, starting transfers between devices, swap(): return lax.all_to_all(blocks, axis, 0, 0)  35.5 us
    psum x1, blocking collectives, log_domain(): target_bar_one = -lax.psum(jnp.sum(weighted, axis=0), ROW)  34.9 us
  transfers between devices with their start and end apart: 25, of which 15 were waited for; matrix products, arithmetic and copies ran while one was open for 3% of the time, Pallas kernels for 0%

profile of v6, /device:TPU:7, one launch (start us, length us, event | category | flops | bytes accessed | tf_op | source)
XLA Modules:
  0.0 794.5 jit_solution(946012504125672659)
XLA Ops:
  40.3 5.5 shard_map.50
  45.8 14.5 %all_to_all.57.parts = f32[16,8,128]{2,1,0:T(8,128)S(1)} all-to-all(f32[16,8,128]{2,1,0:T(8,128)S(1)} %get-tuple-element.101), channel_id=1, replica_groups=mesh['z_lo'=2,'x'=4,'core'=2,'y'=4,'z_hi'=4] {'y','z_hi'}, dimensions={0} | all-to-all | bytes 131072 | tf_op jit(solution)/shard_map/all_to_all | solution.py:78
  61.0 10.8 %all_to_all.58.parts = f32[16,16,128]{2,1,0:T(8,128)S(1)} all-to-all(f32[16,16,128]{2,1,0:T(8,128)S(1)} %get-tuple-element.102), channel_id=1, replica_groups=mesh['z_lo'=2,'x'=4,'core'=2,'y'=4,'z_hi'=4] {'z_lo','x','core'}, dimensions={0} | all-to-all | bytes 262144 | tf_op jit(solution)/shard_map/all_to_all | solution.py:78
  72.4 11.8 %all_to_all.59.parts = f32[16,8,128]{2,1,0:T(8,128)S(1)} all-to-all(f32[16,8,128]{2,1,0:T(8,128)S(1)} %get-tuple-element.103), channel_id=1, replica_groups=mesh['z_lo'=2,'x'=4,'core'=2,'y'=4,'z_hi'=4] {'y','z_hi'}, dimensions={0} | all-to-all | bytes 131072 | tf_op jit(solution)/shard_map/all_to_all | solution.py:78
  84.9 10.3 %all_to_all.60.parts = f32[16,16,128]{2,1,0:T(8,128)S(1)} all-to-all(f32[16,16,128]{2,1,0:T(8,128)S(1)} %get-tuple-element.104), channel_id=1, replica_groups=mesh['z_lo'=2,'x'=4,'core'=2,'y'=4,'z_hi'=4] {'z_lo','x','core'}, dimensions={0} | all-to-all | bytes 262144 | tf_op jit(solution)/shard_map/all_to_all | solution.py:78
  95.8 11.8 %all_to_all.61.parts = f32[16,8,128]{2,1,0:T(8,128)S(1)} all-to-all(f32[16,8,128]{2,1,0:T(8,128)S(1)} %get-tuple-element.105), channel_id=1, replica_groups=mesh['z_lo'=2,'x'=4,'core'=2,'y'=4,'z_hi'=4] {'y','z_hi'}, dimensions={0} | all-to-all | bytes 131072 | tf_op jit(solution)/shard_map/all_to_all | solution.py:78
  108.3 10.4 %all_to_all.62.parts = f32[16,16,128]{2,1,0:T(8,128)S(1)} all-to-all(f32[16,16,128]{2,1,0:T(8,128)S(1)} %get-tuple-element.108), channel_id=1, replica_groups=mesh['z_lo'=2,'x'=4,'core'=2,'y'=4,'z_hi'=4] {'z_lo','x','core'}, dimensions={0} | all-to-all | bytes 262144 | tf_op jit(solution)/shard_map/all_to_all | solution.py:78
  119.3 12.2 %all_to_all.63.parts = f32[16,8,128]{2,1,0:T(8,128)S(1)} all-to-all(f32[16,8,128]{2,1,0:T(8,128)S(1)} %get-tuple-element.110), channel_id=1, replica_groups=mesh['z_lo'=2,'x'=4,'core'=2,'y'=4,'z_hi'=4] {'y','z_hi'}, dimensions={0} | all-to-all | bytes 131072 | tf_op jit(solution)/shard_map/all_to_all | solution.py:78
  131.5 7.2 shard_map.57
  156.2 6.3 collective-permute-done.14.refs_1_
  177.7 615.6 %while.11 = (pred[]{:T(512)}, f32[64,256]{1,0:T(8,128)}, f32[128,256]{1,0:T(8,128)}, f32[2048]{0:T(1024)S(1)}, f32[64,256]{1,0:T(8,128)S(1)}, /*index=5*/f32[128,256]{1,0:T(8,128)S(1)}) while((pred[]{:T(512)}, f32[64,256]{1,0:T(8,128)}, f32[128,256]{1,0:T(8,128)}, f32[2048]{0:T(1024)S(1)}, f32[64,256]{1,0:T(8,128)S(1)}, ...), condition=%region_30.0_spmd, body=%region_1.0_spmd | while | flops 19470446592 | bytes 200188080 | solution.py:387
  199.8 31.3 %all_to_all.56 = f32[16,64,256]{2,1,0:T(8,128)S(1)} all-to-all(f32[16,64,256]{2,1,0:T(8,128)S(1)} %broadcast_in_dim.0), channel_id=1, replica_groups=mesh['z_lo'=2,'x'=4,'core'=2,'y'=4,'z_hi'=4] {'y','z_hi'}, dimensions={0} | all-to-all | bytes 2097152 | tf_op jit(solution)/shard_map/while/body/all_to_all | solution.py:78
  232.6 13.4 %all-to-all-start.1 = ((f32[16,128,256]{2,1,0:T(8,128)}), f32[16,128,256]{2,1,0:T(8,128)S(1)}, u32[]{:S(2)}, u32[]{:S(2)}) async-start(f32[16,128,256]{2,1,0:T(8,128)} %broadcast_in_dim.1), calls=%async_computation.1 | async-start | bytes 4194304 | tf_op jit(solution)/shard_map/while/body/all_to_all | solution.py:78
  246.3 29.2 %all-to-all-done.1 = f32[16,128,256]{2,1,0:T(8,128)S(1)} async-done(((f32[16,128,256]{2,1,0:T(8,128)}), f32[16,128,256]{2,1,0:T(8,128)S(1)}, u32[]{:S(2)}, u32[]{:S(2)}) %all-to-all-start.1) | async-done | bytes 2097184 | tf_op jit(solution)/shard_map/while/body/all_to_all | solution.py:78
  275.8 10.5 %fusion.3 = (f32[1024]{0:T(1024)S(1)}, f32[1024,2048]{1,0:T(8,128)}) fusion(f32[2048]{0:T(1024)S(1)} %get-tuple-element.178, f32[1024,256]{1,0:T(8,128)S(1)} %bitcast.22, f32[2048,256]{1,0:T(8,128)S(1)} %bitcast.18, f32[2048]{0:T(1024)S(1)} %bitcast.27, f32[1024]{0:T(1024)S(1)} %add.22), kind=kOutput, calls=%fused_computation.16 | convolution fusion | flops 6455032832 | bytes 11558912 | tf_op jit(solution)/shard_map/while/body/dot_general | solution.py:38
  286.3 34.0 %pmax.24 = f32[1024]{0:T(1024)S(1)} all-reduce(f32[1024]{0:T(1024)S(1)} %get-tuple-element.155), channel_id=1, replica_groups=mesh['z_lo'=2,'x'=4,'core'=2,'y'=4,'z_hi'=4] {'y','z_hi'}, use_global_device_ids=true, to_apply=%region_5.0 | all-reduce | flops 1024 | bytes 8192 | tf_op jit(solution)/shard_map/while/body/pmax | solution.py:21
  324.8 33.3 %psum.42 = f32[1024]{0:T(1024)S(1)} all-reduce(f32[1024]{0:T(1024)S(1)} %exponential_reduce_fusion.3), channel_id=1, replica_groups=mesh['z_lo'=2,'x'=4,'core'=2,'y'=4,'z_hi'=4] {'y','z_hi'}, use_global_device_ids=true, to_apply=%region_7.0 | all-reduce | flops 1024 | bytes 8192 | tf_op jit(solution)/shard_map/while/body/psum | solution.py:22
  362.4 36.9 %pmax.25 = f32[2048]{0:T(1024)S(1)} all-reduce(f32[2048]{0:T(1024)S(1)} %fusion.4), channel_id=1, replica_groups=mesh['z_lo'=2,'x'=4,'core'=2,'y'=4,'z_hi'=4] {'z_lo','x','core'}, use_global_device_ids=true, to_apply=%region_9.0 | all-reduce | flops 2048 | bytes 16384 | tf_op jit(solution)/shard_map/while/body/pmax | solution.py:27
  403.8 27.8 %psum.43 = f32[2048]{0:T(1024)S(1)} all-reduce(f32[2048]{0:T(1024)S(1)} %exponential_reduce_fusion.2), channel_id=1, replica_groups=mesh['z_lo'=2,'x'=4,'core'=2,'y'=4,'z_hi'=4] {'z_lo','x','core'}, use_global_device_ids=true, to_apply=%region_11.0 | all-reduce | flops 2048 | bytes 16384 | tf_op jit(solution)/shard_map/while/body/psum | solution.py:28
  435.9 34.3 %pmax.26 = f32[1024]{0:T(1024)S(1)} all-reduce(f32[1024]{0:T(1024)S(1)} %fusion.5), channel_id=1, replica_groups=mesh['z_lo'=2,'x'=4,'core'=2,'y'=4,'z_hi'=4] {'y','z_hi'}, use_global_device_ids=true, to_apply=%region_13.0 | all-reduce | flops 1024 | bytes 8192 | tf_op jit(solution)/shard_map/while/body/pmax | solution.py:21
  474.6 32.6 %psum.44 = f32[1024]{0:T(1024)S(1)} all-reduce(f32[1024]{0:T(1024)S(1)} %exponential_reduce_fusion.1), channel_id=1, replica_groups=mesh['z_lo'=2,'x'=4,'core'=2,'y'=4,'z_hi'=4] {'y','z_hi'}, use_global_device_ids=true, to_apply=%region_15.0 | all-reduce | flops 1024 | bytes 8192 | tf_op jit(solution)/shard_map/while/body/psum | solution.py:22
  511.5 41.8 %pmax.27 = f32[2048]{0:T(1024)S(1)} all-reduce(f32[2048]{0:T(1024)S(1)} %fusion.6), channel_id=1, replica_groups=mesh['z_lo'=2,'x'=4,'core'=2,'y'=4,'z_hi'=4] {'z_lo','x','core'}, use_global_device_ids=true, to_apply=%region_17.0 | all-reduce | flops 2048 | bytes 16384 | tf_op jit(solution)/shard_map/while/body/pmax | solution.py:27
  557.9 27.7 %psum.45 = f32[2048]{0:T(1024)S(1)} all-reduce(f32[2048]{0:T(1024)S(1)} %exponential_reduce_fusion), channel_id=1, replica_groups=mesh['z_lo'=2,'x'=4,'core'=2,'y'=4,'z_hi'=4] {'z_lo','x','core'}, use_global_device_ids=true, to_apply=%region_19.0 | all-reduce | flops 2048 | bytes 16384 | tf_op jit(solution)/shard_map/while/body/psum | solution.py:28
  590.1 34.0 %psum.46 = f32[1024]{0:T(1024)S(1)} all-reduce(f32[1024]{0:T(1024)S(1)} %fusion), channel_id=1, replica_groups=mesh['z_lo'=2,'x'=4,'core'=2,'y'=4,'z_hi'=4] {'y','z_hi'}, use_global_device_ids=true, to_apply=%region_21.0 | all-reduce | flops 1024 | bytes 8192 | tf_op jit(solution)/shard_map/while/body/psum | solution.py:53
  628.6 34.9 %psum.47 = f32[2048]{0:T(1024)S(1)} all-reduce(f32[2048]{0:T(1024)S(1)} %fusion.1), channel_id=1, replica_groups=mesh['z_lo'=2,'x'=4,'core'=2,'y'=4,'z_hi'=4] {'z_lo','x','core'}, use_global_device_ids=true, to_apply=%region_23.0 | all-reduce | flops 2048 | bytes 16384 | tf_op jit(solution)/shard_map/while/body/psum | solution.py:57
  668.1 32.6 %psum.48 = f32[1024]{0:T(1024)S(1)} all-reduce(f32[1024]{0:T(1024)S(1)} %fusion.2), channel_id=1, replica_groups=mesh['z_lo'=2,'x'=4,'core'=2,'y'=4,'z_hi'=4] {'y','z_hi'}, use_global_device_ids=true, to_apply=%region_25.0 | all-reduce | flops 1024 | bytes 8192 | tf_op jit(solution)/shard_map/while/body/psum | solution.py:61
  700.8 10.7 %fusion.9 = (f32[2048]{0:T(1024)S(1)}, f32[1024]{0:T(1024)S(1)}, f32[1024,2048]{1,0:T(8,128)S(1)}) fusion(f32[1024]{0:T(1024)S(1)} %get-tuple-element.154, f32[1024,2048]{1,0:T(8,128)} %get-tuple-element.156, f32[2048]{0:T(1024)S(1)} %get-tuple-element.178, f32[1024]{0:T(1024)S(1)} %neg.5, f32[2048]{0:T(1024)S(1)} %get-tuple-element.152, ...), kind=kLoop, calls=%fused_computation.40 | loop fusion | flops 44037120 | bytes 16855040 | tf_op jit(solution)/shard_map/while/body/reduce_sum | solution.py:69
  714.7 7.7 fusion.8
  726.7 16.6 %fusion.7 = f32[2048,256]{1,0:T(8,128)} fusion(f32[1024,2048]{1,0:T(8,128)} %copy-done, f32[1024,256]{1,0:T(8,128)S(1)} %bitcast.24, f32[2048,256]{1,0:T(8,128)S(1)} %bitcast.20, f32[2048]{0:T(1024)S(1)} %get-tuple-element.134), kind=kOutput, calls=%fused_computation.21 | convolution fusion | flops 6444023808 | bytes 13639680 | tf_op jit(solution)/shard_map/while/body/dot_general | solution.py:68
  743.3 7.6 all-to-all-done.2
  750.9 12.3 %all-to-all-start.3 = ((f32[16,128,256]{2,1,0:T(8,128)}), f32[16,128,256]{2,1,0:T(8,128)S(1)}, u32[]{:S(2)}, u32[]{:S(2)}) async-start(f32[16,128,256]{2,1,0:T(8,128)} %bitcast.21), calls=%async_computation.3 | async-start | bytes 4194304 | tf_op jit(solution)/shard_map/while/body/all_to_all | solution.py:78
  765.1 27.2 %all-to-all-done.3 = f32[16,128,256]{2,1,0:T(8,128)S(1)} async-done(((f32[16,128,256]{2,1,0:T(8,128)}), f32[16,128,256]{2,1,0:T(8,128)S(1)}, u32[]{:S(2)}, u32[]{:S(2)}) %all-to-all-start.3) | async-done | bytes 2097184 | tf_op jit(solution)/shard_map/while/body/all_to_all | solution.py:78
  (94 shorter events, 132.0 us)
Async XLA Ops:
  0.6 16.4 %collective-permute-start.3 = (f32[128,256]{1,0:T(8,128)}, f32[128,256]{1,0:T(8,128)S(1)}, u32[]{:S(2)}, u32[]{:S(2)}) collective-permute-start(f32[128,256]{1,0:T(8,128)} %param.6), channel_id=1, source_target_pairs={{0,128},{128,0},{1,129},{129,1},{2,130},{130,2},{3,131},{131,3},{4... | collective-permute-start | bytes 393224 | tf_op jit(solution)/shard_map/ppermute | solution.py:326
  2.4 10.7 %collective-permute-start = (f32[64,256]{1,0:T(8,128)}, f32[64,256]{1,0:T(8,128)S(1)}, u32[]{:S(2)}, u32[]{:S(2)}) collective-permute-start(f32[64,256]{1,0:T(8,128)} %own.1), channel_id=1, source_target_pairs={{0,1},{1,2},{2,3},{3,0},{4,5},{5,6},{6,7},{7,4},{8,9},{9,10},{10,1... | collective-permute-start | bytes 196616 | tf_op jit(solution)/shard_map/ppermute | solution.py:326
  5.3 10.2 %collective-permute-start.1 = (f32[64,256]{1,0:T(8,128)}, f32[64,256]{1,0:T(8,128)S(1)}, u32[]{:S(2)}, u32[]{:S(2)}) collective-permute-start(f32[64,256]{1,0:T(8,128)} %own.1), channel_id=1, source_target_pairs={{0,2},{1,3},{2,0},{3,1},{4,6},{5,7},{6,4},{7,5},{8,10},{9,11},{10,... | collective-permute-start | bytes 196616 | tf_op jit(solution)/shard_map/ppermute | solution.py:326
  9.6 7.5 collective-permute-start.2
  17.9 7.8 collective-permute-start.4
  19.3 13.1 %collective-permute-start.5 = (f32[256,256]{1,0:T(8,128)S(1)}, f32[256,256]{1,0:T(8,128)S(1)}, u32[]{:S(2)}, u32[]{:S(2)}) collective-permute-start(f32[256,256]{1,0:T(8,128)S(1)} %constant_dynamic-update-slice_fusion.refs_0_), channel_id=1, source_target_pairs={{0,8},{4,12},{8,0},{12,4},{1,9},{5,13},{9,1},{13,5},{2,10},{6,14},... | collective-permute-start | bytes 786440 | tf_op jit(solution)/shard_map/ppermute | solution.py:326
  22.9 11.9 %collective-permute-start.7 = (f32[256,256]{1,0:T(8,128)S(1)}, f32[256,256]{1,0:T(8,128)S(1)}, u32[]{:S(2)}, u32[]{:S(2)}) collective-permute-start(f32[256,256]{1,0:T(8,128)S(1)} %constant_dynamic-update-slice_fusion.4.refs_4_), channel_id=1, source_target_pairs={{0,32},{32,64},{64,96},{96,0},{1,33},{33,65},{65,97},{97,1},{2,34}... | collective-permute-start | bytes 786440 | tf_op jit(solution)/shard_map/ppermute | solution.py:326
  23.1 11.7 %collective-permute-start.8 = (f32[256,256]{1,0:T(8,128)S(1)}, f32[256,256]{1,0:T(8,128)S(1)}, u32[]{:S(2)}, u32[]{:S(2)}) collective-permute-start(f32[256,256]{1,0:T(8,128)S(1)} %constant_dynamic-update-slice_fusion.4.refs_4_), channel_id=1, source_target_pairs={{0,64},{32,96},{64,0},{96,32},{1,65},{33,97},{65,1},{97,33},{2,66}... | collective-permute-start | bytes 786440 | tf_op jit(solution)/shard_map/ppermute | solution.py:326
  25.3 12.2 %collective-permute-start.9 = (f32[256,256]{1,0:T(8,128)S(1)}, f32[256,256]{1,0:T(8,128)S(1)}, u32[]{:S(2)}, u32[]{:S(2)}) collective-permute-start(f32[256,256]{1,0:T(8,128)S(1)} %constant_dynamic-update-slice_fusion.4.refs_4_), channel_id=1, source_target_pairs={{0,96},{32,0},{64,32},{96,64},{1,97},{33,1},{65,33},{97,65},{2,98}... | collective-permute-start | bytes 786440 | tf_op jit(solution)/shard_map/ppermute | solution.py:326
  25.7 13.6 %collective-permute-start.6 = (f32[256,256]{1,0:T(8,128)S(1)}, f32[256,256]{1,0:T(8,128)S(1)}, u32[]{:S(2)}, u32[]{:S(2)}) collective-permute-start(f32[256,256]{1,0:T(8,128)S(1)} %constant_dynamic-update-slice_fusion.refs_0_), channel_id=1, source_target_pairs={{0,12},{4,0},{8,4},{12,8},{1,13},{5,1},{9,5},{13,9},{2,14},{6,2},{... | collective-permute-start | bytes 786440 | tf_op jit(solution)/shard_map/ppermute | solution.py:326
  32.4 6.8 collective-permute-start.10
  34.8 4.5 collective-permute-start.11
  34.8 4.5 collective-permute-start.12
  37.5 2.9 collective-permute-start.13
  138.7 38.3 %copy-start.2 = (f32[64,256]{1,0:T(8,128)S(1)}, f32[64,256]{1,0:T(8,128)}, u32[]{:S(2)}) copy-start(f32[64,256]{1,0:T(8,128)} %own.1) | copy-start | bytes 196612
  138.7 39.0 %copy-start.1 = (f32[128,256]{1,0:T(8,128)S(1)}, f32[128,256]{1,0:T(8,128)}, u32[]{:S(2)}) copy-start(f32[128,256]{1,0:T(8,128)} %param.6) | copy-start | bytes 393220
  138.8 39.0 %copy-start.3 = (f32[2048]{0:T(1024)S(1)}, f32[2048]{0:T(1024)}, u32[]{:S(2)}) copy-start(f32[2048]{0:T(1024)} %param.7) | copy-start | bytes 24580
  143.0 3.7 collective-permute-start.20
  147.9 29.1 %all-to-all-start.11 = ((f32[8,128,256]{2,1,0:T(8,128)}), f32[8,128,256]{2,1,0:T(8,128)S(1)}, u32[]{:S(2)}, u32[]{:S(2)}) async-start(f32[8,128,256]{2,1,0:T(8,128)} %bitcast.11), calls=%async_computation.11 | async-start | bytes 2097152 | tf_op jit(solution)/shard_map/all_to_all | solution.py:78
  153.3 9.1 %collective-permute-start.14 = (f32[256,256]{1,0:T(8,128)S(1)}, f32[256,256]{1,0:T(8,128)S(1)}, u32[]{:S(2)}, u32[]{:S(2)}) collective-permute-start(f32[256,256]{1,0:T(8,128)S(1)} %get-tuple-element.117), channel_id=1, source_target_pairs={{0,4},{4,8},{8,12},{12,0},{1,5},{5,9},{9,13},{13,1},{2,6},{6,10},{... | collective-permute-start | bytes 786440 | tf_op jit(solution)/shard_map/ppermute | solution.py:326
  153.4 13.2 %collective-permute-start.15 = (f32[256,256]{1,0:T(8,128)S(1)}, f32[256,256]{1,0:T(8,128)S(1)}, u32[]{:S(2)}, u32[]{:S(2)}) collective-permute-start(f32[256,256]{1,0:T(8,128)S(1)} %get-tuple-element.118), channel_id=1, source_target_pairs={{0,8},{4,12},{8,0},{12,4},{1,9},{5,13},{9,1},{13,5},{2,10},{6,14},... | collective-permute-start | bytes 786440 | tf_op jit(solution)/shard_map/ppermute | solution.py:326
  155.2 12.5 %collective-permute-start.16 = (f32[256,256]{1,0:T(8,128)S(1)}, f32[256,256]{1,0:T(8,128)S(1)}, u32[]{:S(2)}, u32[]{:S(2)}) collective-permute-start(f32[256,256]{1,0:T(8,128)S(1)} %get-tuple-element.119), channel_id=1, source_target_pairs={{0,12},{4,0},{8,4},{12,8},{1,13},{5,1},{9,5},{13,9},{2,14},{6,2},{... | collective-permute-start | bytes 786440 | tf_op jit(solution)/shard_map/ppermute | solution.py:326
  168.3 6.3 collective-permute-start.17
  169.1 7.8 collective-permute-start.18
  171.2 5.8 collective-permute-start.19
  232.6 42.9 %all-to-all-start.1 = ((f32[16,128,256]{2,1,0:T(8,128)}), f32[16,128,256]{2,1,0:T(8,128)S(1)}, u32[]{:S(2)}, u32[]{:S(2)}) async-start(f32[16,128,256]{2,1,0:T(8,128)} %broadcast_in_dim.1), calls=%async_computation.1 | async-start | bytes 4194304 | tf_op jit(solution)/shard_map/while/body/all_to_all | solution.py:78
  711.5 3.2 copy-start
  722.3 28.5 %all-to-all-start.2 = ((f32[16,64,256]{2,1,0:T(8,128)}), f32[16,64,256]{2,1,0:T(8,128)}, u32[]{:S(2)}, u32[]{:S(2)}) async-start(f32[16,64,256]{2,1,0:T(8,128)} %bitcast.25), calls=%async_computation.2 | async-start | bytes 2097152 | tf_op jit(solution)/shard_map/while/body/all_to_all | solution.py:78
  750.9 41.5 %all-to-all-start.3 = ((f32[16,128,256]{2,1,0:T(8,128)}), f32[16,128,256]{2,1,0:T(8,128)S(1)}, u32[]{:S(2)}, u32[]{:S(2)}) async-start(f32[16,128,256]{2,1,0:T(8,128)} %bitcast.21), calls=%async_computation.3 | async-start | bytes 4194304 | tf_op jit(solution)/shard_map/while/body/all_to_all | solution.py:78

commit v7 on v6

--- a/solution.py
+++ b/solution.py
@@ -334,9 +334,7 @@
 def local(embed_docs, embed_targets, start):
     rows, cols = lax.axis_size(ROW), lax.axis_size(COL)
     place = jnp.stack([lax.axis_index(a) for a in ("y", "z_hi", "core", "x", "z_lo")]).astype(jnp.int32)
-    near, beside = lax.optimization_barrier(
-        (ring([embed_docs] * SIZES["z_hi"], "z_hi"), ring([embed_targets] * SIZES["z_lo"], "z_lo"))
-    )
+    near, beside = ring([embed_docs] * SIZES["z_hi"], "z_hi"), ring([embed_targets] * SIZES["z_lo"], "z_lo")
     mine = ring([jnp.concatenate(beside, axis=0)] * SIZES["x"], "x")
     doc_pieces = ring([jnp.concatenate(near, axis=0)] * SIZES["y"], "y")
     other = [other_core(block) for block in mine]

time: 802 us -> 800 us (level)
  transfers between devices with their start and end apart: 25 -> 25, of which waited for: 15 -> 13; matrix products, arithmetic and copies ran while one was open for 3% -> 3% of each run, Pallas kernels for 0% -> 0%
where the time goes in v7:
time: 800 us; the launch traced here: 792 us
  blocking collectives  483 us (60%)
  waiting for transfers between devices  93.9 us (12%)
  starting transfers between devices  66 us (8%)
  other arithmetic  59.1 us (7%)
  matrix products  34.8 us (4%)
  Pallas kernels  23.3 us (3%)
  loops' own time  22.3 us (3%)
    all_to_all x8, blocking collectives, swap(): return lax.all_to_all(blocks, axis, 0, 0)  113 us
    pmax x2, blocking collectives, column_log_mass(): largest = lax.pmax(jnp.max(scores, axis=0), ROW)  78.7 us
    pmax x2, blocking collectives, row_log_mass(): largest = lax.pmax(jnp.max(scores, axis=1), COL)  68.2 us
    psum x2, blocking collectives, row_log_mass(): lax.psum(jnp.sum(jnp.exp(scores - largest[:, None]), axis=1), COL)  66 us
    all_to_all x4, waiting for transfers between devices, swap(): return lax.all_to_all(blocks, axis, 0, 0)  64 us
    psum x2, blocking collectives, column_log_mass(): lax.psum(jnp.sum(jnp.exp(scores - largest[None, :]), axis=0), ROW)  55.4 us
    all_to_all x4, starting transfers between devices, swap(): return lax.all_to_all(blocks, axis, 0, 0)  35.5 us
    psum x1, blocking collectives, log_domain(): target_bar_one = -lax.psum(jnp.sum(weighted, axis=0), ROW)  34.9 us
  transfers between devices with their start and end apart: 25, of which 13 were waited for; matrix products, arithmetic and copies ran while one was open for 3% of the time, Pallas kernels for 0%

profile of v7, /device:TPU:7, one launch (start us, length us, event | category | flops | bytes accessed | tf_op | source)
XLA Modules:
  0.0 792.2 jit_solution(4602644747176032266)
XLA Ops:
  38.0 5.5 shard_map.50
  43.5 13.8 %all_to_all.57.parts = f32[16,8,128]{2,1,0:T(8,128)S(1)} all-to-all(f32[16,8,128]{2,1,0:T(8,128)S(1)} %get-tuple-element.89), channel_id=1, replica_groups=mesh['z_lo'=2,'x'=4,'core'=2,'y'=4,'z_hi'=4] {'y','z_hi'}, dimensions={0} | all-to-all | bytes 131072 | tf_op jit(solution)/shard_map/all_to_all | solution.py:78
  57.9 11.5 %all_to_all.58.parts = f32[16,16,128]{2,1,0:T(8,128)S(1)} all-to-all(f32[16,16,128]{2,1,0:T(8,128)S(1)} %get-tuple-element.90), channel_id=1, replica_groups=mesh['z_lo'=2,'x'=4,'core'=2,'y'=4,'z_hi'=4] {'z_lo','x','core'}, dimensions={0} | all-to-all | bytes 262144 | tf_op jit(solution)/shard_map/all_to_all | solution.py:78
  70.0 11.8 %all_to_all.59.parts = f32[16,8,128]{2,1,0:T(8,128)S(1)} all-to-all(f32[16,8,128]{2,1,0:T(8,128)S(1)} %get-tuple-element.91), channel_id=1, replica_groups=mesh['z_lo'=2,'x'=4,'core'=2,'y'=4,'z_hi'=4] {'y','z_hi'}, dimensions={0} | all-to-all | bytes 131072 | tf_op jit(solution)/shard_map/all_to_all | solution.py:78
  82.5 10.3 %all_to_all.60.parts = f32[16,16,128]{2,1,0:T(8,128)S(1)} all-to-all(f32[16,16,128]{2,1,0:T(8,128)S(1)} %get-tuple-element.92), channel_id=1, replica_groups=mesh['z_lo'=2,'x'=4,'core'=2,'y'=4,'z_hi'=4] {'z_lo','x','core'}, dimensions={0} | all-to-all | bytes 262144 | tf_op jit(solution)/shard_map/all_to_all | solution.py:78
  93.4 11.8 %all_to_all.61.parts = f32[16,8,128]{2,1,0:T(8,128)S(1)} all-to-all(f32[16,8,128]{2,1,0:T(8,128)S(1)} %get-tuple-element.93), channel_id=1, replica_groups=mesh['z_lo'=2,'x'=4,'core'=2,'y'=4,'z_hi'=4] {'y','z_hi'}, dimensions={0} | all-to-all | bytes 131072 | tf_op jit(solution)/shard_map/all_to_all | solution.py:78
  105.9 10.4 %all_to_all.62.parts = f32[16,16,128]{2,1,0:T(8,128)S(1)} all-to-all(f32[16,16,128]{2,1,0:T(8,128)S(1)} %get-tuple-element.96), channel_id=1, replica_groups=mesh['z_lo'=2,'x'=4,'core'=2,'y'=4,'z_hi'=4] {'z_lo','x','core'}, dimensions={0} | all-to-all | bytes 262144 | tf_op jit(solution)/shard_map/all_to_all | solution.py:78
  117.0 12.2 %all_to_all.63.parts = f32[16,8,128]{2,1,0:T(8,128)S(1)} all-to-all(f32[16,8,128]{2,1,0:T(8,128)S(1)} %get-tuple-element.98), channel_id=1, replica_groups=mesh['z_lo'=2,'x'=4,'core'=2,'y'=4,'z_hi'=4] {'y','z_hi'}, dimensions={0} | all-to-all | bytes 131072 | tf_op jit(solution)/shard_map/all_to_all | solution.py:78
  129.1 7.2 shard_map.57
  153.8 6.3 collective-permute-done.14.refs_1_
  175.4 615.6 %while.11 = (pred[]{:T(512)}, f32[64,256]{1,0:T(8,128)}, f32[128,256]{1,0:T(8,128)}, f32[2048]{0:T(1024)S(1)}, f32[64,256]{1,0:T(8,128)S(1)}, /*index=5*/f32[128,256]{1,0:T(8,128)S(1)}) while((pred[]{:T(512)}, f32[64,256]{1,0:T(8,128)}, f32[128,256]{1,0:T(8,128)}, f32[2048]{0:T(1024)S(1)}, f32[64,256]{1,0:T(8,128)S(1)}, ...), condition=%region_30.0_spmd, body=%region_1.0_spmd | while | flops 19470446592 | bytes 200188080 | solution.py:385
  197.4 31.3 %all_to_all.56 = f32[16,64,256]{2,1,0:T(8,128)S(1)} all-to-all(f32[16,64,256]{2,1,0:T(8,128)S(1)} %broadcast_in_dim.0), channel_id=1, replica_groups=mesh['z_lo'=2,'x'=4,'core'=2,'y'=4,'z_hi'=4] {'y','z_hi'}, dimensions={0} | all-to-all | bytes 2097152 | tf_op jit(solution)/shard_map/while/body/all_to_all | solution.py:78
  230.2 13.4 %all-to-all-start.1 = ((f32[16,128,256]{2,1,0:T(8,128)}), f32[16,128,256]{2,1,0:T(8,128)S(1)}, u32[]{:S(2)}, u32[]{:S(2)}) async-start(f32[16,128,256]{2,1,0:T(8,128)} %broadcast_in_dim.1), calls=%async_computation.1 | async-start | bytes 4194304 | tf_op jit(solution)/shard_map/while/body/all_to_all | solution.py:78
  243.9 29.2 %all-to-all-done.1 = f32[16,128,256]{2,1,0:T(8,128)S(1)} async-done(((f32[16,128,256]{2,1,0:T(8,128)}), f32[16,128,256]{2,1,0:T(8,128)S(1)}, u32[]{:S(2)}, u32[]{:S(2)}) %all-to-all-start.1) | async-done | bytes 2097184 | tf_op jit(solution)/shard_map/while/body/all_to_all | solution.py:78
  273.5 10.5 %fusion.3 = (f32[1024]{0:T(1024)S(1)}, f32[1024,2048]{1,0:T(8,128)}) fusion(f32[2048]{0:T(1024)S(1)} %get-tuple-element.166, f32[1024,256]{1,0:T(8,128)S(1)} %bitcast.22, f32[2048,256]{1,0:T(8,128)S(1)} %bitcast.18, f32[2048]{0:T(1024)S(1)} %bitcast.27, f32[1024]{0:T(1024)S(1)} %add.22), kind=kOutput, calls=%fused_computation.16 | convolution fusion | flops 6455032832 | bytes 11558912 | tf_op jit(solution)/shard_map/while/body/dot_general | solution.py:38
  284.0 34.0 %pmax.24 = f32[1024]{0:T(1024)S(1)} all-reduce(f32[1024]{0:T(1024)S(1)} %get-tuple-element.143), channel_id=1, replica_groups=mesh['z_lo'=2,'x'=4,'core'=2,'y'=4,'z_hi'=4] {'y','z_hi'}, use_global_device_ids=true, to_apply=%region_5.0 | all-reduce | flops 1024 | bytes 8192 | tf_op jit(solution)/shard_map/while/body/pmax | solution.py:21
  322.4 33.3 %psum.42 = f32[1024]{0:T(1024)S(1)} all-reduce(f32[1024]{0:T(1024)S(1)} %exponential_reduce_fusion.3), channel_id=1, replica_groups=mesh['z_lo'=2,'x'=4,'core'=2,'y'=4,'z_hi'=4] {'y','z_hi'}, use_global_device_ids=true, to_apply=%region_7.0 | all-reduce | flops 1024 | bytes 8192 | tf_op jit(solution)/shard_map/while/body/psum | solution.py:22
  360.1 36.9 %pmax.25 = f32[2048]{0:T(1024)S(1)} all-reduce(f32[2048]{0:T(1024)S(1)} %fusion.4), channel_id=1, replica_groups=mesh['z_lo'=2,'x'=4,'core'=2,'y'=4,'z_hi'=4] {'z_lo','x','core'}, use_global_device_ids=true, to_apply=%region_9.0 | all-reduce | flops 2048 | bytes 16384 | tf_op jit(solution)/shard_map/while/body/pmax | solution.py:27
  401.5 27.8 %psum.43 = f32[2048]{0:T(1024)S(1)} all-reduce(f32[2048]{0:T(1024)S(1)} %exponential_reduce_fusion.2), channel_id=1, replica_groups=mesh['z_lo'=2,'x'=4,'core'=2,'y'=4,'z_hi'=4] {'z_lo','x','core'}, use_global_device_ids=true, to_apply=%region_11.0 | all-reduce | flops 2048 | bytes 16384 | tf_op jit(solution)/shard_map/while/body/psum | solution.py:28
  433.5 34.3 %pmax.26 = f32[1024]{0:T(1024)S(1)} all-reduce(f32[1024]{0:T(1024)S(1)} %fusion.5), channel_id=1, replica_groups=mesh['z_lo'=2,'x'=4,'core'=2,'y'=4,'z_hi'=4] {'y','z_hi'}, use_global_device_ids=true, to_apply=%region_13.0 | all-reduce | flops 1024 | bytes 8192 | tf_op jit(solution)/shard_map/while/body/pmax | solution.py:21
  472.3 32.6 %psum.44 = f32[1024]{0:T(1024)S(1)} all-reduce(f32[1024]{0:T(1024)S(1)} %exponential_reduce_fusion.1), channel_id=1, replica_groups=mesh['z_lo'=2,'x'=4,'core'=2,'y'=4,'z_hi'=4] {'y','z_hi'}, use_global_device_ids=true, to_apply=%region_15.0 | all-reduce | flops 1024 | bytes 8192 | tf_op jit(solution)/shard_map/while/body/psum | solution.py:22
  509.2 41.8 %pmax.27 = f32[2048]{0:T(1024)S(1)} all-reduce(f32[2048]{0:T(1024)S(1)} %fusion.6), channel_id=1, replica_groups=mesh['z_lo'=2,'x'=4,'core'=2,'y'=4,'z_hi'=4] {'z_lo','x','core'}, use_global_device_ids=true, to_apply=%region_17.0 | all-reduce | flops 2048 | bytes 16384 | tf_op jit(solution)/shard_map/while/body/pmax | solution.py:27
  555.5 27.7 %psum.45 = f32[2048]{0:T(1024)S(1)} all-reduce(f32[2048]{0:T(1024)S(1)} %exponential_reduce_fusion), channel_id=1, replica_groups=mesh['z_lo'=2,'x'=4,'core'=2,'y'=4,'z_hi'=4] {'z_lo','x','core'}, use_global_device_ids=true, to_apply=%region_19.0 | all-reduce | flops 2048 | bytes 16384 | tf_op jit(solution)/shard_map/while/body/psum | solution.py:28
  587.7 33.9 %psum.46 = f32[1024]{0:T(1024)S(1)} all-reduce(f32[1024]{0:T(1024)S(1)} %fusion), channel_id=1, replica_groups=mesh['z_lo'=2,'x'=4,'core'=2,'y'=4,'z_hi'=4] {'y','z_hi'}, use_global_device_ids=true, to_apply=%region_21.0 | all-reduce | flops 1024 | bytes 8192 | tf_op jit(solution)/shard_map/while/body/psum | solution.py:53
  626.2 34.9 %psum.47 = f32[2048]{0:T(1024)S(1)} all-reduce(f32[2048]{0:T(1024)S(1)} %fusion.1), channel_id=1, replica_groups=mesh['z_lo'=2,'x'=4,'core'=2,'y'=4,'z_hi'=4] {'z_lo','x','core'}, use_global_device_ids=true, to_apply=%region_23.0 | all-reduce | flops 2048 | bytes 16384 | tf_op jit(solution)/shard_map/while/body/psum | solution.py:57
  665.8 32.6 %psum.48 = f32[1024]{0:T(1024)S(1)} all-reduce(f32[1024]{0:T(1024)S(1)} %fusion.2), channel_id=1, replica_groups=mesh['z_lo'=2,'x'=4,'core'=2,'y'=4,'z_hi'=4] {'y','z_hi'}, use_global_device_ids=true, to_apply=%region_25.0 | all-reduce | flops 1024 | bytes 8192 | tf_op jit(solution)/shard_map/while/body/psum | solution.py:61
  698.4 10.7 %fusion.9 = (f32[2048]{0:T(1024)S(1)}, f32[1024]{0:T(1024)S(1)}, f32[1024,2048]{1,0:T(8,128)S(1)}) fusion(f32[1024]{0:T(1024)S(1)} %get-tuple-element.142, f32[1024,2048]{1,0:T(8,128)} %get-tuple-element.144, f32[2048]{0:T(1024)S(1)} %get-tuple-element.166, f32[1024]{0:T(1024)S(1)} %neg.5, f32[2048]{0:T(1024)S(1)} %get-tuple-element.140, ...), kind=kLoop, calls=%fused_computation.40 | loop fusion | flops 44037120 | bytes 16855040 | tf_op jit(solution)/shard_map/while/body/reduce_sum | solution.py:69
  712.3 7.7 fusion.8
  724.3 16.6 %fusion.7 = f32[2048,256]{1,0:T(8,128)} fusion(f32[1024,2048]{1,0:T(8,128)} %copy-done, f32[1024,256]{1,0:T(8,128)S(1)} %bitcast.24, f32[2048,256]{1,0:T(8,128)S(1)} %bitcast.20, f32[2048]{0:T(1024)S(1)} %get-tuple-element.122), kind=kOutput, calls=%fused_computation.21 | convolution fusion | flops 6444023808 | bytes 13639680 | tf_op jit(solution)/shard_map/while/body/dot_general | solution.py:68
  740.9 7.6 all-to-all-done.2
  748.5 12.4 %all-to-all-start.3 = ((f32[16,128,256]{2,1,0:T(8,128)}), f32[16,128,256]{2,1,0:T(8,128)S(1)}, u32[]{:S(2)}, u32[]{:S(2)}) async-start(f32[16,128,256]{2,1,0:T(8,128)} %bitcast.21), calls=%async_computation.3 | async-start | bytes 4194304 | tf_op jit(solution)/shard_map/while/body/all_to_all | solution.py:78
  762.8 27.2 %all-to-all-done.3 = f32[16,128,256]{2,1,0:T(8,128)S(1)} async-done(((f32[16,128,256]{2,1,0:T(8,128)}), f32[16,128,256]{2,1,0:T(8,128)S(1)}, u32[]{:S(2)}, u32[]{:S(2)}) %all-to-all-start.3) | async-done | bytes 2097184 | tf_op jit(solution)/shard_map/while/body/all_to_all | solution.py:78
  (94 shorter events, 129.7 us)
Async XLA Ops:
  0.6 13.1 %collective-permute-start = (f32[64,256]{1,0:T(8,128)}, f32[64,256]{1,0:T(8,128)S(1)}, u32[]{:S(2)}, u32[]{:S(2)}) collective-permute-start(f32[64,256]{1,0:T(8,128)} %own.1), channel_id=1, source_target_pairs={{0,1},{1,2},{2,3},{3,0},{4,5},{5,6},{6,7},{7,4},{8,9},{9,10},{10,1... | collective-permute-start | bytes 196616 | tf_op jit(solution)/shard_map/ppermute | solution.py:326
  3.7 10.0 %collective-permute-start.1 = (f32[64,256]{1,0:T(8,128)}, f32[64,256]{1,0:T(8,128)S(1)}, u32[]{:S(2)}, u32[]{:S(2)}) collective-permute-start(f32[64,256]{1,0:T(8,128)} %own.1), channel_id=1, source_target_pairs={{0,2},{1,3},{2,0},{3,1},{4,6},{5,7},{6,4},{7,5},{8,10},{9,11},{10,... | collective-permute-start | bytes 196616 | tf_op jit(solution)/shard_map/ppermute | solution.py:326
  8.8 7.8 collective-permute-start.2
  11.2 9.3 %collective-permute-start.6 = (f32[128,256]{1,0:T(8,128)}, f32[128,256]{1,0:T(8,128)S(1)}, u32[]{:S(2)}, u32[]{:S(2)}) collective-permute-start(f32[128,256]{1,0:T(8,128)} %param.6), channel_id=1, source_target_pairs={{0,128},{128,0},{1,129},{129,1},{2,130},{130,2},{3,131},{131,3},{4... | collective-permute-start | bytes 393224 | tf_op jit(solution)/shard_map/ppermute | solution.py:326
  16.6 8.7 %collective-permute-start.3 = (f32[256,256]{1,0:T(8,128)S(1)}, f32[256,256]{1,0:T(8,128)S(1)}, u32[]{:S(2)}, u32[]{:S(2)}) collective-permute-start(f32[256,256]{1,0:T(8,128)S(1)} %constant_dynamic-update-slice_fusion.refs_0_), channel_id=1, source_target_pairs={{0,4},{4,8},{8,12},{12,0},{1,5},{5,9},{9,13},{13,1},{2,6},{6,10},{... | collective-permute-start | bytes 786440 | tf_op jit(solution)/shard_map/ppermute | solution.py:326
  17.9 14.1 %collective-permute-start.4 = (f32[256,256]{1,0:T(8,128)S(1)}, f32[256,256]{1,0:T(8,128)S(1)}, u32[]{:S(2)}, u32[]{:S(2)}) collective-permute-start(f32[256,256]{1,0:T(8,128)S(1)} %constant_dynamic-update-slice_fusion.refs_0_), channel_id=1, source_target_pairs={{0,8},{4,12},{8,0},{12,4},{1,9},{5,13},{9,1},{13,5},{2,10},{6,14},... | collective-permute-start | bytes 786440 | tf_op jit(solution)/shard_map/ppermute | solution.py:326
  20.5 12.9 %collective-permute-start.7 = (f32[256,256]{1,0:T(8,128)S(1)}, f32[256,256]{1,0:T(8,128)S(1)}, u32[]{:S(2)}, u32[]{:S(2)}) collective-permute-start(f32[256,256]{1,0:T(8,128)S(1)} %constant_dynamic-update-slice_fusion.4.refs_4_), channel_id=1, source_target_pairs={{0,32},{32,64},{64,96},{96,0},{1,33},{33,65},{65,97},{97,1},{2,34}... | collective-permute-start | bytes 786440 | tf_op jit(solution)/shard_map/ppermute | solution.py:326
  20.8 12.6 %collective-permute-start.8 = (f32[256,256]{1,0:T(8,128)S(1)}, f32[256,256]{1,0:T(8,128)S(1)}, u32[]{:S(2)}, u32[]{:S(2)}) collective-permute-start(f32[256,256]{1,0:T(8,128)S(1)} %constant_dynamic-update-slice_fusion.4.refs_4_), channel_id=1, source_target_pairs={{0,64},{32,96},{64,0},{96,32},{1,65},{33,97},{65,1},{97,33},{2,66}... | collective-permute-start | bytes 786440 | tf_op jit(solution)/shard_map/ppermute | solution.py:326
  23.0 13.2 %collective-permute-start.9 = (f32[256,256]{1,0:T(8,128)S(1)}, f32[256,256]{1,0:T(8,128)S(1)}, u32[]{:S(2)}, u32[]{:S(2)}) collective-permute-start(f32[256,256]{1,0:T(8,128)S(1)} %constant_dynamic-update-slice_fusion.4.refs_4_), channel_id=1, source_target_pairs={{0,96},{32,0},{64,32},{96,64},{1,97},{33,1},{65,33},{97,65},{2,98}... | collective-permute-start | bytes 786440 | tf_op jit(solution)/shard_map/ppermute | solution.py:326
  25.3 11.7 %collective-permute-start.5 = (f32[256,256]{1,0:T(8,128)S(1)}, f32[256,256]{1,0:T(8,128)S(1)}, u32[]{:S(2)}, u32[]{:S(2)}) collective-permute-start(f32[256,256]{1,0:T(8,128)S(1)} %constant_dynamic-update-slice_fusion.refs_0_), channel_id=1, source_target_pairs={{0,12},{4,0},{8,4},{12,8},{1,13},{5,1},{9,5},{13,9},{2,14},{6,2},{... | collective-permute-start | bytes 786440 | tf_op jit(solution)/shard_map/ppermute | solution.py:326
  32.0 5.0 collective-permute-start.10
  33.4 3.5 collective-permute-start.11
  33.4 3.5 collective-permute-start.12
  36.1 1.9 collective-permute-start.13
  136.4 38.3 %copy-start.2 = (f32[64,256]{1,0:T(8,128)S(1)}, f32[64,256]{1,0:T(8,128)}, u32[]{:S(2)}) copy-start(f32[64,256]{1,0:T(8,128)} %own.1) | copy-start | bytes 196612
  136.4 39.0 %copy-start.1 = (f32[128,256]{1,0:T(8,128)S(1)}, f32[128,256]{1,0:T(8,128)}, u32[]{:S(2)}) copy-start(f32[128,256]{1,0:T(8,128)} %param.6) | copy-start | bytes 393220
  136.4 39.0 %copy-start.3 = (f32[2048]{0:T(1024)S(1)}, f32[2048]{0:T(1024)}, u32[]{:S(2)}) copy-start(f32[2048]{0:T(1024)} %param.7) | copy-start | bytes 24580
  140.7 3.7 collective-permute-start.20
  145.5 29.1 %all-to-all-start.11 = ((f32[8,128,256]{2,1,0:T(8,128)}), f32[8,128,256]{2,1,0:T(8,128)S(1)}, u32[]{:S(2)}, u32[]{:S(2)}) async-start(f32[8,128,256]{2,1,0:T(8,128)} %bitcast.11), calls=%async_computation.11 | async-start | bytes 2097152 | tf_op jit(solution)/shard_map/all_to_all | solution.py:78
  150.9 9.1 %collective-permute-start.14 = (f32[256,256]{1,0:T(8,128)S(1)}, f32[256,256]{1,0:T(8,128)S(1)}, u32[]{:S(2)}, u32[]{:S(2)}) collective-permute-start(f32[256,256]{1,0:T(8,128)S(1)} %get-tuple-element.105), channel_id=1, source_target_pairs={{0,4},{4,8},{8,12},{12,0},{1,5},{5,9},{9,13},{13,1},{2,6},{6,10},{... | collective-permute-start | bytes 786440 | tf_op jit(solution)/shard_map/ppermute | solution.py:326
  151.1 13.2 %collective-permute-start.15 = (f32[256,256]{1,0:T(8,128)S(1)}, f32[256,256]{1,0:T(8,128)S(1)}, u32[]{:S(2)}, u32[]{:S(2)}) collective-permute-start(f32[256,256]{1,0:T(8,128)S(1)} %get-tuple-element.106), channel_id=1, source_target_pairs={{0,8},{4,12},{8,0},{12,4},{1,9},{5,13},{9,1},{13,5},{2,10},{6,14},... | collective-permute-start | bytes 786440 | tf_op jit(solution)/shard_map/ppermute | solution.py:326
  152.9 12.5 %collective-permute-start.16 = (f32[256,256]{1,0:T(8,128)S(1)}, f32[256,256]{1,0:T(8,128)S(1)}, u32[]{:S(2)}, u32[]{:S(2)}) collective-permute-start(f32[256,256]{1,0:T(8,128)S(1)} %get-tuple-element.107), channel_id=1, source_target_pairs={{0,12},{4,0},{8,4},{12,8},{1,13},{5,1},{9,5},{13,9},{2,14},{6,2},{... | collective-permute-start | bytes 786440 | tf_op jit(solution)/shard_map/ppermute | solution.py:326
  166.0 6.3 collective-permute-start.17
  166.8 7.8 collective-permute-start.18
  168.8 5.8 collective-permute-start.19
  230.2 42.9 %all-to-all-start.1 = ((f32[16,128,256]{2,1,0:T(8,128)}), f32[16,128,256]{2,1,0:T(8,128)S(1)}, u32[]{:S(2)}, u32[]{:S(2)}) async-start(f32[16,128,256]{2,1,0:T(8,128)} %broadcast_in_dim.1), calls=%async_computation.1 | async-start | bytes 4194304 | tf_op jit(solution)/shard_map/while/body/all_to_all | solution.py:78
  709.1 3.2 copy-start
  720.0 28.5 %all-to-all-start.2 = ((f32[16,64,256]{2,1,0:T(8,128)}), f32[16,64,256]{2,1,0:T(8,128)}, u32[]{:S(2)}, u32[]{:S(2)}) async-start(f32[16,64,256]{2,1,0:T(8,128)} %bitcast.25), calls=%async_computation.2 | async-start | bytes 2097152 | tf_op jit(solution)/shard_map/while/body/all_to_all | solution.py:78
  748.5 41.5 %all-to-all-start.3 = ((f32[16,128,256]{2,1,0:T(8,128)}), f32[16,128,256]{2,1,0:T(8,128)S(1)}, u32[]{:S(2)}, u32[]{:S(2)}) async-start(f32[16,128,256]{2,1,0:T(8,128)} %bitcast.21), calls=%async_computation.3 | async-start | bytes 4194304 | tf_op jit(solution)/shard_map/while/body/all_to_all | solution.py:78
